TPU v7x, 128 devices: a whole 4x4x4 slice. The times are simulated.
128 devices in a mesh: row: 16 (over y, x_hi, core), col: 8 (over z, x_lo).
Axes of the slice: x: 4 (x_hi: 2, x_lo: 2; x = x_hi * 2 + x_lo), y: 4, z: 4, core: 2. Of those that a mesh axis runs over, the one named last changes fastest.
Arguments:
- cotangent: bfloat16 [512, 512, 128], P('row', 'col'), may hold values from -6 to 6
- activations: bfloat16 [3, 512, 512, 128], P(None, 'row', 'col'), may hold values from 0 to 2
- active_masks: int32 [3, 512, 512, 128], P(None, 'row', 'col'), may hold values 0 or 1
- weights: bfloat16 [3, 9, 128, 128], replicated, may hold values from -0.1875 to 0.1875
Outputs:
- data_gradient: bfloat16 [512, 512, 128], P('row', 'col')
- weight_gradients: float32 [3, 9, 128, 128], replicated
All inputs are finite; a program needn't handle non-finite values. No bound on the sum of `active_masks` on one device may be relied on, other than what follows from the above.
Results may differ from a plain program's by a relative error of at most 0.0054.
Values may be sent and summed in bfloat16 or wider, within the bound.
No kernel may reach another device: no remote copies, remote signals or barrier semaphores. Data moves between devices by JAX's collectives and lax.ppermute only.
A program may use at most 64 MiB of HBM per device.

v0:
```python
import jax
import jax.numpy as jnp
from jax import lax
from jax.sharding import PartitionSpec as P


def extended(block, sides, width):
    for axis, dim in sides:
        count = lax.axis_size(axis)
        forward = [(i, i + 1) for i in range(count - 1)]
        backward = [(target, source) for source, target in forward]
        low = lax.ppermute(
            lax.slice_in_dim(block, block.shape[dim] - width, None, axis=dim), axis, forward
        )
        high = lax.ppermute(lax.slice_in_dim(block, 0, width, axis=dim), axis, backward)
        block = jnp.concatenate([low, block, high], axis=dim)
    return block


def tap_columns(padded, height, extent, dilation):
    pieces = []
    for tap_down in range(3):
        for tap_across in range(3):
            start_down = dilation * (2 - tap_down)
            start_across = dilation * (2 - tap_across)
            pieces.append(
                padded[start_down : start_down + height, start_across : start_across + extent]
            )
    return jnp.stack(pieces, axis=2)


def mirrored(local_tile):
    stripe = lax.all_to_all(local_tile, "col", split_axis=0, concat_axis=1, tiled=True)
    arrived = lax.all_to_all(stripe, ("row", "col"), split_axis=1, concat_axis=0, tiled=True)
    flipped = jnp.transpose(arrived, (1, 0, 2))
    return lax.all_to_all(flipped, "col", split_axis=1, concat_axis=0, tiled=True)


def per_device(cotangent, activations, active_masks, weights):
    height, extent, channels = cotangent.shape
    map_side = height * lax.axis_size("row")
    layers = weights.shape[0]
    gradient = cotangent
    collected = []
    for layer_index in reversed(range(layers)):
        dilation = 2**layer_index
        mask_now = active_masks[layer_index] > 0
        inputs_now = jnp.where(
            mask_now, activations[layer_index], jnp.zeros_like(activations[layer_index])
        )
        mirror = mirrored(gradient)
        symmetric = ((gradient.astype(jnp.float32) + mirror.astype(jnp.float32)) * 0.5).astype(
            jnp.bfloat16
        )
        padded = extended(symmetric, (("row", 0), ("col", 1)), dilation)
        stacked = tap_columns(padded, height, extent, dilation)
        partial_value = (
            jnp.einsum("yxi,yxko->kio", inputs_now, stacked, preferred_element_type=jnp.float32)
            / map_side
        )
        input_change = jnp.einsum(
            "yxko,kio->yxi", stacked, weights[layer_index], preferred_element_type=jnp.float32
        )
        gradient = (
            gradient.astype(jnp.float32) + jnp.where(mask_now, input_change, jnp.float32(0.0))
        ).astype(jnp.bfloat16)
        collected.append(lax.psum(partial_value, ("row", "col")))
    kernel_stack = jnp.stack(collected[::-1])
    return (gradient, kernel_stack)


def solution(mesh):
    in_specs = (
        P("row", "col", None),
        P(None, "row", "col", None),
        P(None, "row", "col", None),
        P(),
    )
    out_specs = (P("row", "col", None), P())
    return jax.shard_map(
        per_device, mesh=mesh, in_specs=in_specs, out_specs=out_specs, check_vma=False
    )
```

profile of v0, /device:TPU:1, one launch (start us, length us, event | category | flops | bytes accessed | tf_op | source)
XLA Modules:
  0.0 380.1 jit_solution(12694586066596044938)
XLA Ops:
  7.2 16.0 %all_to_all.135 = bf16[32,64,128]{2,1,0:T(8,128)(2,1)S(1)} all-to-all(bf16[32,64,128]{2,1,0:T(8,128)(2,1)} %param.4), channel_id=1, replica_groups=mesh['row'=16,'col'=8] {'col'}, dimensions={0} | all-to-all | bytes 1048576 | tf_op jit(solution)/shard_map/all_to_all | solution.py:33
  23.7 22.2 %all_to_all.136 = bf16[4,512,128]{2,0,1:T(4,128)(2,1)S(1)} all-to-all(bf16[4,512,128]{2,0,1:T(4,128)(2,1)S(1)} %copy.57), channel_id=1, replica_groups=mesh['row'=16,'col'=8] {'row','col'}, dimensions={1} | all-to-all | bytes 1048576 | tf_op jit(solution)/shard_map/all_to_all | solution.py:34
  46.5 11.6 %all_to_all.137 = bf16[4,512,128]{2,0,1:T(4,128)(2,1)S(1)} all-to-all(bf16[4,512,128]{2,0,1:T(4,128)(2,1)S(1)} %copy.59), channel_id=1, replica_groups=mesh['row'=16,'col'=8] {'col'}, dimensions={1} | all-to-all | bytes 1048576 | tf_op jit(solution)/shard_map/all_to_all | solution.py:36
  58.7 5.6 %collective-permute-start = (bf16[4,64,128]{2,1,0:T(8,128)(2,1)S(1)}, bf16[4,64,128]{2,1,0:T(8,128)(2,1)S(1)}, u32[]{:S(2)}, u32[]{:S(2)}) collective-permute-start(bf16[4,64,128]{2,1,0:T(8,128)(2,1)S(1)} %get-tuple-element.32), channel_id=1, source_target_pairs={{0,8},{8,16},{16,24},{24,32},{32,40},{40,48},{48,56},{56,64},{64,7... | collective-permute-start | bytes 196616 | tf_op jit(solution)/shard_map/ppermute | solution.py:12
  64.3 1.9 collective-permute-start.1
  66.2 5.2 %collective-permute-done.1 = bf16[4,64,128]{2,1,0:T(8,128)(2,1)S(1)} collective-permute-done((bf16[4,64,128]{2,1,0:T(8,128)(2,1)S(1)}, bf16[4,64,128]{2,1,0:T(8,128)(2,1)S(1)}, u32[]{:S(2)}, u32[]{:S(2)}) %collective-permute-start.1) | collective-permute-done | bytes 65568 | tf_op jit(solution)/shard_map/ppermute | solution.py:15
  71.4 1.8 collective-permute-start.3
  75.0 3.0 collective-permute-done.2
  81.0 13.2 %all_to_all.138 = bf16[32,64,128]{2,1,0:T(8,128)(2,1)S(1)} all-to-all(bf16[32,64,128]{2,1,0:T(8,128)(2,1)S(1)} %fusion.3), channel_id=1, replica_groups=mesh['row'=16,'col'=8] {'col'}, dimensions={0} | all-to-all | bytes 1048576 | tf_op jit(solution)/shard_map/all_to_all | solution.py:33
  94.7 20.1 %all_to_all.139 = bf16[4,512,128]{2,0,1:T(4,128)(2,1)S(1)} all-to-all(bf16[4,512,128]{2,0,1:T(4,128)(2,1)S(1)} %copy.71), channel_id=1, replica_groups=mesh['row'=16,'col'=8] {'row','col'}, dimensions={1} | all-to-all | bytes 1048576 | tf_op jit(solution)/shard_map/all_to_all | solution.py:34
  115.4 11.5 %all_to_all.140 = bf16[4,512,128]{2,0,1:T(4,128)(2,1)S(1)} all-to-all(bf16[4,512,128]{2,0,1:T(4,128)(2,1)S(1)} %copy.73), channel_id=1, replica_groups=mesh['row'=16,'col'=8] {'col'}, dimensions={1} | all-to-all | bytes 1048576 | tf_op jit(solution)/shard_map/all_to_all | solution.py:36
  127.4 5.6 %collective-permute-start.4 = (bf16[2,64,128]{2,1,0:T(8,128)(2,1)S(1)}, bf16[2,64,128]{2,1,0:T(8,128)(2,1)S(1)}, u32[]{:S(2)}, u32[]{:S(2)}) collective-permute-start(bf16[2,64,128]{2,1,0:T(8,128)(2,1)S(1)} %get-tuple-element.30), channel_id=1, source_target_pairs={{0,8},{8,16},{16,24},{24,32},{32,40},{40,48},{48,56},{56,64},{64,7... | collective-permute-start | bytes 98312 | tf_op jit(solution)/shard_map/ppermute | solution.py:12
  133.0 1.9 collective-permute-start.5
  134.9 4.8 %collective-permute-done.5 = bf16[2,64,128]{2,1,0:T(8,128)(2,1)S(1)} collective-permute-done((bf16[2,64,128]{2,1,0:T(8,128)(2,1)S(1)}, bf16[2,64,128]{2,1,0:T(8,128)(2,1)S(1)}, u32[]{:S(2)}, u32[]{:S(2)}) %collective-permute-start.5) | collective-permute-done | bytes 32800 | tf_op jit(solution)/shard_map/ppermute | solution.py:15
  139.8 1.8 collective-permute-start.7
  142.9 3.2 collective-permute-done.6
  147.6 1.4 fusion.4
  149.1 13.6 %all_to_all.141 = bf16[32,64,128]{2,1,0:T(8,128)(2,1)S(1)} all-to-all(bf16[32,64,128]{2,1,0:T(8,128)(2,1)S(1)} %fusion.4), channel_id=1, replica_groups=mesh['row'=16,'col'=8] {'col'}, dimensions={0} | all-to-all | bytes 1048576 | tf_op jit(solution)/shard_map/all_to_all | solution.py:33
  163.1 19.9 %all_to_all.142 = bf16[4,512,128]{2,0,1:T(4,128)(2,1)S(1)} all-to-all(bf16[4,512,128]{2,0,1:T(4,128)(2,1)S(1)} %copy.77), channel_id=1, replica_groups=mesh['row'=16,'col'=8] {'row','col'}, dimensions={1} | all-to-all | bytes 1048576 | tf_op jit(solution)/shard_map/all_to_all | solution.py:34
  183.6 11.6 %all_to_all.143 = bf16[4,512,128]{2,0,1:T(4,128)(2,1)S(1)} all-to-all(bf16[4,512,128]{2,0,1:T(4,128)(2,1)S(1)} %copy.79), channel_id=1, replica_groups=mesh['row'=16,'col'=8] {'col'}, dimensions={1} | all-to-all | bytes 1048576 | tf_op jit(solution)/shard_map/all_to_all | solution.py:36
  195.7 5.6 %collective-permute-start.8 = (bf16[1,64,128]{2,1,0:T(8,128)(2,1)S(1)}, bf16[1,64,128]{2,1,0:T(8,128)(2,1)S(1)}, u32[]{:S(2)}, u32[]{:S(2)}) collective-permute-start(bf16[1,64,128]{2,1,0:T(8,128)(2,1)S(1)} %get-tuple-element.28), channel_id=1, source_target_pairs={{0,8},{8,16},{16,24},{24,32},{32,40},{40,48},{48,56},{56,64},{64,7... | collective-permute-start | bytes 49160 | tf_op jit(solution)/shard_map/ppermute | solution.py:12
  201.3 1.9 collective-permute-start.9
  203.2 2.3 fusion.7
  205.5 2.4 collective-permute-done.9
  207.9 1.8 collective-permute-start.11
  211.0 2.3 fusion.9
  215.7 2.1 copy-done.2
  217.8 2.3 fusion.11
  220.1 4.5 %fusion.5 = bf16[32,64,128]{2,1,0:T(8,128)(2,1)} fusion(pred[32,64,128]{2,1,0:T(32,128)(4,1)S(1)} %get-tuple-element.14, bf16[32,64,9,128]{3,1,0,2:T(8,128)(2,1)} %copy-done.2, bf16[32,64,128]{2,1,0:T(8,128)(2,1)S(1)} %fusion.4, bf16[3,9,128,128]{3,2,1,0:T(8,128)(2,1)S(1)} %copy-done.4), kind=kOutput, calls=%fused_computation.15 | convolution fusion | flops 605028352 | bytes 6324224 | tf_op jit(solution)/shard_map/yxko,kio->yxi/dot_general | solution.py:61
  224.6 145.2 %all-reduce.3.cloned.1.call-done = (f32[1,9,128,128]{2,3,1,0:T(8,128)}, f32[1,9,128,128]{2,3,1,0:T(8,128)}, f32[1,9,128,128]{2,3,1,0:T(8,128)}) async-done(((f32[1,9,128,128]{2,3,1,0:T(8,128)}, f32[1,9,128,128]{2,3,1,0:T(8,128)}, f32[1,9,128,128]{2,3,1,0:T(8,128)}), (f32[1,9,128,128]{2,3,1,0:T(8,128)}, f32[1,9,128,128]{2,3,1,0:T(8,128)}, f32[1,9,128,128]{2,3,1,0:T(8,128)})) %all-reduce.3.cloned.1.call-update) | async-done | bytes 1769488 | tf_op jit(solution)/shard_map/psum | solution.py:67
  369.8 1.5 pad_maximum_fusion
  371.3 1.9 copy.82
  (83 shorter events, 15.6 us)
Async XLA Ops:
  7.2 362.6 %all-reduce.3.cloned.1.call-start = ((), (), s32[]{:S(2)}) async-start(), calls=%async_computation.9 | async-start | bytes 3538944 | tf_op jit(solution)/shard_map/psum | solution.py:67
  23.7 34.8 %copy-start.1 = (bf16[32,64,128]{2,1,0:T(8,128)(2,1)S(1)}, bf16[32,64,128]{2,1,0:T(8,128)(2,1)}, u32[]{:S(2)}) copy-start(bf16[32,64,128]{2,1,0:T(8,128)(2,1)} %param.4) | copy-start | bytes 1572868
  46.1 28.5 %copy-start = (s32[3,32,64,128]{3,2,1,0:T(8,128)S(1)}, s32[3,32,64,128]{3,2,1,0:T(8,128)}, u32[]{:S(2)}) copy-start(s32[3,32,64,128]{3,2,1,0:T(8,128)} %param.6) | copy-start | bytes 9437188
  58.7 7.5 %collective-permute-start = (bf16[4,64,128]{2,1,0:T(8,128)(2,1)S(1)}, bf16[4,64,128]{2,1,0:T(8,128)(2,1)S(1)}, u32[]{:S(2)}, u32[]{:S(2)}) collective-permute-start(bf16[4,64,128]{2,1,0:T(8,128)(2,1)S(1)} %get-tuple-element.32), channel_id=1, source_target_pairs={{0,8},{8,16},{16,24},{24,32},{32,40},{40,48},{48,56},{56,64},{64,7... | collective-permute-start | bytes 196616 | tf_op jit(solution)/shard_map/ppermute | solution.py:12
  64.3 7.1 %collective-permute-start.1 = (bf16[4,64,128]{2,1,0:T(8,128)(2,1)S(1)}, bf16[4,64,128]{2,1,0:T(8,128)(2,1)S(1)}, u32[]{:S(2)}, u32[]{:S(2)}) collective-permute-start(bf16[4,64,128]{2,1,0:T(8,128)(2,1)S(1)} %get-tuple-element.33), channel_id=1, source_target_pairs={{8,0},{16,8},{24,16},{32,24},{40,32},{48,40},{56,48},{64,56},{72,6... | collective-permute-start | bytes 196616 | tf_op jit(solution)/shard_map/ppermute | solution.py:15
  71.4 3.6 collective-permute-start.3
  73.2 4.7 %collective-permute-start.2 = (bf16[40,4,128]{2,1,0:T(4,128)(2,1)S(1)}, bf16[40,4,128]{2,1,0:T(4,128)(2,1)S(1)}, u32[]{:S(2)}, u32[]{:S(2)}) collective-permute-start(bf16[40,4,128]{2,1,0:T(4,128)(2,1)S(1)} %get-tuple-element.19), channel_id=1, source_target_pairs={{1,0},{2,1},{3,2},{4,3},{5,4},{6,5},{7,6},{9,8},{10,9},{11,10},{12... | collective-permute-start | bytes 122888 | tf_op jit(solution)/shard_map/ppermute | solution.py:15
  78.4 1.2 copy-start.4
  127.4 7.5 %collective-permute-start.4 = (bf16[2,64,128]{2,1,0:T(8,128)(2,1)S(1)}, bf16[2,64,128]{2,1,0:T(8,128)(2,1)S(1)}, u32[]{:S(2)}, u32[]{:S(2)}) collective-permute-start(bf16[2,64,128]{2,1,0:T(8,128)(2,1)S(1)} %get-tuple-element.30), channel_id=1, source_target_pairs={{0,8},{8,16},{16,24},{24,32},{32,40},{40,48},{48,56},{56,64},{64,7... | collective-permute-start | bytes 98312 | tf_op jit(solution)/shard_map/ppermute | solution.py:12
  133.0 6.7 %collective-permute-start.5 = (bf16[2,64,128]{2,1,0:T(8,128)(2,1)S(1)}, bf16[2,64,128]{2,1,0:T(8,128)(2,1)S(1)}, u32[]{:S(2)}, u32[]{:S(2)}) collective-permute-start(bf16[2,64,128]{2,1,0:T(8,128)(2,1)S(1)} %get-tuple-element.31), channel_id=1, source_target_pairs={{8,0},{16,8},{24,16},{32,24},{40,32},{48,40},{56,48},{64,56},{72,6... | collective-permute-start | bytes 98312 | tf_op jit(solution)/shard_map/ppermute | solution.py:15
  139.8 3.1 collective-permute-start.7
  141.6 4.5 %collective-permute-start.6 = (bf16[36,2,128]{2,1,0:T(2,128)(2,1)S(1)}, bf16[36,2,128]{2,1,0:T(2,128)(2,1)S(1)}, u32[]{:S(2)}, u32[]{:S(2)}) collective-permute-start(bf16[36,2,128]{2,1,0:T(2,128)(2,1)S(1)} %get-tuple-element.23), channel_id=1, source_target_pairs={{1,0},{2,1},{3,2},{4,3},{5,4},{6,5},{7,6},{9,8},{10,9},{11,10},{12... | collective-permute-start | bytes 55304 | tf_op jit(solution)/shard_map/ppermute | solution.py:15
  183.1 20.0 %copy-start.3 = (bf16[3,32,64,128]{3,2,1,0:T(8,128)(2,1)S(1)}, bf16[3,32,64,128]{3,2,1,0:T(8,128)(2,1)}, u32[]{:S(2)}) copy-start(bf16[3,32,64,128]{3,2,1,0:T(8,128)(2,1)} %param.5) | copy-start | bytes 4718596
  195.7 9.8 %collective-permute-start.8 = (bf16[1,64,128]{2,1,0:T(8,128)(2,1)S(1)}, bf16[1,64,128]{2,1,0:T(8,128)(2,1)S(1)}, u32[]{:S(2)}, u32[]{:S(2)}) collective-permute-start(bf16[1,64,128]{2,1,0:T(8,128)(2,1)S(1)} %get-tuple-element.28), channel_id=1, source_target_pairs={{0,8},{8,16},{16,24},{24,32},{32,40},{40,48},{48,56},{56,64},{64,7... | collective-permute-start | bytes 49160 | tf_op jit(solution)/shard_map/ppermute | solution.py:12
  201.3 6.6 %collective-permute-start.9 = (bf16[1,64,128]{2,1,0:T(8,128)(2,1)S(1)}, bf16[1,64,128]{2,1,0:T(8,128)(2,1)S(1)}, u32[]{:S(2)}, u32[]{:S(2)}) collective-permute-start(bf16[1,64,128]{2,1,0:T(8,128)(2,1)S(1)} %get-tuple-element.29), channel_id=1, source_target_pairs={{8,0},{16,8},{24,16},{32,24},{40,32},{48,40},{56,48},{64,56},{72,6... | collective-permute-start | bytes 49160 | tf_op jit(solution)/shard_map/ppermute | solution.py:15
  207.9 5.4 %collective-permute-start.11 = (bf16[34,1,128]{2,1,0:T(2,128)(2,1)S(1)}, bf16[34,1,128]{2,1,0:T(2,128)(2,1)S(1)}, u32[]{:S(2)}, u32[]{:S(2)}) collective-permute-start(bf16[34,1,128]{2,1,0:T(2,128)(2,1)S(1)} %get-tuple-element.26), channel_id=1, source_target_pairs={{0,1},{1,2},{2,3},{3,4},{4,5},{5,6},{6,7},{8,9},{9,10},{10,11},{11... | collective-permute-start | bytes 26120 | tf_op jit(solution)/shard_map/ppermute | solution.py:12
  209.7 4.5 %collective-permute-start.10 = (bf16[34,1,128]{2,1,0:T(2,128)(2,1)S(1)}, bf16[34,1,128]{2,1,0:T(2,128)(2,1)S(1)}, u32[]{:S(2)}, u32[]{:S(2)}) collective-permute-start(bf16[34,1,128]{2,1,0:T(2,128)(2,1)S(1)} %get-tuple-element.27), channel_id=1, source_target_pairs={{1,0},{2,1},{3,2},{4,3},{5,4},{6,5},{7,6},{9,8},{10,9},{11,10},{12... | collective-permute-start | bytes 26120 | tf_op jit(solution)/shard_map/ppermute | solution.py:15
  215.7 2.1 copy-start.2
Sparse Core Ops, SparseCore 0:
  220.2 149.5 all-reduce.2
where the time goes:
time: 381 us; the launch traced here: 380 us
  waiting for transfers between devices  165 us (43%)
  blocking collectives  140 us (37%)
  starting transfers between devices  31.9 us (8%)
  between operations  14.7 us (4%)
  matrix products  14.2 us (4%)
  local copies, waits for them, and re-layouts  10.4 us (3%)
  other arithmetic  4.45 us (1%)
    psum x1, waiting for transfers between devices, per_device(): collected.append(lax.psum(partial_value, ('row', 'col')))  145 us
    all_to_all x3, blocking collectives, mirrored(): lax.all_to_all(stripe, ('row', 'col'), split_axis=1, concat_axis=0, tiled...  62.2 us
    all_to_all x3, blocking collectives, mirrored(): lax.all_to_all(local_tile, 'col', split_axis=0, concat_axis=1, tiled=True)  42.9 us
    all_to_all x3, blocking collectives, mirrored(): lax.all_to_all(flipped, 'col', split_axis=1, concat_axis=0, tiled=True)  34.8 us
    ppermute x6, starting transfers between devices, extended(): lax.ppermute(lax.slice_in_dim(block, block.shape[dim] - width, None, axis...  22.3 us
    ppermute x6, waiting for transfers between devices, extended(): lax.ppermute(lax.slice_in_dim(block, 0, width, axis=dim), axis, backward)  19.4 us
    ppermute x6, starting transfers between devices, extended(): lax.ppermute(lax.slice_in_dim(block, 0, width, axis=dim), axis, backward)  9.64 us
  transfers between devices with their start and end apart: 13, of which 7 were waited for; matrix products, arithmetic and copies ran while one was open for 2% of the time, Pallas kernels for 0%

commit v1 on v0

v1 whole, which is shorter than its diff:
```python
import numpy as np
import jax
import jax.numpy as jnp
from jax import lax
from jax.sharding import Mesh, PartitionSpec as P

NAMES = ("y", "xh", "core", "z", "xl")
SIZES = (4, 2, 2, 4, 2)
CHIPS = ("y", "xh", "z", "xl")
BF = jnp.bfloat16
F32 = jnp.float32


def index_grid():
    return np.arange(128).reshape(SIZES)


def neighbour(down, across):
    pairs = []
    for r in range(16):
        for c in range(8):
            if 0 <= r + down < 16 and 0 <= c + across < 8:
                pairs.append((r * 8 + c, (r + down) * 8 + c + across))
    return pairs


def mirror_steps(part):
    grid = index_grid()
    first, second = [], []
    step = 1 if part == 0 else -1
    for y, xh, c, z, xl in np.ndindex(*SIZES):
        core = c if part == 0 else 1 - c
        source = int(grid[y, xh, c, z, xl])
        if (z - y) % 4 == 2:
            middle = int(grid[(y + step) % 4, xh, c, (z + step) % 4, xl])
            first.append((source, middle))
            second.append((middle, int(grid[(y + 2 * step) % 4, xl, core, (z + 2 * step) % 4, xh])))
        else:
            first.append((source, int(grid[z, xl, core, y, xh])))
    return first, second


def shift(x, pairs):
    return lax.ppermute(x, NAMES, pairs)


def halo(x, width, dim):
    rank = x.ndim
    low = neighbour(1, 0) if dim == rank - 3 else neighbour(0, 1)
    high = neighbour(-1, 0) if dim == rank - 3 else neighbour(0, -1)
    size = x.shape[dim]
    before = shift(lax.slice_in_dim(x, size - width, size, axis=dim), low)
    after = shift(lax.slice_in_dim(x, 0, width, axis=dim), high)
    return jnp.concatenate([before, x, after], axis=dim)


def halos(x, width):
    x = halo(x, width, x.ndim - 3)
    return halo(x, width, x.ndim - 2)


def mirrored(x, margin):
    core = lax.axis_index("core")
    rows, cols = x.shape[-3] - 2 * margin, x.shape[-2] - 2 * margin
    half = cols // 2
    got = []
    for part in (0, 1):
        which = core if part == 0 else 1 - core
        piece = lax.dynamic_slice_in_dim(x, margin * core, rows + margin, axis=x.ndim - 3)
        piece = lax.dynamic_slice_in_dim(piece, half * which, half + 2 * margin, axis=x.ndim - 2)
        first, second = mirror_steps(part)
        direct = shift(piece, first)
        relayed = shift(direct, second)
        got.append((direct, relayed))
    far = ((lax.axis_index("z") - lax.axis_index("y")) % 4) == 2
    got = [jnp.swapaxes(jnp.where(far, r, d), -3, -2) for d, r in got]
    left = jnp.where(core == 0, got[0], got[1])
    right = jnp.where(core == 0, got[1], got[0])
    return jnp.concatenate([left, right], axis=-2)


def total(x):
    core = lax.axis_index("core")
    rows = x.shape[0] // 2
    x = x.reshape(2, rows, 128)
    keep = lax.dynamic_index_in_dim(x, core, 0, False)
    send = lax.dynamic_index_in_dim(x, 1 - core, 0, False).astype(BF)
    grid = index_grid()
    swap = [(int(grid[y, a, c, z, b]), int(grid[y, a, 1 - c, z, b])) for y, a, c, z, b in np.ndindex(*SIZES)]
    part = (keep + shift(send, swap).astype(F32)).astype(BF).reshape(64, rows // 64, 128)
    terms = lax.all_to_all(part, CHIPS, 0, 0, tiled=True)
    mine = jnp.sum(terms.astype(F32), axis=0).astype(BF)
    copies = jnp.broadcast_to(mine[None], terms.shape)
    whole = lax.all_to_all(copies, CHIPS, 0, 0, tiled=True).reshape(rows, 128)
    other = shift(whole, swap)
    low = jnp.where(core == 0, whole, other)
    high = jnp.where(core == 0, other, whole)
    return jnp.concatenate([low, high], axis=0).astype(F32)


def conv(sym, kernel, dilation):
    return lax.conv_general_dilated(
        sym[None], kernel, (1, 1), "VALID", rhs_dilation=(dilation, dilation),
        dimension_numbers=("NHWC", "HWIO", "NHWC"), preferred_element_type=F32,
    )[0]


def taps(sym, height, extent, dilation):
    pieces = []
    for a in range(3):
        for b in range(3):
            u, v = dilation * (2 - a), dilation * (2 - b)
            pieces.append(sym[u : u + height, v : v + extent])
    return jnp.stack(pieces, axis=2)


def middle(x, margin):
    return x[margin : x.shape[0] - margin, margin : x.shape[1] - margin]


def per_device(cotangent, activations, active_masks, weights):
    height, extent, channels = cotangent.shape
    side = height * 16
    inputs = jnp.where(active_masks > 0, activations, jnp.zeros_like(activations))
    flip = mirrored(cotangent, 0)
    wide = cotangent.astype(F32)
    sym = ((wide + flip.astype(F32)) * 0.5).astype(BF)
    own = halos((active_masks[1:] > 0).astype(BF), 3)
    sym = halos(sym, 7)
    turned = mirrored(own, 3)

    kernels = weights.reshape(3, 3, 3, channels, channels)[:, ::-1, ::-1].transpose(0, 1, 2, 4, 3)
    both = jnp.concatenate([kernels, kernels.transpose(0, 2, 1, 3, 4)], axis=-1)
    gradient = wide
    collected = []
    for layer, margin in ((2, 3), (1, 1), (0, 0)):
        dilation = 2**layer
        stacked = taps(middle(sym, margin), height, extent, dilation) if margin else taps(sym, height, extent, dilation)
        collected.append(
            jnp.einsum("yxi,yxko->kio", inputs[layer], stacked, preferred_element_type=F32) / side
        )
        if layer:
            change = conv(sym, both[layer], dilation)
            crop = 3 - margin
            ahead = middle(own[layer - 1], crop).astype(F32) * change[..., :channels]
            back = middle(turned[layer - 1], crop).astype(F32) * change[..., channels:]
            gradient = gradient + middle(ahead, margin)
            sym = (middle(sym, dilation).astype(F32) + 0.5 * (ahead + back)).astype(BF)
        else:
            change = conv(sym, kernels[0], 1)
            gradient = gradient + jnp.where(active_masks[0] > 0, change, 0.0)
    terms = jnp.stack(collected[::-1])
    return gradient.astype(BF), total(terms.reshape(-1, channels)).reshape(terms.shape)


def solution(mesh):
    fine = Mesh(mesh.devices.reshape(SIZES), NAMES)
    rows, cols = ("y", "xh", "core"), ("z", "xl")
    in_specs = (P(rows, cols, None), P(None, rows, cols, None), P(None, rows, cols, None), P())
    out_specs = (P(rows, cols, None), P())
    return jax.shard_map(per_device, mesh=fine, in_specs=in_specs, out_specs=out_specs, check_vma=False)
```

time: 381 us -> 183 us (0.48)
  waiting for transfers between devices: 165 us -> 13.3 us
  blocking collectives: 140 us -> 73.7 us
  other arithmetic: 4.45 us -> 17.7 us
  between operations: 14.7 us -> 1.57 us
  starting transfers between devices: 31.9 us -> 44.1 us
  local copies, waits for them, and re-layouts: 10.4 us -> 22.3 us
  matrix products: 14.2 us -> 9.63 us
    psum x1 -> x0, waiting for transfers between devices: 145 us -> none  [per_device(): collected.append(lax.psum(partial_value, ('row', 'col')))]
    all_to_all x9 -> x1, blocking collectives: 140 us -> 73.7 us  [total(): terms = lax.all_to_all(part, CHIPS, 0, 0, tiled=True)]
    ppermute x12 -> x18, waiting for transfers between devices: 19.4 us -> 2.53 us  [shift(): return lax.ppermute(x, NAMES, pairs)]
    dot_general x6 -> x3, matrix products: 14.2 us -> 3.04 us  [per_device(): jnp.einsum('yxi,yxko->kio', inputs[layer], stacked, preferred_element_typ...]
    all_to_all x0 -> x1, waiting for transfers between devices: none -> 10.8 us  [total(): whole = lax.all_to_all(copies, CHIPS, 0, 0, tiled=True).reshape(rows, 128)]
    convert_element_type x6 -> x7, other arithmetic: 0.86 us -> 11.3 us  [the longest x2 3.7 us: per_device(): sym = (middle(sym, dilation).astype(F32) + 0.5 * (ahead + back)).astype(BF)]
    ppermute x12 -> x18, starting transfers between devices: 31.9 us -> 39.2 us  [shift(): return lax.ppermute(x, NAMES, pairs)]
    conv_general_dilated x0 -> x3, matrix products: none -> 6.58 us  [conv(): lax.conv_general_dilated(sym[None], kernel, (1, 1), 'VALID', rhs_dilation...]
  transfers between devices with their start and end apart: 13 -> 19, of which waited for: 7 -> 3; matrix products, arithmetic and copies ran while one was open for 2% -> 15% of each run, Pallas kernels for 0% -> 0%
where the time goes in v1:
time: 183 us; the launch traced here: 182 us
  blocking collectives  73.7 us (40%)
  starting transfers between devices  44.1 us (24%)
  local copies, waits for them, and re-layouts  22.3 us (12%)
  other arithmetic  17.7 us (10%)
  waiting for transfers between devices  13.3 us (7%)
  matrix products  9.63 us (5%)
    all_to_all x1, blocking collectives, total(): terms = lax.all_to_all(part, CHIPS, 0, 0, tiled=True)  73.7 us
    ppermute x18, starting transfers between devices, shift(): return lax.ppermute(x, NAMES, pairs)  39.2 us
    all_to_all x1, waiting for transfers between devices, total(): whole = lax.all_to_all(copies, CHIPS, 0, 0, tiled=True).reshape(rows, 128)  10.8 us
    unnamed x51, local copies, waits for them, and re-layouts  10.5 us
    conv_general_dilated x3, matrix products, conv(): lax.conv_general_dilated(sym[None], kernel, (1, 1), 'VALID', rhs_dilation...  6.58 us
    all_to_all x1, starting transfers between devices, total(): whole = lax.all_to_all(copies, CHIPS, 0, 0, tiled=True).reshape(rows, 128)  4.86 us
    conv_general_dilated x12, local copies, waits for them, and re-layouts, conv(): lax.conv_general_dilated(sym[None], kernel, (1, 1), 'VALID', rhs_dilation...  4.2 us
    convert_element_type x2, other arithmetic, per_device(): sym = (middle(sym, dilation).astype(F32) + 0.5 * (ahead + back)).astype(BF)  3.7 us
  transfers between devices with their start and end apart: 19, of which 3 were waited for; matrix products, arithmetic and copies ran while one was open for 15% of the time, Pallas kernels for 0%

profile of v1, /device:TPU:1, one launch (start us, length us, event | category | flops | bytes accessed | tf_op | source)
XLA Modules:
  0.0 182.3 jit_solution(971148014736366513)
XLA Ops:
  0.6 1.1 constant_dynamic-slice_fusion.2
  2.5 3.6 %collective-permute-start.4 = (bf16[32,32,128]{2,0,1:T(8,128)(2,1)}, bf16[32,32,128]{2,0,1:T(8,128)(2,1)}, u32[]{:S(2)}, u32[]{:S(2)}) collective-permute-start(bf16[32,32,128]{2,0,1:T(8,128)(2,1)} %copy.65), channel_id=1, source_target_pairs={{0,0},{1,16},{2,32},{3,48},{4,38},{5,39},{6,96},{7,112},{8,8},{9,2... | collective-permute-start | bytes 786440 | tf_op jit(solution)/shard_map/ppermute | solution.py:44
  6.9 1.4 collective-permute-start.6
  8.4 1.9 %fusion.1 = bf16[2,32,64,128]{3,2,1,0:T(8,128)(2,1)S(1)} fusion(s32[3,32,64,128]{3,2,1,0:T(8,128)} %param.6), kind=kLoop, calls=%fused_computation.6 | loop fusion | flops 1048576 | bytes 3145728 | tf_op jit(solution)/shard_map/convert_element_type | solution.py:128
  10.3 1.0 copy-done.1
  11.3 2.1 %collective-permute-start.1 = (bf16[2,3,64,128]{3,2,1,0:T(8,128)(2,1)S(1)}, bf16[2,3,64,128]{3,2,1,0:T(8,128)(2,1)S(1)}, u32[]{:S(2)}, u32[]{:S(2)}) collective-permute-start(bf16[2,3,64,128]{3,2,1,0:T(8,128)(2,1)S(1)} %get-tuple-element.13), channel_id=1, source_target_pairs={{8,0},{9,1},{10,2},{11,3},{12,4},{13,5},{14,6},{15,7},{16,8},{17,9... | collective-permute-start | bytes 294920 | tf_op jit(solution)/shard_map/ppermute | solution.py:44
  13.3 5.0 %collective-permute-start = (bf16[2,3,64,128]{3,2,1,0:T(8,128)(2,1)S(1)}, bf16[2,3,64,128]{3,2,1,0:T(8,128)(2,1)S(1)}, u32[]{:S(2)}, u32[]{:S(2)}) collective-permute-start(bf16[2,3,64,128]{3,2,1,0:T(8,128)(2,1)S(1)} %get-tuple-element.12), channel_id=1, source_target_pairs={{0,8},{1,9},{2,10},{3,11},{4,12},{5,13},{6,14},{7,15},{8,16},{9,17... | collective-permute-start | bytes 294920 | tf_op jit(solution)/shard_map/ppermute | solution.py:44
  18.4 2.3 %copy.41 = bf16[3,3,3,128,128]{3,4,1,2,0:T(8,128)(2,1)} copy(bf16[3,3,3,128,128]{4,3,2,1,0:T(8,128)(2,1)} %bitcast.251) | data formatting | bytes 1769472 | tf_op jit(solution)/shard_map/reshape | solution.py:132
  20.7 1.8 %compare_select_fusion = bf16[3,32,64,128]{3,2,1,0:T(8,128)(2,1)S(1)} fusion(bf16[3,32,64,128]{3,2,1,0:T(8,128)(2,1)} %param.5, s32[3,32,64,128]{3,2,1,0:T(8,128)S(1)} %copy-done), kind=kLoop, calls=%fused_computation.2 | loop fusion | flops 1572864 | bytes 6291456 | tf_op jit(solution)/shard_map/jit(_where)/select_n | solution.py:124
  24.6 1.4 collective-permute-start.3
  26.0 4.0 %collective-permute-start.2 = (bf16[2,38,3,128]{3,2,1,0:T(4,128)(2,1)S(1)}, bf16[2,38,3,128]{3,2,1,0:T(4,128)(2,1)S(1)}, u32[]{:S(2)}, u32[]{:S(2)}) collective-permute-start(bf16[2,38,3,128]{3,2,1,0:T(4,128)(2,1)S(1)} %get-tuple-element.10), channel_id=1, source_target_pairs={{0,1},{1,2},{2,3},{3,4},{4,5},{5,6},{6,7},{8,9},{9,10},{10,11},{11... | collective-permute-start | bytes 175112 | tf_op jit(solution)/shard_map/ppermute | solution.py:44
  30.1 1.1 select_bitcast_fusion.3
  31.4 1.9 %collective-permute-start.9 = (bf16[7,64,128]{2,1,0:T(8,128)(2,1)S(1)}, bf16[7,64,128]{2,1,0:T(8,128)(2,1)S(1)}, u32[]{:S(2)}, u32[]{:S(2)}) collective-permute-start(bf16[7,64,128]{2,1,0:T(8,128)(2,1)S(1)} %get-tuple-element.25), channel_id=1, source_target_pairs={{8,0},{9,1},{10,2},{11,3},{12,4},{13,5},{14,6},{15,7},{16,8},{17,9... | collective-permute-start | bytes 344072 | tf_op jit(solution)/shard_map/ppermute | solution.py:44
  33.3 5.1 %collective-permute-start.8 = (bf16[7,64,128]{2,1,0:T(8,128)(2,1)S(1)}, bf16[7,64,128]{2,1,0:T(8,128)(2,1)S(1)}, u32[]{:S(2)}, u32[]{:S(2)}) collective-permute-start(bf16[7,64,128]{2,1,0:T(8,128)(2,1)S(1)} %get-tuple-element.24), channel_id=1, source_target_pairs={{0,8},{1,9},{2,10},{3,11},{4,12},{5,13},{6,14},{7,15},{8,16},{9,17... | collective-permute-start | bytes 344072 | tf_op jit(solution)/shard_map/ppermute | solution.py:44
  40.3 1.3 collective-permute-start.11
  41.6 5.7 %collective-permute-start.10 = (bf16[46,7,128]{2,1,0:T(8,128)(2,1)S(1)}, bf16[46,7,128]{2,1,0:T(8,128)(2,1)S(1)}, u32[]{:S(2)}, u32[]{:S(2)}) collective-permute-start(bf16[46,7,128]{2,1,0:T(8,128)(2,1)S(1)} %get-tuple-element.22), channel_id=1, source_target_pairs={{0,1},{1,2},{2,3},{3,4},{4,5},{5,6},{6,7},{8,9},{9,10},{10,11},{11... | collective-permute-start | bytes 247304 | tf_op jit(solution)/shard_map/ppermute | solution.py:44
  53.6 2.3 %convolution_select_fusion = f32[38,8,10,256]{3,1,2,0:T(8,128)S(1)} fusion(bf16[46,1,7,8,128]{4,2,3,0,1:T(8,128)(2,1)S(1)} %slice.267, bf16[46,1,8,10,128]{4,2,3,0,1:T(8,128)(2,1)S(1)} %copy.40, pred[8,10]{0,1:T(8,128)(4,1)S(1)} %copy-done.10, bf16[3,3,3,128,128]{4,3,2,1,0:T(8,128)(2,1)S(1)} %get-tuple-element.19, ...), kind=kOutput, calls=%fused_computation.10 | convolution fusion | flops 1800110080 | bytes 6484048 | tf_op jit(solution)/shard_map/conv_general_dilated | solution.py:102
  57.6 1.8 copy.43
  62.5 1.8 fusion.13
  65.3 1.8 convolution_select_fusion.1
  70.5 1.2 fusion.21
  71.7 1.9 %fusion.17 = (bf16[34,66,128]{2,1,0:T(8,128)(2,1)S(1)}, f32[34,66,128]{2,1,0:T(8,128)}) fusion(f32[34,66,256]{2,1,0:T(8,128)S(1)} %bitcast.243, bf16[38,70,128]{2,1,0:T(8,128)(2,1)S(1)} %get-tuple-element.28, bf16[38,70,128]{2,1,0:T(8,128)(2,1)S(1)} %get-tuple-element.4, bf16[38,70,128]{2,1,0:T(8,128)(2,1)S(1)} %get-tuple-element.29), kind=kLoop, calls=%fused_computation.35 | loop fusion | flops 2585088 | bytes 5744640 | tf_op jit(solution)/shard_map/convert_element_type | solution.py:148
  76.8 1.6 collective-permute-done.16
  78.4 1.1 fusion.37
  79.7 73.7 %all_to_all.10 = bf16[64,27,128]{2,1,0:T(8,128)(2,1)S(1)} all-to-all(bf16[64,27,128]{2,1,0:T(8,128)(2,1)S(1)} %reshape.28), channel_id=1, replica_groups=mesh['y'=4,'xh'=2,'core'=2,'z'=4,'xl'=2] {'y','xh','z','xl'}, dimensions={0} | all-to-all | bytes 884736 | tf_op jit(solution)/shard_map/all_to_all | solution.py:91
  154.3 4.9 %all-to-all-start.1 = ((bf16[64,27,128]{2,1,0:T(8,128)(2,1)}), bf16[64,27,128]{2,1,0:T(8,128)(2,1)S(1)}, u32[]{:S(2)}, u32[]{:S(2)}) async-start(bf16[64,27,128]{2,1,0:T(8,128)(2,1)} %broadcast_in_dim.27), calls=%async_computation.1 | async-start | bytes 1048576 | tf_op jit(solution)/shard_map/all_to_all | solution.py:94
  159.5 10.8 %all-to-all-done.1 = bf16[64,27,128]{2,1,0:T(8,128)(2,1)S(1)} async-done(((bf16[64,27,128]{2,1,0:T(8,128)(2,1)}), bf16[64,27,128]{2,1,0:T(8,128)(2,1)S(1)}, u32[]{:S(2)}, u32[]{:S(2)}) %all-to-all-start.1) | async-done | bytes 442400 | tf_op jit(solution)/shard_map/all_to_all | solution.py:94
  170.5 3.0 %collective-permute-start.17 = (bf16[1728,128]{1,0:T(8,128)(2,1)S(1)}, bf16[1728,128]{1,0:T(8,128)(2,1)S(1)}, u32[]{:S(2)}, u32[]{:S(2)}) collective-permute-start(bf16[1728,128]{1,0:T(8,128)(2,1)S(1)} %reshape.29), channel_id=1, source_target_pairs={{0,8},{1,9},{2,10},{3,11},{4,12},{5,13},{6,14},{7,15},{8,0},{9,1},... | collective-permute-start | bytes 1327112 | tf_op jit(solution)/shard_map/ppermute | solution.py:44
  173.5 2.5 %convolution_select_fusion.2 = f32[32,8,9,128]{3,1,2,0:T(8,128)S(1)} fusion(bf16[34,1,7,2,128]{4,2,3,0,1:T(8,128)(2,1)S(1)} %slice.284, bf16[34,1,8,9,128]{4,2,3,0,1:T(8,128)(2,1)S(1)} %copy.58, pred[8,9]{0,1:T(8,128)(4,1)S(1)} %copy-done.8, bf16[3,3,3,128,128]{4,3,1,2,0:T(8,128)(2,1)} %copy-done.7), kind=kOutput, calls=%fused_computation.28 | convolution fusion | flops 682070016 | bytes 2223176 | tf_op jit(solution)/shard_map/conv_general_dilated | solution.py:102
  176.4 1.0 copy-done.4
  177.7 3.0 %fusion.28 = bf16[32,64,128]{2,1,0:T(8,128)(2,1)} fusion(bf16[32,64,128]{2,1,0:T(8,128)(2,1)S(1)} %copy-done.3, f32[34,66,128]{2,1,0:T(8,128)S(1)} %copy-done.5, f32[38,70,128]{2,1,0:T(8,128)S(1)} %copy-done.4, f32[32,1,64,128]{3,0,2,1:T(8,128)S(1)} %slice.286, s32[3,32,64,128]{3,2,1,0:T(8,128)} %param.6), kind=kLoop, calls=%fused_computation.50 | loop fusion | flops 1835008 | bytes 5242880 | tf_op jit(solution)/shard_map/convert_element_type | solution.py:153
  180.9 1.4 convert.6
  (117 shorter events, 26.2 us)
Async XLA Ops:
  2.5 20.0 %collective-permute-start.4 = (bf16[32,32,128]{2,0,1:T(8,128)(2,1)}, bf16[32,32,128]{2,0,1:T(8,128)(2,1)}, u32[]{:S(2)}, u32[]{:S(2)}) collective-permute-start(bf16[32,32,128]{2,0,1:T(8,128)(2,1)} %copy.65), channel_id=1, source_target_pairs={{0,0},{1,16},{2,32},{3,48},{4,38},{5,39},{6,96},{7,112},{8,8},{9,2... | collective-permute-start | bytes 786440 | tf_op jit(solution)/shard_map/ppermute | solution.py:44
  6.9 13.7 %copy-start = (s32[3,32,64,128]{3,2,1,0:T(8,128)S(1)}, s32[3,32,64,128]{3,2,1,0:T(8,128)}, u32[]{:S(2)}) copy-start(s32[3,32,64,128]{3,2,1,0:T(8,128)} %param.6) | copy-start | bytes 9437188
  6.9 16.4 %collective-permute-start.6 = (bf16[32,32,128]{2,0,1:T(8,128)(2,1)}, bf16[32,32,128]{2,0,1:T(8,128)(2,1)}, u32[]{:S(2)}, u32[]{:S(2)}) collective-permute-start(bf16[32,32,128]{2,0,1:T(8,128)(2,1)} %copy.66), channel_id=1, source_target_pairs={{0,8},{1,24},{2,40},{3,56},{4,98},{5,99},{6,104},{7,120},{8,0},{9,... | collective-permute-start | bytes 786440 | tf_op jit(solution)/shard_map/ppermute | solution.py:44
  10.3 1.0 copy-start.1
  11.3 13.3 %collective-permute-start.1 = (bf16[2,3,64,128]{3,2,1,0:T(8,128)(2,1)S(1)}, bf16[2,3,64,128]{3,2,1,0:T(8,128)(2,1)S(1)}, u32[]{:S(2)}, u32[]{:S(2)}) collective-permute-start(bf16[2,3,64,128]{3,2,1,0:T(8,128)(2,1)S(1)} %get-tuple-element.13), channel_id=1, source_target_pairs={{8,0},{9,1},{10,2},{11,3},{12,4},{13,5},{14,6},{15,7},{16,8},{17,9... | collective-permute-start | bytes 294920 | tf_op jit(solution)/shard_map/ppermute | solution.py:44
  13.3 11.2 %collective-permute-start = (bf16[2,3,64,128]{3,2,1,0:T(8,128)(2,1)S(1)}, bf16[2,3,64,128]{3,2,1,0:T(8,128)(2,1)S(1)}, u32[]{:S(2)}, u32[]{:S(2)}) collective-permute-start(bf16[2,3,64,128]{3,2,1,0:T(8,128)(2,1)S(1)} %get-tuple-element.12), channel_id=1, source_target_pairs={{0,8},{1,9},{2,10},{3,11},{4,12},{5,13},{6,14},{7,15},{8,16},{9,17... | collective-permute-start | bytes 294920 | tf_op jit(solution)/shard_map/ppermute | solution.py:44
  20.7 3.4 %copy-start.6 = (bf16[3,3,3,128,128]{3,4,1,2,0:T(8,128)(2,1)S(1)}, bf16[3,3,3,128,128]{3,4,1,2,0:T(8,128)(2,1)}, u32[]{:S(2)}) copy-start(bf16[3,3,3,128,128]{3,4,1,2,0:T(8,128)(2,1)} %copy.41) | copy-start | bytes 2654212
  22.5 2.0 %copy-start.2 = (bf16[2,32,64,128]{3,2,1,0:T(8,128)(2,1)S(1)}, bf16[2,32,64,128]{3,2,1,0:T(8,128)(2,1)}, u32[]{:S(2)}) copy-start(bf16[2,32,64,128]{3,2,1,0:T(8,128)(2,1)} %copy-done.1) | copy-start | bytes 3145732
  22.5 7.5 %collective-permute-start.5 = (bf16[32,32,128]{2,0,1:T(8,128)(2,1)}, bf16[32,32,128]{2,0,1:T(8,128)(2,1)S(1)}, u32[]{:S(2)}, u32[]{:S(2)}) collective-permute-start(bf16[32,32,128]{2,0,1:T(8,128)(2,1)} %collective-permute-done.4), channel_id=1, source_target_pairs={{38,64},{39,80},{46,72},{47,88},{54,65},{55,81},{62,73},{63,89},{6... | collective-permute-start | bytes 786440 | tf_op jit(solution)/shard_map/ppermute | solution.py:44
  23.4 6.7 %collective-permute-start.7 = (bf16[32,32,128]{2,0,1:T(8,128)(2,1)}, bf16[32,32,128]{2,0,1:T(8,128)(2,1)S(1)}, u32[]{:S(2)}, u32[]{:S(2)}) collective-permute-start(bf16[32,32,128]{2,0,1:T(8,128)(2,1)} %collective-permute-done.6), channel_id=1, source_target_pairs={{98,72},{99,88},{106,64},{107,80},{114,73},{115,89},{122,65},{123,... | collective-permute-start | bytes 786440 | tf_op jit(solution)/shard_map/ppermute | solution.py:44
  24.5 40.4 %copy-start.7 = (bf16[3,3,3,128,128]{4,3,1,2,0:T(8,128)(2,1)}, bf16[3,3,3,128,128]{4,3,1,2,0:T(8,128)(2,1)S(1)}, u32[]{:S(2)}) copy-start(bf16[3,3,3,128,128]{4,3,1,2,0:T(8,128)(2,1)S(1)} %get-tuple-element.18) | copy-start | bytes 2654212
  24.5 6.7 %copy-start.3 = (bf16[32,64,128]{2,1,0:T(8,128)(2,1)S(1)}, bf16[32,64,128]{2,1,0:T(8,128)(2,1)}, u32[]{:S(2)}) copy-start(bf16[32,64,128]{2,1,0:T(8,128)(2,1)} %param.4) | copy-start | bytes 1572868
  24.6 13.9 %collective-permute-start.3 = (bf16[2,38,3,128]{3,2,1,0:T(4,128)(2,1)S(1)}, bf16[2,38,3,128]{3,2,1,0:T(4,128)(2,1)S(1)}, u32[]{:S(2)}, u32[]{:S(2)}) collective-permute-start(bf16[2,38,3,128]{3,2,1,0:T(4,128)(2,1)S(1)} %get-tuple-element.11), channel_id=1, source_target_pairs={{1,0},{2,1},{3,2},{4,3},{5,4},{6,5},{7,6},{9,8},{10,9},{11,10},{12... | collective-permute-start | bytes 175112 | tf_op jit(solution)/shard_map/ppermute | solution.py:44
  26.0 12.5 %collective-permute-start.2 = (bf16[2,38,3,128]{3,2,1,0:T(4,128)(2,1)S(1)}, bf16[2,38,3,128]{3,2,1,0:T(4,128)(2,1)S(1)}, u32[]{:S(2)}, u32[]{:S(2)}) collective-permute-start(bf16[2,38,3,128]{3,2,1,0:T(4,128)(2,1)S(1)} %get-tuple-element.10), channel_id=1, source_target_pairs={{0,1},{1,2},{2,3},{3,4},{4,5},{5,6},{6,7},{8,9},{9,10},{10,11},{11... | collective-permute-start | bytes 175112 | tf_op jit(solution)/shard_map/ppermute | solution.py:44
  31.4 7.9 %collective-permute-start.9 = (bf16[7,64,128]{2,1,0:T(8,128)(2,1)S(1)}, bf16[7,64,128]{2,1,0:T(8,128)(2,1)S(1)}, u32[]{:S(2)}, u32[]{:S(2)}) collective-permute-start(bf16[7,64,128]{2,1,0:T(8,128)(2,1)S(1)} %get-tuple-element.25), channel_id=1, source_target_pairs={{8,0},{9,1},{10,2},{11,3},{12,4},{13,5},{14,6},{15,7},{16,8},{17,9... | collective-permute-start | bytes 344072 | tf_op jit(solution)/shard_map/ppermute | solution.py:44
  33.3 6.9 %collective-permute-start.8 = (bf16[7,64,128]{2,1,0:T(8,128)(2,1)S(1)}, bf16[7,64,128]{2,1,0:T(8,128)(2,1)S(1)}, u32[]{:S(2)}, u32[]{:S(2)}) collective-permute-start(bf16[7,64,128]{2,1,0:T(8,128)(2,1)S(1)} %get-tuple-element.24), channel_id=1, source_target_pairs={{0,8},{1,9},{2,10},{3,11},{4,12},{5,13},{6,14},{7,15},{8,16},{9,17... | collective-permute-start | bytes 344072 | tf_op jit(solution)/shard_map/ppermute | solution.py:44
  40.3 9.8 %collective-permute-start.11 = (bf16[46,7,128]{2,1,0:T(8,128)(2,1)S(1)}, bf16[46,7,128]{2,1,0:T(8,128)(2,1)S(1)}, u32[]{:S(2)}, u32[]{:S(2)}) collective-permute-start(bf16[46,7,128]{2,1,0:T(8,128)(2,1)S(1)} %get-tuple-element.23), channel_id=1, source_target_pairs={{1,0},{2,1},{3,2},{4,3},{5,4},{6,5},{7,6},{9,8},{10,9},{11,10},{12... | collective-permute-start | bytes 247304 | tf_op jit(solution)/shard_map/ppermute | solution.py:44
  41.6 8.5 %collective-permute-start.10 = (bf16[46,7,128]{2,1,0:T(8,128)(2,1)S(1)}, bf16[46,7,128]{2,1,0:T(8,128)(2,1)S(1)}, u32[]{:S(2)}, u32[]{:S(2)}) collective-permute-start(bf16[46,7,128]{2,1,0:T(8,128)(2,1)S(1)} %get-tuple-element.22), channel_id=1, source_target_pairs={{0,1},{1,2},{2,3},{3,4},{4,5},{5,6},{6,7},{8,9},{9,10},{10,11},{11... | collective-permute-start | bytes 247304 | tf_op jit(solution)/shard_map/ppermute | solution.py:44
  48.7 7.3 %collective-permute-start.12 = (bf16[2,35,38,128]{3,0,2,1:T(2,128)(2,1)S(1)}, bf16[2,35,38,128]{3,0,2,1:T(2,128)(2,1)S(1)}, u32[]{:S(2)}, u32[]{:S(2)}) collective-permute-start(bf16[2,35,38,128]{3,0,2,1:T(2,128)(2,1)S(1)} %copy.45), channel_id=1, source_target_pairs={{0,0},{1,16},{2,32},{3,48},{4,38},{5,39},{6,96},{7,112},{8,8},{9,2... | collective-permute-start | bytes 2042888 | tf_op jit(solution)/shard_map/ppermute | solution.py:44
  49.9 6.7 %collective-permute-start.14 = (bf16[2,35,38,128]{3,0,2,1:T(2,128)(2,1)S(1)}, bf16[2,35,38,128]{3,0,2,1:T(2,128)(2,1)S(1)}, u32[]{:S(2)}, u32[]{:S(2)}) collective-permute-start(bf16[2,35,38,128]{3,0,2,1:T(2,128)(2,1)S(1)} %copy.48), channel_id=1, source_target_pairs={{0,8},{1,24},{2,40},{3,56},{4,98},{5,99},{6,104},{7,120},{8,0},{9,... | collective-permute-start | bytes 2042888 | tf_op jit(solution)/shard_map/ppermute | solution.py:44
  52.8 0.8 copy-start.10
  55.9 5.8 %collective-permute-start.13 = (bf16[2,35,38,128]{3,0,2,1:T(2,128)(2,1)S(1)}, bf16[2,35,38,128]{3,0,2,1:T(2,128)(2,1)S(1)}, u32[]{:S(2)}, u32[]{:S(2)}) collective-permute-start(bf16[2,35,38,128]{3,0,2,1:T(2,128)(2,1)S(1)} %collective-permute-done.12), channel_id=1, source_target_pairs={{38,64},{39,80},{46,72},{47,88},{54,65},{55,81},{62,73},{63,89},{6... | collective-permute-start | bytes 2042888 | tf_op jit(solution)/shard_map/ppermute | solution.py:44
  56.6 5.1 %collective-permute-start.15 = (bf16[2,35,38,128]{3,0,2,1:T(2,128)(2,1)S(1)}, bf16[2,35,38,128]{3,0,2,1:T(2,128)(2,1)S(1)}, u32[]{:S(2)}, u32[]{:S(2)}) collective-permute-start(bf16[2,35,38,128]{3,0,2,1:T(2,128)(2,1)S(1)} %collective-permute-done.14), channel_id=1, source_target_pairs={{98,72},{99,88},{106,64},{107,80},{114,73},{115,89},{122,65},{123,... | collective-permute-start | bytes 2042888 | tf_op jit(solution)/shard_map/ppermute | solution.py:44
  64.6 0.7 copy-start.9
  76.3 2.1 %collective-permute-start.16 = (bf16[1728,128]{1,0:T(8,128)(2,1)S(1)}, bf16[1728,128]{1,0:T(8,128)(2,1)}, u32[]{:S(2)}, u32[]{:S(2)}) collective-permute-start(bf16[1728,128]{1,0:T(8,128)(2,1)S(1)} %fusion.82), channel_id=1, source_target_pairs={{0,8},{1,9},{2,10},{3,11},{4,12},{5,13},{6,14},{7,15},{8,0},{9,1},... | collective-permute-start | bytes 1327112 | tf_op jit(solution)/shard_map/ppermute | solution.py:44
  154.3 16.0 %all-to-all-start.1 = ((bf16[64,27,128]{2,1,0:T(8,128)(2,1)}), bf16[64,27,128]{2,1,0:T(8,128)(2,1)S(1)}, u32[]{:S(2)}, u32[]{:S(2)}) async-start(bf16[64,27,128]{2,1,0:T(8,128)(2,1)} %broadcast_in_dim.27), calls=%async_computation.1 | async-start | bytes 1048576 | tf_op jit(solution)/shard_map/all_to_all | solution.py:94
  159.3 14.2 %copy-start.8 = (pred[8,9]{0,1:T(8,128)(4,1)S(1)}, pred[8,9]{0,1:T(8,128)(4,1)}, u32[]{:S(2)}) copy-start(pred[8,9]{0,1:T(8,128)(4,1)} %constant.118) | copy-start | bytes 220
  170.5 10.3 %collective-permute-start.17 = (bf16[1728,128]{1,0:T(8,128)(2,1)S(1)}, bf16[1728,128]{1,0:T(8,128)(2,1)S(1)}, u32[]{:S(2)}, u32[]{:S(2)}) collective-permute-start(bf16[1728,128]{1,0:T(8,128)(2,1)S(1)} %reshape.29), channel_id=1, source_target_pairs={{0,8},{1,9},{2,10},{3,11},{4,12},{5,13},{6,14},{7,15},{8,0},{9,1},... | collective-permute-start | bytes 1327112 | tf_op jit(solution)/shard_map/ppermute | solution.py:44
  176.0 1.4 copy-start.4
  176.0 1.7 copy-start.5

commit v2 on v1

v2 whole, which is shorter than its diff:
```python
import numpy as np
import jax
import jax.numpy as jnp
from jax import lax
from jax.experimental import pallas as pl
from jax.experimental.pallas import tpu as pltpu
from jax.sharding import Mesh, PartitionSpec as P

NAMES = ("y", "xh", "core", "z", "xl")
SIZES = (4, 2, 2, 4, 2)
CHIPS = ("y", "xh", "z", "xl")
BF = jnp.bfloat16
F32 = jnp.float32


def index_grid():
    return np.arange(128).reshape(SIZES)


def neighbour(down, across):
    pairs = []
    for r in range(16):
        for c in range(8):
            if 0 <= r + down < 16 and 0 <= c + across < 8:
                pairs.append((r * 8 + c, (r + down) * 8 + c + across))
    return pairs


def mirror_steps():
    grid = index_grid()
    first, second = [], []
    for y, xh, c, z, xl in np.ndindex(*SIZES):
        source = int(grid[y, xh, c, z, xl])
        target = int(grid[z, xl, c, y, xh])
        if (z - y) % 4 == 2:
            step = 1 if c == 0 else -1
            relay = ((y + step) % 4, xl, c, (z + step) % 4, xh) if c == 0 else ((y + step) % 4, xh, c, (z + step) % 4, xl)
            first.append((source, int(grid[relay])))
            second.append((int(grid[relay]), target))
        else:
            first.append((source, target))
    return first, second


def core_swap():
    grid = index_grid()
    return [
        (int(grid[y, a, c, z, b]), int(grid[y, a, 1 - c, z, b]))
        for y, a, c, z, b in np.ndindex(*SIZES)
    ]


def shift(x, pairs):
    return lax.ppermute(x, NAMES, pairs)


WIDTHS = (7, 1, 3, 1, 3)
STARTS = (0, 7, 8, 11, 12)
VMEM = 50 * 2**20


def roll8(x, by):
    by = by % 8
    return pltpu.roll(x, by, 1) if by else x


def pack_kernel(sym_ref, own_ref, turned_ref, low_ref, high_ref, right_ref, left_ref, edges):
    edges[...] = jnp.zeros_like(edges)
    tiles = (sym_ref, own_ref.at[0], own_ref.at[1], turned_ref.at[0], turned_ref.at[1])
    for k, (tile, w, at) in enumerate(zip(tiles, WIDTHS, STARTS)):
        for side, cols in ((0, slice(48, 64)), (1, slice(0, 16))):
            for rows, part in (
                (slice(8 - w, 8), low_ref[at : at + w, cols]),
                (slice(8, 40), tile[:, cols]),
                (slice(40, 40 + w), high_ref[at : at + w, cols]),
            ):
                wide = part.astype(F32)
                edges[side, k, rows] = wide[:, 8:] if side == 0 else wide[:, :8]
    place = lax.broadcasted_iota(jnp.int32, (48, 8, 128), 1)
    for side, out, moves in ((0, right_ref, (1, 4, 5, 0)), (1, left_ref, (0, 1, 4, 5))):
        one = [roll8(edges[side, 1 + k], by) for k, by in enumerate(moves)]
        block = jnp.where(place == 0, one[0], jnp.where(place < 4, one[1], jnp.where(place == 4, one[2], one[3])))
        out[...] = jnp.concatenate([edges[side, 0], block], axis=1).astype(BF)


def pack(sym, own, turned, low, high):
    shape = jax.ShapeDtypeStruct((48, 16, 128), BF)
    return pl.pallas_call(
        pack_kernel,
        out_shape=(shape, shape),
        scratch_shapes=[pltpu.VMEM((2, 5, 48, 8, 128), F32)],
        compiler_params=pltpu.CompilerParams(vmem_limit_bytes=VMEM),
        name="pack",
    )(sym, own, turned, low, high)


def blocks_kernel(
    sym_ref, own_ref, turned_ref, low_ref, high_ref, left_ref, right_ref, inputs_ref, weights_ref,
    terms_ref, last_ref, ahead_ref, sym, masks, patches, change,
):
    sym[0:1] = jnp.zeros((1, 96, 128), F32)
    sym[47:48] = jnp.zeros((1, 96, 128), F32)
    sym[8:40, 8:72] = sym_ref[...].astype(F32)
    sym[1:8, 8:72] = low_ref[0:7].astype(F32)
    sym[40:47, 8:72] = high_ref[0:7].astype(F32)
    before, after = left_ref[...].astype(F32), right_ref[...].astype(F32)
    sym[:, 80:88] = before[:, :8]
    sym[:, 72:80] = after[:, :8]
    masks[:, 4:8] = jnp.zeros((4, 4, 80, 128), F32)
    masks[:, 40:44] = jnp.zeros((4, 4, 80, 128), F32)
    tiles = (own_ref.at[0], own_ref.at[1], turned_ref.at[0], turned_ref.at[1])
    for k, (lows, highs) in enumerate(((7, 0), (4, 7), (3, 4), (0, 3))):
        w, at = WIDTHS[k + 1], STARTS[k + 1]
        masks[k, 8:40, 0:64] = tiles[k][...].astype(F32)
        masks[k, 8 - w : 8, 0:64] = low_ref[at : at + w].astype(F32)
        masks[k, 40 : 40 + w, 0:64] = high_ref[at : at + w].astype(F32)
        masks[k, :, 72:80] = roll8(before[:, 8:], lows)
        masks[k, :, 64:72] = roll8(after[:, 8:], highs)

    for layer in (2, 1, 0):
        d = 2**layer
        first, count = ((8, 32), (6, 36), (4, 40))[layer]
        sym[:, 0:8] = sym[:, 80:88]
        sym[:, 88:96] = sym[:, 8:16]
        if layer:
            def gather(f, carry):
                for v in range(3):
                    patches[f, :, v * 128 : (v + 1) * 128] = sym[f, 8 + d * (v - 1) : 88 + d * (v - 1)].astype(BF)
                return carry

            lax.fori_loop(first - d, first + count + d, gather, 0, unroll=2)
            source, base = patches, 8
        else:
            def gather(f, carry):
                for v in range(3):
                    last_ref[f - 7, :, v * 128 : (v + 1) * 128] = sym[f, 7 + v : 71 + v].astype(BF)
                return carry

            lax.fori_loop(7, 41, gather, 0, unroll=2)
            source, base = last_ref, 1

        total = None
        for r in (0, 16):
            right = jnp.concatenate(
                [
                    source[base + r + d * (u - 1) : base + r + 16 + d * (u - 1), 0:64].reshape(1024, 384)
                    for u in range(3)
                ],
                axis=1,
            )
            term = jnp.dot(inputs_ref[layer, :, r * 64 : (r + 16) * 64], right, preferred_element_type=F32)
            total = term if total is None else total + term
        for t in range(9):
            terms_ref[layer, 8 - t] = total[:, t * 128 : (t + 1) * 128] * (1.0 / 512.0)
        if layer:
            def step(i, carry):
                f = first + 4 * i
                rows = jnp.concatenate(
                    [patches[pl.ds(f + d * (u - 1), 4)].reshape(320, 384) for u in range(3)], axis=1
                )
                out = jnp.dot(rows, weights_ref[layer], preferred_element_type=F32)
                ahead = masks[layer - 1, pl.ds(f, 4)] * out[:, :128].reshape(4, 80, 128)
                back = masks[layer + 1, pl.ds(f, 4)] * out[:, 128:].reshape(4, 80, 128)
                sym[pl.ds(f, 4), 8:88] = sym[pl.ds(f, 4), 8:88] + 0.5 * (ahead + back)
                if layer == 2:
                    change[pl.ds(f, 4)] = ahead[:, :64]
                else:
                    change[pl.ds(f, 4)] = change[pl.ds(f, 4)] + ahead[:, :64]
                return carry

            lax.fori_loop(0, count // 4, step, 0)
    ahead_ref[...] = change[8:40]


def blocks(sym, own, turned, low, high, left, right, inputs, weights):
    return pl.pallas_call(
        blocks_kernel,
        out_shape=(
            jax.ShapeDtypeStruct((3, 9, 128, 128), F32),
            jax.ShapeDtypeStruct((34, 64, 384), BF),
            jax.ShapeDtypeStruct((32, 64, 128), F32),
        ),
        scratch_shapes=[
            pltpu.VMEM((48, 96, 128), F32),
            pltpu.VMEM((4, 48, 80, 128), F32),
            pltpu.VMEM((48, 80, 384), BF),
            pltpu.VMEM((48, 64, 128), F32),
        ],
        compiler_params=pltpu.CompilerParams(vmem_limit_bytes=VMEM),
        cost_estimate=pl.CostEstimate(flops=8 * 10**9, bytes_accessed=2 * 10**7, transcendentals=0),
        name="blocks",
    )(sym, own, turned, low, high, left, right, inputs, weights)


def last_kernel(patches_ref, weights_ref, mask_ref, cotangent_ref, ahead_ref, out_ref):
    def step(i, carry):
        f = 8 * i
        rows = jnp.concatenate([patches_ref[pl.ds(f + u, 8)].reshape(512, 384) for u in range(3)], axis=1)
        change = jnp.dot(rows, weights_ref[...], preferred_element_type=F32).reshape(8, 64, 128)
        here = pl.ds(f, 8)
        wide = cotangent_ref[here].astype(F32) + ahead_ref[here]
        out_ref[here] = (wide + jnp.where(mask_ref[here] > 0, change, 0.0)).astype(BF)
        return carry

    lax.fori_loop(0, 4, step, 0)


def last(patches, weights, mask, cotangent, ahead):
    return pl.pallas_call(
        last_kernel,
        out_shape=jax.ShapeDtypeStruct((32, 64, 128), BF),
        compiler_params=pltpu.CompilerParams(vmem_limit_bytes=VMEM),
        cost_estimate=pl.CostEstimate(flops=6 * 10**8, bytes_accessed=5 * 10**6, transcendentals=0),
        name="last",
    )(patches, weights, mask, cotangent, ahead)


def mirrored(x):
    core = lax.axis_index("core")
    half = x.shape[2] // 2
    keep = lax.dynamic_slice_in_dim(x, half * core, half, axis=2)
    send = lax.dynamic_slice_in_dim(x, half * (1 - core), half, axis=2)
    got = shift(send, core_swap())
    low = jnp.where(core == 0, keep, got)
    high = jnp.where(core == 0, got, keep)
    piece = jnp.concatenate([low, high], axis=1)
    first, second = mirror_steps()
    direct = shift(piece, first)
    relayed = shift(direct, second)
    far = ((lax.axis_index("z") - lax.axis_index("y")) % 4) == 2
    return jnp.swapaxes(jnp.where(far, relayed, direct), 1, 2)


def total(x):
    core = lax.axis_index("core")
    rows = x.shape[0] // 2
    x = x.reshape(2, rows, 128)
    keep = lax.dynamic_index_in_dim(x, core, 0, False)
    send = lax.dynamic_index_in_dim(x, 1 - core, 0, False).astype(BF)
    swap = core_swap()
    part = (keep + shift(send, swap).astype(F32)).astype(BF).reshape(64, rows // 64, 128)
    terms = lax.all_to_all(part, CHIPS, 0, 0, tiled=True)
    mine = jnp.sum(terms.astype(F32), axis=0).astype(BF)
    copies = jnp.broadcast_to(mine[None], terms.shape)
    whole = lax.all_to_all(copies, CHIPS, 0, 0, tiled=True).reshape(rows, 128)
    other = shift(whole, swap)
    low = jnp.where(core == 0, whole, other)
    high = jnp.where(core == 0, other, whole)
    return jnp.concatenate([low, high], axis=0).astype(F32)


def per_device(cotangent, activations, active_masks, weights):
    channels = cotangent.shape[-1]
    own = (active_masks[1:] > 0).astype(BF)
    flip = mirrored(jnp.concatenate([cotangent[None], own], axis=0))
    sym = ((cotangent.astype(F32) + flip[0].astype(F32)) * 0.5).astype(BF)
    turned = flip[1:]
    parts = [sym, own[0], own[1], turned[0], turned[1]]
    low = shift(jnp.concatenate([p[32 - w :] for p, w in zip(parts, WIDTHS)]), neighbour(1, 0))
    high = shift(jnp.concatenate([p[:w] for p, w in zip(parts, WIDTHS)]), neighbour(-1, 0))
    ends, starts = pack(sym, own, turned, low, high)
    left = shift(ends, neighbour(0, 1))
    right = shift(starts, neighbour(0, -1))

    inputs = jnp.where(active_masks > 0, activations, jnp.zeros_like(activations))
    inputs = inputs.reshape(3, -1, channels).swapaxes(1, 2)
    kernels = weights.reshape(3, 3, 3, channels, channels)[:, ::-1, ::-1].swapaxes(3, 4)
    both = jnp.concatenate([kernels, kernels.swapaxes(1, 2)], axis=-1).reshape(3, -1, 2 * channels)
    terms, patches, ahead = blocks(sym, own, turned, low, high, left, right, inputs, both)
    gradient = last(patches, kernels[0].reshape(-1, channels), active_masks[0], cotangent, ahead)
    return gradient, total(terms.reshape(-1, channels)).reshape(terms.shape)


def solution(mesh):
    fine = Mesh(mesh.devices.reshape(SIZES), NAMES)
    rows, cols = ("y", "xh", "core"), ("z", "xl")
    in_specs = (P(rows, cols, None), P(None, rows, cols, None), P(None, rows, cols, None), P())
    out_specs = (P(rows, cols, None), P())
    return jax.shard_map(per_device, mesh=fine, in_specs=in_specs, out_specs=out_specs, check_vma=False)
```

time: 183 us -> 159 us (0.87)
  blocking collectives: 73.7 us -> 47.8 us
  Pallas kernels: 0 us -> 21.6 us
  starting transfers between devices: 44.1 us -> 54.8 us
  matrix products: 9.63 us -> 0 us
  other arithmetic: 17.7 us -> 9.9 us
  local copies, waits for them, and re-layouts: 22.3 us -> 16.2 us
  waiting for transfers between devices: 13.3 us -> 7.2 us
    all_to_all x1, blocking collectives: 73.7 us -> 32 us  [total(): terms = lax.all_to_all(part, CHIPS, 0, 0, tiled=True)]
    pallas_call x0 -> x3, Pallas kernels: none -> 21.6 us  [the longest x1 15.6 us: blocks(): pl.pallas_call(blocks_kernel, out_shape=(jax.ShapeDtypeStruct((3, 9, 128,...]
    all_to_all x0 -> x1, blocking collectives: none -> 15.8 us  [total(): whole = lax.all_to_all(copies, CHIPS, 0, 0, tiled=True).reshape(rows, 128)]
    ppermute x18 -> x9, starting transfers between devices: 39.2 us -> 54.8 us  [shift(): return lax.ppermute(x, NAMES, pairs)]
    all_to_all x1 -> x0, waiting for transfers between devices: 10.8 us -> none  [total(): whole = lax.all_to_all(copies, CHIPS, 0, 0, tiled=True).reshape(rows, 128)]
    convert_element_type x5 -> x2, other arithmetic: 8.82 us -> 2.15 us  [the longest x1 1.96 us: per_device(): own = (active_masks[1:] > 0).astype(BF)]
    conv_general_dilated x3 -> x0, matrix products: 6.58 us -> none  [conv(): lax.conv_general_dilated(sym[None], kernel, (1, 1), 'VALID', rhs_dilation...]
    unnamed x51 -> x22, local copies, waits for them, and re-layouts: 10.5 us -> 4.19 us
  transfers between devices with their start and end apart: 19 -> 9, of which waited for: 3 -> 4; matrix products, arithmetic and copies ran while one was open for 15% -> 8% of each run, Pallas kernels for 0% -> 3%
where the time goes in v2:
time: 159 us; the launch traced here: 158 us
  starting transfers between devices  54.8 us (34%)
  blocking collectives  47.8 us (30%)
  Pallas kernels  21.6 us (14%)
  local copies, waits for them, and re-layouts  16.2 us (10%)
  other arithmetic  9.9 us (6%)
  waiting for transfers between devices  7.2 us (5%)
    ppermute x9, starting transfers between devices, shift(): return lax.ppermute(x, NAMES, pairs)  54.8 us
    all_to_all x1, blocking collectives, total(): terms = lax.all_to_all(part, CHIPS, 0, 0, tiled=True)  32 us
    all_to_all x1, blocking collectives, total(): whole = lax.all_to_all(copies, CHIPS, 0, 0, tiled=True).reshape(rows, 128)  15.8 us
    pallas_call x1, Pallas kernels, blocks(): pl.pallas_call(blocks_kernel, out_shape=(jax.ShapeDtypeStruct((3, 9, 128,...  15.6 us
    ppermute x9, waiting for transfers between devices, shift(): return lax.ppermute(x, NAMES, pairs)  7.2 us
    unnamed x22, local copies, waits for them, and re-layouts  4.19 us
    pallas_call x1, Pallas kernels, last(): pl.pallas_call(last_kernel, out_shape=jax.ShapeDtypeStruct((32, 64, 128),...  4.17 us
  transfers between devices with their start and end apart: 9, of which 4 were waited for; matrix products, arithmetic and copies ran while one was open for 8% of the time, Pallas kernels for 3%

profile of v2, /device:TPU:1, one launch (start us, length us, event | category | flops | bytes accessed | tf_op | source)
XLA Modules:
  0.0 158.3 jit_solution(10384056401112825647)
XLA Ops:
  0.6 2.0 %fusion.own_ref = bf16[2,32,64,128]{3,2,1,0:T(8,128)(2,1)S(1)} fusion(s32[3,32,64,128]{3,2,1,0:T(8,128)} %param.6), kind=kLoop, calls=%fused_computation.2 | loop fusion | flops 1048576 | bytes 3145728 | tf_op jit(solution)/shard_map/convert_element_type | solution.py:254
  2.7 1.5 collective-permute-start
  4.2 1.9 %collective-permute-done = bf16[3,32,32,128]{3,2,1,0:T(8,128)(2,1)S(1)} collective-permute-done((bf16[3,32,32,128]{3,2,1,0:T(8,128)(2,1)S(1)}, bf16[3,32,32,128]{3,2,1,0:T(8,128)(2,1)S(1)}, u32[]{:S(2)}, u32[]{:S(2)}) %collective-permute-start) | collective-permute-done | bytes 786464 | tf_op jit(solution)/shard_map/ppermute | solution.py:54
  6.6 0.8 collective-permute-start.1
  7.4 1.8 %collective-permute-start.2 = (bf16[3,64,32,128]{3,2,1,0:T(8,128)(2,1)S(1)}, bf16[3,64,32,128]{3,2,1,0:T(8,128)(2,1)}, u32[]{:S(2)}, u32[]{:S(2)}) collective-permute-start(bf16[3,64,32,128]{3,2,1,0:T(8,128)(2,1)S(1)} %collective-permute-done.1), channel_id=1, source_target_pairs={{38,64},{54,80},{106,72},{107,88},{39,65},{55,81},{122,73},{123,89... | collective-permute-start | bytes 4718600 | tf_op jit(solution)/shard_map/ppermute | solution.py:54
  10.3 0.7 slice_dynamic-update-slice_fusion
  13.4 42.5 %collective-permute-start.3 = (bf16[15,64,128]{2,1,0:T(8,128)(2,1)}, bf16[15,64,128]{2,1,0:T(8,128)(2,1)S(1)}, u32[]{:S(2)}, u32[]{:S(2)}) collective-permute-start(bf16[15,64,128]{2,1,0:T(8,128)(2,1)} %get-tuple-element.15), channel_id=1, source_target_pairs={{0,8},{1,9},{2,10},{3,11},{4,12},{5,13},{6,14},{7,15},{8,16},{9,17... | collective-permute-start | bytes 737288 | tf_op jit(solution)/shard_map/ppermute | solution.py:54
  56.0 1.9 %collective-permute-start.4 = (bf16[15,64,128]{2,1,0:T(8,128)(2,1)}, bf16[15,64,128]{2,1,0:T(8,128)(2,1)}, u32[]{:S(2)}, u32[]{:S(2)}) collective-permute-start(bf16[15,64,128]{2,1,0:T(8,128)(2,1)} %get-tuple-element.14), channel_id=1, source_target_pairs={{8,0},{9,1},{10,2},{11,3},{12,4},{13,5},{14,6},{15,7},{16,8},{17,9... | collective-permute-start | bytes 737288 | tf_op jit(solution)/shard_map/ppermute | solution.py:54
  57.9 1.5 compare_select_fusion
  59.4 2.0 %copy.12 = bf16[3,3,3,128,128]{3,4,1,2,0:T(8,128)(2,1)S(1)} copy(bf16[3,3,3,128,128]{4,3,2,1,0:T(8,128)(2,1)} %bitcast.74) | data formatting | bytes 1769472 | tf_op jit(solution)/shard_map/reshape | solution.py:267
  61.4 0.9 copy-done.3
  62.4 1.0 copy_bitcast_fusion.1
  63.4 0.7 copy-done.6
  64.2 1.1 collective-permute-done.4.high_ref
  65.3 1.8 %pack.1 = (bf16[48,16,128]{2,1,0:T(8,128)(2,1)}, bf16[48,16,128]{2,1,0:T(8,128)(2,1)}) custom-call(bf16[32,64,128]{2,1,0:T(8,128)(2,1)S(1)} %fusion.2.sym_ref, bf16[2,32,64,128]{3,2,1,0:T(8,128)(2,1)S(1)} %fusion.own_ref, bf16[2,32,64,128]{3,2,1,0:T(8,128)(2,1)S(1)} %slice.107.turned_ref, bf16[15,64,128]{2,1,0:T(8,128)(2,1)S(1)} %collective-permute-done.3.low_ref, ...), custom_call_target="tpu_custom_call" | custom-call | tf_op jit(solution)/shard_map/pack/pallas_call | solution.py:88
  67.1 2.0 %collective-permute-start.5 = (bf16[48,16,128]{2,1,0:T(8,128)(2,1)}, bf16[48,16,128]{2,1,0:T(8,128)(2,1)}, u32[]{:S(2)}, u32[]{:S(2)}) collective-permute-start(bf16[48,16,128]{2,1,0:T(8,128)(2,1)} %get-tuple-element.7), channel_id=1, source_target_pairs={{0,1},{1,2},{2,3},{3,4},{4,5},{5,6},{6,7},{8,9},{9,10},{10,11},{11... | collective-permute-start | bytes 589832 | tf_op jit(solution)/shard_map/ppermute | solution.py:54
  69.1 1.3 collective-permute-start.6
  70.4 1.0 reverse_bitcast_fusion
  71.4 2.7 %copy.11 = bf16[3,2048,128]{1,2,0:T(8,128)(2,1)} copy(bf16[3,2048,128]{2,1,0:T(8,128)(2,1)} %bitcast.68) | data formatting | bytes 3145728 | tf_op jit(solution)/shard_map/reshape | solution.py:266
  74.1 2.6 %pad_maximum_fusion = bf16[3,3,3,128,256]{4,3,2,1,0:T(8,128)(2,1)} fusion(bf16[3,3,3,128,128]{4,3,2,1,0:T(8,128)(2,1)} %reverse_bitcast_fusion, bf16[3,3,3,128,128]{4,3,2,1,0:T(8,128)(2,1)S(1)} %copy-done.7), kind=kLoop, calls=%fused_computation.5 | loop fusion | flops 3538944 | bytes 3538944 | tf_op jit(solution)/shard_map/concatenate | solution.py:268
  76.7 2.4 %collective-permute-done.6.right_ref = bf16[48,16,128]{2,1,0:T(8,128)(2,1)} collective-permute-done((bf16[48,16,128]{2,1,0:T(8,128)(2,1)}, bf16[48,16,128]{2,1,0:T(8,128)(2,1)}, u32[]{:S(2)}, u32[]{:S(2)}) %collective-permute-start.6) | collective-permute-done | bytes 196640 | tf_op jit(solution)/shard_map/ppermute | solution.py:54
  79.1 15.6 %blocks.1 = (f32[3,9,128,128]{3,2,1,0:T(8,128)}, bf16[34,64,384]{2,1,0:T(8,128)(2,1)}, f32[32,64,128]{2,1,0:T(8,128)S(1)}) custom-call(bf16[32,64,128]{2,1,0:T(8,128)(2,1)S(1)} %fusion.2.sym_ref, bf16[2,32,64,128]{3,2,1,0:T(8,128)(2,1)S(1)} %fusion.own_ref, bf16[2,32,64,128]{3,2,1,0:T(8,128)(2,1)} %copy-done.1, ...), custom_call_target="tpu_custom_call" | custom-call | flops 8000000000 | bytes 20000000 | tf_op jit(solution)/shard_map/blocks/pallas_call | solution.py:176
  94.7 1.2 fusion.6
  96.0 1.8 %collective-permute-done.7 = bf16[1728,128]{1,0:T(8,128)(2,1)S(1)} collective-permute-done((bf16[1728,128]{1,0:T(8,128)(2,1)S(1)}, bf16[1728,128]{1,0:T(8,128)(2,1)S(1)}, u32[]{:S(2)}, u32[]{:S(2)}) %collective-permute-start.7) | collective-permute-done | bytes 442400 | tf_op jit(solution)/shard_map/ppermute | solution.py:54
  97.8 1.3 fusion.3
  99.2 32.0 %all_to_all.10 = bf16[64,27,128]{2,1,0:T(8,128)(2,1)S(1)} all-to-all(bf16[64,27,128]{2,1,0:T(8,128)(2,1)S(1)} %reshape.38), channel_id=1, replica_groups=mesh['y'=4,'xh'=2,'core'=2,'z'=4,'xl'=2] {'y','xh','z','xl'}, dimensions={0} | all-to-all | bytes 884736 | tf_op jit(solution)/shard_map/all_to_all | solution.py:242
  131.4 15.8 %all_to_all.11 = bf16[64,27,128]{2,1,0:T(8,128)(2,1)S(1)} all-to-all(bf16[64,27,128]{2,1,0:T(8,128)(2,1)S(1)} %broadcast_in_dim.14), channel_id=1, replica_groups=mesh['y'=4,'xh'=2,'core'=2,'z'=4,'xl'=2] {'y','xh','z','xl'}, dimensions={0} | all-to-all | bytes 884736 | tf_op jit(solution)/shard_map/all_to_all | solution.py:245
  147.3 2.9 %collective-permute-start.8 = (bf16[1728,128]{1,0:T(8,128)(2,1)S(1)}, bf16[1728,128]{1,0:T(8,128)(2,1)S(1)}, u32[]{:S(2)}, u32[]{:S(2)}) collective-permute-start(bf16[1728,128]{1,0:T(8,128)(2,1)S(1)} %reshape.39), channel_id=1, source_target_pairs={{0,8},{1,9},{2,10},{3,11},{4,12},{5,13},{6,14},{7,15},{8,0},{9,1},... | collective-permute-start | bytes 1327112 | tf_op jit(solution)/shard_map/ppermute | solution.py:54
  150.3 1.0 slice.118
  151.3 1.3 slice_bitcast_fusion.mask_ref
  152.6 4.2 %last.1 = bf16[32,64,128]{2,1,0:T(8,128)(2,1)} custom-call(bf16[34,64,384]{2,1,0:T(8,128)(2,1)} %get-tuple-element.9.patches_ref, bf16[1152,128]{1,0:T(8,128)(2,1)S(1)} %bitcast.63, s32[32,64,128]{2,1,0:T(8,128)S(1)} %slice_bitcast_fusion.mask_ref, bf16[32,64,128]{2,1,0:T(8,128)(2,1)S(1)} %copy-done, f32[32,64,128]{2,1,0:T(8,128)S(1)} %get-tuple-element.10.ahead_ref), custom_call_target="tpu_custom_call" | custom-call | flops 600000000 | bytes 5000000 | tf_op jit(solution)/shard_map/last/pallas_call | solution.py:209
  156.9 1.4 convert.4
  (39 shorter events, 4.8 us)
Async XLA Ops:
  0.6 2.0 %copy-start = (bf16[32,64,128]{2,1,0:T(8,128)(2,1)S(1)}, bf16[32,64,128]{2,1,0:T(8,128)(2,1)}, u32[]{:S(2)}) copy-start(bf16[32,64,128]{2,1,0:T(8,128)(2,1)} %cotangent_ref.1) | copy-start | bytes 1572868
  2.7 3.4 %collective-permute-start = (bf16[3,32,32,128]{3,2,1,0:T(8,128)(2,1)S(1)}, bf16[3,32,32,128]{3,2,1,0:T(8,128)(2,1)S(1)}, u32[]{:S(2)}, u32[]{:S(2)}) collective-permute-start(bf16[3,32,32,128]{3,2,1,0:T(8,128)(2,1)S(1)} %fusion.4), channel_id=1, source_target_pairs={{0,8},{1,9},{2,10},{3,11},{4,12},{5,13},{6,14},{7,15},{8,0},{9,1},... | collective-permute-start | bytes 2359304 | tf_op jit(solution)/shard_map/ppermute | solution.py:54
  6.6 0.8 collective-permute-start.1
  7.4 1.8 %collective-permute-start.2 = (bf16[3,64,32,128]{3,2,1,0:T(8,128)(2,1)S(1)}, bf16[3,64,32,128]{3,2,1,0:T(8,128)(2,1)}, u32[]{:S(2)}, u32[]{:S(2)}) collective-permute-start(bf16[3,64,32,128]{3,2,1,0:T(8,128)(2,1)S(1)} %collective-permute-done.1), channel_id=1, source_target_pairs={{38,64},{54,80},{106,72},{107,88},{39,65},{55,81},{122,73},{123,89... | collective-permute-start | bytes 4718600 | tf_op jit(solution)/shard_map/ppermute | solution.py:54
  9.4 48.5 %copy-start.2 = (s32[3,32,64,128]{3,2,1,0:T(8,128)S(1)}, s32[3,32,64,128]{3,2,1,0:T(8,128)}, u32[]{:S(2)}) copy-start(s32[3,32,64,128]{3,2,1,0:T(8,128)} %param.6) | copy-start | bytes 9437188
  10.0 3.4 %copy-start.5 = (bf16[3,64,32,128]{3,1,2,0:T(8,128)(2,1)}, bf16[3,64,32,128]{3,1,2,0:T(8,128)(2,1)S(1)}, u32[]{:S(2)}) copy-start(bf16[3,64,32,128]{3,1,2,0:T(8,128)(2,1)S(1)} %copy.16) | copy-start | bytes 4718596
  10.0 47.9 %copy-start.8 = (bf16[3,32,64,128]{3,2,1,0:T(8,128)(2,1)S(1)}, bf16[3,32,64,128]{3,2,1,0:T(8,128)(2,1)}, u32[]{:S(2)}) copy-start(bf16[3,32,64,128]{3,2,1,0:T(8,128)(2,1)} %param.5) | copy-start | bytes 4718596
  13.4 50.7 %collective-permute-start.3 = (bf16[15,64,128]{2,1,0:T(8,128)(2,1)}, bf16[15,64,128]{2,1,0:T(8,128)(2,1)S(1)}, u32[]{:S(2)}, u32[]{:S(2)}) collective-permute-start(bf16[15,64,128]{2,1,0:T(8,128)(2,1)} %get-tuple-element.15), channel_id=1, source_target_pairs={{0,8},{1,9},{2,10},{3,11},{4,12},{5,13},{6,14},{7,15},{8,16},{9,17... | collective-permute-start | bytes 737288 | tf_op jit(solution)/shard_map/ppermute | solution.py:54
  56.0 9.3 %collective-permute-start.4 = (bf16[15,64,128]{2,1,0:T(8,128)(2,1)}, bf16[15,64,128]{2,1,0:T(8,128)(2,1)}, u32[]{:S(2)}, u32[]{:S(2)}) collective-permute-start(bf16[15,64,128]{2,1,0:T(8,128)(2,1)} %get-tuple-element.14), channel_id=1, source_target_pairs={{8,0},{9,1},{10,2},{11,3},{12,4},{13,5},{14,6},{15,7},{16,8},{17,9... | collective-permute-start | bytes 737288 | tf_op jit(solution)/shard_map/ppermute | solution.py:54
  61.4 0.9 copy-start.3
  62.4 1.7 %copy-start.6 = (bf16[3,64,32,128]{3,1,2,0:T(8,128)(2,1)S(1)}, bf16[3,64,32,128]{3,1,2,0:T(8,128)(2,1)}, u32[]{:S(2)}) copy-start(bf16[3,64,32,128]{3,1,2,0:T(8,128)(2,1)} %copy-done.5) | copy-start | bytes 4718596
  64.2 7.2 %copy-start.1 = (bf16[2,32,64,128]{3,2,1,0:T(8,128)(2,1)}, bf16[2,32,64,128]{3,2,1,0:T(8,128)(2,1)S(1)}, u32[]{:S(2)}) copy-start(bf16[2,32,64,128]{3,2,1,0:T(8,128)(2,1)S(1)} %slice.107.turned_ref) | copy-start | bytes 3145732
  64.2 6.2 %copy-start.4 = (bf16[3,3,3,128,128]{3,4,1,2,0:T(8,128)(2,1)S(1)}, bf16[3,3,3,128,128]{3,4,1,2,0:T(8,128)(2,1)}, u32[]{:S(2)}) copy-start(bf16[3,3,3,128,128]{3,4,1,2,0:T(8,128)(2,1)} %copy-done.3) | copy-start | bytes 2654212
  67.1 9.6 %collective-permute-start.5 = (bf16[48,16,128]{2,1,0:T(8,128)(2,1)}, bf16[48,16,128]{2,1,0:T(8,128)(2,1)}, u32[]{:S(2)}, u32[]{:S(2)}) collective-permute-start(bf16[48,16,128]{2,1,0:T(8,128)(2,1)} %get-tuple-element.7), channel_id=1, source_target_pairs={{0,1},{1,2},{2,3},{3,4},{4,5},{5,6},{6,7},{8,9},{9,10},{10,11},{11... | collective-permute-start | bytes 589832 | tf_op jit(solution)/shard_map/ppermute | solution.py:54
  69.1 10.0 %collective-permute-start.6 = (bf16[48,16,128]{2,1,0:T(8,128)(2,1)}, bf16[48,16,128]{2,1,0:T(8,128)(2,1)}, u32[]{:S(2)}, u32[]{:S(2)}) collective-permute-start(bf16[48,16,128]{2,1,0:T(8,128)(2,1)} %get-tuple-element.8), channel_id=1, source_target_pairs={{1,0},{2,1},{3,2},{4,3},{5,4},{6,5},{7,6},{9,8},{10,9},{11,10},{12... | collective-permute-start | bytes 589832 | tf_op jit(solution)/shard_map/ppermute | solution.py:54
  71.4 2.7 %copy-start.7 = (bf16[3,3,3,128,128]{4,3,2,1,0:T(8,128)(2,1)S(1)}, bf16[3,3,3,128,128]{4,3,2,1,0:T(8,128)(2,1)}, u32[]{:S(2)}) copy-start(bf16[3,3,3,128,128]{4,3,2,1,0:T(8,128)(2,1)} %copy_bitcast_fusion.1) | copy-start | bytes 2654212
  95.9 1.9 %collective-permute-start.7 = (bf16[1728,128]{1,0:T(8,128)(2,1)S(1)}, bf16[1728,128]{1,0:T(8,128)(2,1)S(1)}, u32[]{:S(2)}, u32[]{:S(2)}) collective-permute-start(bf16[1728,128]{1,0:T(8,128)(2,1)S(1)} %fusion.6), channel_id=1, source_target_pairs={{0,8},{1,9},{2,10},{3,11},{4,12},{5,13},{6,14},{7,15},{8,0},{9,1},... | collective-permute-start | bytes 1327112 | tf_op jit(solution)/shard_map/ppermute | solution.py:54
  147.3 9.4 %collective-permute-start.8 = (bf16[1728,128]{1,0:T(8,128)(2,1)S(1)}, bf16[1728,128]{1,0:T(8,128)(2,1)S(1)}, u32[]{:S(2)}, u32[]{:S(2)}) collective-permute-start(bf16[1728,128]{1,0:T(8,128)(2,1)S(1)} %reshape.39), channel_id=1, source_target_pairs={{0,8},{1,9},{2,10},{3,11},{4,12},{5,13},{6,14},{7,15},{8,0},{9,1},... | collective-permute-start | bytes 1327112 | tf_op jit(solution)/shard_map/ppermute | solution.py:54

commit v3 on v2

v3 whole, which is shorter than its diff:
```python
import numpy as np
import jax
import jax.numpy as jnp
from jax import lax
from jax.experimental import pallas as pl
from jax.experimental.layout import Layout, with_layout_constraint
from jax.experimental.pallas import tpu as pltpu
from jax.sharding import Mesh, PartitionSpec as P

NAMES = ("y", "xh", "core", "z", "xl")
SIZES = (4, 2, 2, 4, 2)
CHIPS = ("y", "xh", "z", "xl")
BF = jnp.bfloat16
F32 = jnp.float32


def index_grid():
    return np.arange(128).reshape(SIZES)


def neighbour(down, across):
    pairs = []
    for r in range(16):
        for c in range(8):
            if 0 <= r + down < 16 and 0 <= c + across < 8:
                pairs.append((r * 8 + c, (r + down) * 8 + c + across))
    return pairs


def mirror_steps():
    grid = index_grid()
    first, second = [], []
    for y, xh, c, z, xl in np.ndindex(*SIZES):
        source = int(grid[y, xh, c, z, xl])
        target = int(grid[z, xl, c, y, xh])
        if (z - y) % 4 == 2:
            step = 1 if c == 0 else -1
            relay = ((y + step) % 4, xl, c, (z + step) % 4, xh) if c == 0 else ((y + step) % 4, xh, c, (z + step) % 4, xl)
            first.append((source, int(grid[relay])))
            second.append((int(grid[relay]), target))
        else:
            first.append((source, target))
    return first, second


def core_swap():
    grid = index_grid()
    return [
        (int(grid[y, a, c, z, b]), int(grid[y, a, 1 - c, z, b]))
        for y, a, c, z, b in np.ndindex(*SIZES)
    ]


def shift(x, pairs):
    return lax.ppermute(x, NAMES, pairs)


WIDTHS = (7, 1, 3, 1, 3)
STARTS = (0, 7, 8, 11, 12)
STEPS = (32, 18, 20)


def roll8(x, by):
    by = by % 8
    return pltpu.roll(x, by, 1) if by else x


def call(body, name, out_shape, *args, scratch=(), flops=10**6, moved=10**6, room=8, far=0):
    return pl.pallas_call(
        body,
        out_shape=out_shape,
        in_specs=[pl.BlockSpec(memory_space=pltpu.VMEM)] * (len(args) - far) + [pl.BlockSpec(memory_space=pltpu.HBM)] * far,
        scratch_shapes=list(scratch),
        compiler_params=pltpu.CompilerParams(vmem_limit_bytes=room * 2**20),
        cost_estimate=pl.CostEstimate(flops=flops, bytes_accessed=moved, transcendentals=0),
        name=name,
    )(*args)


def symmetric_kernel(cotangent_ref, flip_ref, own_ref, sym_ref, down_ref, up_ref):
    wide = cotangent_ref[...].astype(F32) + flip_ref[0].astype(F32)
    sym_ref[...] = (wide * 0.5).astype(BF)
    tiles = (sym_ref, own_ref.at[0], own_ref.at[1], flip_ref.at[1], flip_ref.at[2])
    for tile, w, at in zip(tiles, WIDTHS, STARTS):
        down_ref[at : at + w] = tile[32 - w : 32]
        up_ref[at : at + w] = tile[0:w]


def pack_kernel(sym_ref, own_ref, flip_ref, low_ref, high_ref, ends_ref, starts_ref, edges):
    edges[...] = jnp.zeros_like(edges)
    tiles = (sym_ref, own_ref.at[0], own_ref.at[1], flip_ref.at[1], flip_ref.at[2])
    for k, (tile, w, at) in enumerate(zip(tiles, WIDTHS, STARTS)):
        for side, cols in ((0, slice(48, 64)), (1, slice(0, 16))):
            for rows, part in (
                (slice(8 - w, 8), low_ref[at : at + w, cols]),
                (slice(8, 40), tile[:, cols]),
                (slice(40, 40 + w), high_ref[at : at + w, cols]),
            ):
                wide = part.astype(F32)
                edges[side, k, rows] = wide[:, 8:] if side == 0 else wide[:, :8]
    place = lax.broadcasted_iota(jnp.int32, (48, 8, 128), 1)
    for side, out, moves in ((0, ends_ref, (1, 4, 5, 0)), (1, starts_ref, (0, 1, 4, 5))):
        one = [roll8(edges[side, 1 + k], by) for k, by in enumerate(moves)]
        block = jnp.where(place == 0, one[0], jnp.where(place < 4, one[1], jnp.where(place == 4, one[2], one[3])))
        out[...] = jnp.concatenate([edges[side, 0], block], axis=1).astype(BF)


def blocks_kernel(
    sym_ref, own_ref, flip_ref, low_ref, high_ref, left_ref, right_ref,
    cotangent_hbm, mask_hbm, inputs_hbm, weights_hbm, gradient_ref, terms_ref,
    sym, masks, patches, change, cotangent_ref, mask_ref, inputs_ref, weights_ref, arrived,
):
    copies = []
    for n, (far, near) in enumerate((
        (inputs_hbm, inputs_ref), (weights_hbm, weights_ref), (cotangent_hbm, cotangent_ref), (mask_hbm, mask_ref),
    )):
        copies.append(pltpu.make_async_copy(far, near, arrived.at[n]))
        copies[-1].start()
    sym[0:1] = jnp.zeros((1, 96, 128), F32)
    sym[47:48] = jnp.zeros((1, 96, 128), F32)
    sym[8:40, 8:72] = sym_ref[...].astype(F32)
    sym[1:8, 8:72] = low_ref[0:7].astype(F32)
    sym[40:47, 8:72] = high_ref[0:7].astype(F32)
    before, after = left_ref[...].astype(F32), right_ref[...].astype(F32)
    sym[:, 80:88] = before[:, :8]
    sym[:, 72:80] = after[:, :8]
    masks[:, 4:8] = jnp.zeros((4, 4, 80, 128), F32)
    masks[:, 40:44] = jnp.zeros((4, 4, 80, 128), F32)
    tiles = (own_ref.at[0], own_ref.at[1], flip_ref.at[1], flip_ref.at[2])
    for k, (lows, highs) in enumerate(((7, 0), (4, 7), (3, 4), (0, 3))):
        w, at = WIDTHS[k + 1], STARTS[k + 1]
        masks[k, 8:40, 0:64] = tiles[k][...].astype(F32)
        masks[k, 8 - w : 8, 0:64] = low_ref[at : at + w].astype(F32)
        masks[k, 40 : 40 + w, 0:64] = high_ref[at : at + w].astype(F32)
        masks[k, :, 72:80] = roll8(before[:, 8:], lows)
        masks[k, :, 64:72] = roll8(after[:, 8:], highs)

    for layer in (2, 1, 0):
        for copy in {2: copies[:2], 1: (), 0: copies[2:]}[layer]:
            copy.wait()
        d = 2**layer
        first, count = ((8, 32), (6, 36), (4, 40))[layer]
        sym[:, 0:8] = sym[:, 80:88]
        sym[:, 88:96] = sym[:, 8:16]

        def gather(f, carry):
            for v in range(3):
                patches[f, :, v * 128 : (v + 1) * 128] = sym[f, 8 + d * (v - 1) : 88 + d * (v - 1)].astype(BF)
            return carry

        lax.fori_loop(first - d, first + count + d, gather, 0, unroll=2)
        total = None
        for r in (8, 24):
            right = jnp.concatenate(
                [patches[r + d * (u - 1) : r + 16 + d * (u - 1), 0:64].reshape(1024, 384) for u in range(3)], axis=1
            )
            term = jnp.dot(inputs_ref[layer, :, (r - 8) * 64 : (r + 8) * 64], right, preferred_element_type=F32)
            total = term if total is None else total + term
        for t in range(9):
            terms_ref[layer, 8 - t] = total[:, t * 128 : (t + 1) * 128] * (1.0 / 512.0)
        if layer:
            def step(i, carry):
                f = first + size * i
                here = pl.ds(f, size)
                rows = jnp.concatenate(
                    [patches[pl.ds(f + d * (u - 1), size)].reshape(size * 80, 384) for u in range(3)], axis=1
                )
                out = jnp.dot(rows, weights_ref[layer], preferred_element_type=F32)
                ahead = masks[layer - 1, here] * out[:, :128].reshape(size, 80, 128)
                back = masks[layer + 1, here] * out[:, 128:].reshape(size, 80, 128)
                sym[here, 8:88] = sym[here, 8:88] + 0.5 * (ahead + back)
                if layer == 2:
                    change[here] = ahead[:, :64]
                else:
                    change[here] = change[here] + ahead[:, :64]
                return carry

            size = STEPS[layer]
            lax.fori_loop(0, count // size, step, 0)
        else:
            def step(i, carry):
                f = size * i
                rows = jnp.concatenate(
                    [patches[pl.ds(7 + f + u, size), 0:64].reshape(size * 64, 384) for u in range(3)], axis=1
                )
                out = jnp.dot(rows, weights_ref[0, :, :128], preferred_element_type=F32).reshape(size, 64, 128)
                here = pl.ds(f, size)
                wide = cotangent_ref[here].astype(F32) + change[pl.ds(8 + f, size)]
                gradient_ref[here] = (wide + mask_ref[here].astype(F32) * out).astype(BF)
                return carry

            size = STEPS[0]
            lax.fori_loop(0, 32 // size, step, 0)


def paired(x):
    core = lax.axis_index("core")
    half = x.shape[2] // 2
    keep = lax.dynamic_slice_in_dim(x, half * core, half, axis=2)
    send = lax.dynamic_slice_in_dim(x, half * (1 - core), half, axis=2)
    got = shift(send, core_swap())
    low = jnp.where(core == 0, keep, got)
    high = jnp.where(core == 0, got, keep)
    return with_layout_constraint(jnp.concatenate([low, high], axis=1), Layout((0, 1, 2, 3)))


def turn(direct, relayed):
    far = ((lax.axis_index("z") - lax.axis_index("y")) % 4) == 2
    arrived = with_layout_constraint(jnp.where(far, relayed, direct), Layout((0, 1, 2, 3)))
    return jnp.swapaxes(arrived, -3, -2)


def total(x):
    core = lax.axis_index("core")
    rows = x.shape[0] // 2
    x = x.reshape(2, rows, 128)
    keep = lax.dynamic_index_in_dim(x, core, 0, False)
    send = lax.dynamic_index_in_dim(x, 1 - core, 0, False).astype(BF)
    swap = core_swap()
    part = (keep + shift(send, swap).astype(F32)).astype(BF).reshape(64, rows // 64, 128)
    terms = lax.all_to_all(part, CHIPS, 0, 0, tiled=True)
    mine = jnp.sum(terms.astype(F32), axis=0).astype(BF)
    copies = jnp.broadcast_to(mine[None], terms.shape)
    whole = lax.all_to_all(copies, CHIPS, 0, 0, tiled=True).reshape(rows, 128)
    other = shift(whole, swap)
    low = jnp.where(core == 0, whole, other)
    high = jnp.where(core == 0, other, whole)
    return jnp.concatenate([low, high], axis=0).astype(F32)


def per_device(cotangent, activations, active_masks, weights):
    channels = cotangent.shape[-1]
    own = (active_masks[1:] > 0).astype(BF)
    piece = paired(jnp.concatenate([cotangent[None], own], axis=0))
    first, second = mirror_steps()
    direct = shift(piece, first)
    bottom = (active_masks[0] > 0).astype(BF)
    inputs = jnp.where(active_masks > 0, activations, jnp.zeros_like(activations))
    inputs = inputs.reshape(3, -1, channels).swapaxes(1, 2)
    kernels = weights.reshape(3, 3, 3, channels, channels)[:, ::-1, ::-1].swapaxes(3, 4)
    both = jnp.concatenate([kernels, kernels.swapaxes(1, 2)], axis=-1).reshape(3, -1, 2 * channels)
    direct, bottom, inputs, both = lax.optimization_barrier((direct, bottom, inputs, both))

    flip = turn(direct, shift(direct, second))
    tile = jax.ShapeDtypeStruct((32, 64, 128), BF)
    strip = jax.ShapeDtypeStruct((15, 64, 128), BF)
    sym, down, up = call(symmetric_kernel, "symmetric", (tile, strip, strip), cotangent, flip, own)
    low, high = shift(down, neighbour(1, 0)), shift(up, neighbour(-1, 0))
    edge = jax.ShapeDtypeStruct((48, 16, 128), BF)
    ends, starts = call(
        pack_kernel, "pack", (edge, edge), sym, own, flip, low, high, scratch=[pltpu.VMEM((2, 5, 48, 8, 128), F32)]
    )
    left, right = shift(ends, neighbour(0, 1)), shift(starts, neighbour(0, -1))
    gradient, terms = call(
        blocks_kernel, "blocks", (tile, jax.ShapeDtypeStruct((3, 9, 128, 128), F32)),
        sym, own, flip, low, high, left, right, cotangent, bottom, inputs, both,
        scratch=[
            pltpu.VMEM((48, 96, 128), F32),
            pltpu.VMEM((4, 48, 80, 128), F32),
            pltpu.VMEM((48, 80, 384), BF),
            pltpu.VMEM((48, 64, 128), F32),
            pltpu.VMEM((32, 64, 128), BF),
            pltpu.VMEM((32, 64, 128), BF),
            pltpu.VMEM((3, 128, 2048), BF),
            pltpu.VMEM((3, 1152, 256), BF),
            pltpu.SemaphoreType.DMA((4,)),
        ],
        far=4,
        flops=8 * 10**9, moved=2 * 10**7, room=60,
    )
    return gradient, total(terms.reshape(-1, channels)).reshape(terms.shape)


def solution(mesh):
    fine = Mesh(mesh.devices.reshape(SIZES), NAMES)
    rows, cols = ("y", "xh", "core"), ("z", "xl")
    in_specs = (P(rows, cols, None), P(None, rows, cols, None), P(None, rows, cols, None), P())
    out_specs = (P(rows, cols, None), P())
    return jax.shard_map(per_device, mesh=fine, in_specs=in_specs, out_specs=out_specs, check_vma=False)
```

time: 159 us -> 148 us (0.931)
  waiting for transfers between devices: 7.2 us -> 21.3 us
  starting transfers between devices: 54.8 us -> 42.3 us
  local copies, waits for them, and re-layouts: 16.2 us -> 8.23 us
  Pallas kernels: 21.6 us -> 15.2 us
  other arithmetic: 9.9 us -> 14.5 us
  blocking collectives: 47.8 us -> 44 us
    ppermute x9, waiting for transfers between devices: 7.2 us -> 21.3 us  [shift(): return lax.ppermute(x, NAMES, pairs)]
    ppermute x9, starting transfers between devices: 54.8 us -> 42.3 us  [shift(): return lax.ppermute(x, NAMES, pairs)]
    pallas_call x3, Pallas kernels: 21.6 us -> 15.2 us  [call(): pl.pallas_call(body, out_shape=out_shape, in_specs=[pl.BlockSpec(memory_s...]
    all_to_all x1, blocking collectives: 32 us -> 28.2 us  [total(): terms = lax.all_to_all(part, CHIPS, 0, 0, tiled=True)]
    unnamed x22 -> x18, local copies, waits for them, and re-layouts: 4.19 us -> 1.16 us
    convert_element_type x1, other arithmetic: 0.19 us -> 2.18 us  [per_device(): bottom = (active_masks[0] > 0).astype(BF)]
  transfers between devices with their start and end apart: 9 -> 9, of which waited for: 4 -> 7; matrix products, arithmetic and copies ran while one was open for 8% -> 8% of each run, Pallas kernels for 3% -> 0%
where the time goes in v3:
time: 148 us; the launch traced here: 146 us
  blocking collectives  44 us (30%)
  starting transfers between devices  42.3 us (29%)
  waiting for transfers between devices  21.3 us (14%)
  Pallas kernels  15.2 us (10%)
  other arithmetic  14.5 us (10%)
  local copies, waits for them, and re-layouts  8.23 us (6%)
    ppermute x9, starting transfers between devices, shift(): return lax.ppermute(x, NAMES, pairs)  42.3 us
    all_to_all x1, blocking collectives, total(): terms = lax.all_to_all(part, CHIPS, 0, 0, tiled=True)  28.2 us
    ppermute x9, waiting for transfers between devices, shift(): return lax.ppermute(x, NAMES, pairs)  21.3 us
    all_to_all x1, blocking collectives, total(): whole = lax.all_to_all(copies, CHIPS, 0, 0, tiled=True).reshape(rows, 128)  15.8 us
    pallas_call x3, Pallas kernels, call(): pl.pallas_call(body, out_shape=out_shape, in_specs=[pl.BlockSpec(memory_s...  15.2 us
  transfers between devices with their start and end apart: 9, of which 7 were waited for; matrix products, arithmetic and copies ran while one was open for 8% of the time, Pallas kernels for 0%

profile of v3, /device:TPU:1, one launch (start us, length us, event | category | flops | bytes accessed | tf_op | source)
XLA Modules:
  0.0 146.4 jit_solution(5907119452596192633)
XLA Ops:
  0.6 2.0 %fusion.own_ref = bf16[2,32,64,128]{3,2,1,0:T(8,128)(2,1)S(1)} fusion(s32[3,32,64,128]{3,2,1,0:T(8,128)} %param.6), kind=kLoop, calls=%fused_computation.2 | loop fusion | flops 1048576 | bytes 3145728 | tf_op jit(solution)/shard_map/convert_element_type | solution.py:233
  2.7 1.5 %collective-permute-start = (bf16[3,32,32,128]{3,2,1,0:T(8,128)(2,1)S(1)}, bf16[3,32,32,128]{3,2,1,0:T(8,128)(2,1)S(1)}, u32[]{:S(2)}, u32[]{:S(2)}) collective-permute-start(bf16[3,32,32,128]{3,2,1,0:T(8,128)(2,1)S(1)} %fusion.3), channel_id=1, source_target_pairs={{0,8},{1,9},{2,10},{3,11},{4,12},{5,13},{6,14},{7,15},{8,0},{9,1},... | collective-permute-start | bytes 2359304 | tf_op jit(solution)/shard_map/ppermute | solution.py:55
  4.2 1.9 %collective-permute-done = bf16[3,32,32,128]{3,2,1,0:T(8,128)(2,1)S(1)} collective-permute-done((bf16[3,32,32,128]{3,2,1,0:T(8,128)(2,1)S(1)}, bf16[3,32,32,128]{3,2,1,0:T(8,128)(2,1)S(1)}, u32[]{:S(2)}, u32[]{:S(2)}) %collective-permute-start) | collective-permute-done | bytes 786464 | tf_op jit(solution)/shard_map/ppermute | solution.py:55
  6.5 1.3 pad_maximum_fusion.1
  7.8 13.3 %collective-permute-start.1 = (bf16[3,64,32,128]{3,2,1,0:T(8,128)(2,1)}, bf16[3,64,32,128]{3,2,1,0:T(8,128)(2,1)}, u32[]{:S(2)}, u32[]{:S(2)}) collective-permute-start(bf16[3,64,32,128]{3,2,1,0:T(8,128)(2,1)} %pad_maximum_fusion.1), channel_id=1, source_target_pairs={{0,0},{1,16},{2,32},{3,48},{4,38},{5,54},{6,96},{7,112},{8,8},{9,2... | collective-permute-start | bytes 4718600 | tf_op jit(solution)/shard_map/ppermute | solution.py:55
  21.1 1.6 %copy.11 = bf16[3,3,3,128,128]{3,4,1,2,0:T(8,128)(2,1)} copy(bf16[3,3,3,128,128]{4,3,2,1,0:T(8,128)(2,1)S(1)} %bitcast.34) | data formatting | bytes 1769472 | tf_op jit(solution)/shard_map/reshape | solution.py:240
  22.7 2.7 %compare_select_fusion = bf16[3,32,64,128]{3,2,1,0:T(8,128)(2,1)S(1)} fusion(bf16[3,32,64,128]{3,2,1,0:T(8,128)(2,1)} %param.5, s32[3,32,64,128]{3,2,1,0:T(8,128)} %param.6), kind=kLoop, calls=%fused_computation | loop fusion | flops 1572864 | bytes 6291456 | tf_op jit(solution)/shard_map/jit(_where)/select_n | solution.py:238
  25.5 1.6 %copy.10 = bf16[3,2048,128]{1,2,0:T(8,128)(2,1)} copy(bf16[3,2048,128]{2,1,0:T(8,128)(2,1)S(1)} %bitcast.28) | data formatting | bytes 3145728 | tf_op jit(solution)/shard_map/reshape | solution.py:239
  27.1 1.6 %reverse_bitcast_fusion.1 = (bf16[3,3,3,128,128]{4,3,1,2,0:T(8,128)(2,1)S(1)}, bf16[3,3,3,128,128]{4,3,2,1,0:T(8,128)(2,1)S(1)}) fusion(bf16[3,3,3,128,128]{3,4,1,2,0:T(8,128)(2,1)} %copy.11), kind=kLoop, calls=%fused_computation.22 | loop fusion | bytes 2654208 | tf_op jit(solution)/shard_map/transpose | solution.py:240
  28.7 2.2 %fusion.5.mask_hbm = bf16[32,64,128]{2,1,0:T(8,128)(2,1)} fusion(s32[3,32,64,128]{3,2,1,0:T(8,128)} %param.6), kind=kLoop, calls=%fused_computation.23 | loop fusion | flops 524288 | bytes 1572864 | tf_op jit(solution)/shard_map/convert_element_type | solution.py:237
  30.9 1.4 pad_maximum_fusion
  32.3 0.8 collective-permute-start.2
  33.1 1.6 %broadcast_select_fusion = bf16[3,64,32,128]{3,2,1,0:T(8,128)(2,1)S(1)} fusion(bf16[3,64,32,128]{3,2,1,0:T(8,128)(2,1)S(1)} %collective-permute-done.2, bf16[3,64,32,128]{3,2,1,0:T(8,128)(2,1)} %collective-permute-done.1, pred[]{:T(512)S(6)} %eq.6), kind=kLoop, calls=%fused_computation.10 | loop fusion | flops 786432 | bytes 4718593 | tf_op jit(solution)/shard_map/jit(_where)/select_n | solution.py:209
  34.7 0.6 copy.17
  35.6 19.1 %collective-permute-start.3 = (bf16[15,64,128]{2,1,0:T(8,128)(2,1)S(1)}, bf16[15,64,128]{2,1,0:T(8,128)(2,1)S(1)}, u32[]{:S(2)}, u32[]{:S(2)}) collective-permute-start(bf16[15,64,128]{2,1,0:T(8,128)(2,1)S(1)} %get-tuple-element.15), channel_id=1, source_target_pairs={{0,8},{1,9},{2,10},{3,11},{4,12},{5,13},{6,14},{7,15},{8,16},{9,17... | collective-permute-start | bytes 737288 | tf_op jit(solution)/shard_map/ppermute | solution.py:55
  54.7 1.9 %collective-permute-start.4 = (bf16[15,64,128]{2,1,0:T(8,128)(2,1)S(1)}, bf16[15,64,128]{2,1,0:T(8,128)(2,1)S(1)}, u32[]{:S(2)}, u32[]{:S(2)}) collective-permute-start(bf16[15,64,128]{2,1,0:T(8,128)(2,1)S(1)} %get-tuple-element.16), channel_id=1, source_target_pairs={{8,0},{9,1},{10,2},{11,3},{12,4},{13,5},{14,6},{15,7},{16,8},{17,9... | collective-permute-start | bytes 737288 | tf_op jit(solution)/shard_map/ppermute | solution.py:55
  56.7 1.2 collective-permute-done.3.low_ref
  57.9 5.9 %collective-permute-done.4.high_ref = bf16[15,64,128]{2,1,0:T(8,128)(2,1)S(1)} collective-permute-done((bf16[15,64,128]{2,1,0:T(8,128)(2,1)S(1)}, bf16[15,64,128]{2,1,0:T(8,128)(2,1)S(1)}, u32[]{:S(2)}, u32[]{:S(2)}) %collective-permute-start.4) | collective-permute-done | bytes 245792 | tf_op jit(solution)/shard_map/ppermute | solution.py:55
  64.4 1.3 collective-permute-start.5
  65.7 1.3 collective-permute-start.6
  67.0 1.3 collective-permute-done.5.left_ref
  68.3 7.8 %collective-permute-done.6.right_ref = bf16[48,16,128]{2,1,0:T(8,128)(2,1)S(1)} collective-permute-done((bf16[48,16,128]{2,1,0:T(8,128)(2,1)S(1)}, bf16[48,16,128]{2,1,0:T(8,128)(2,1)S(1)}, u32[]{:S(2)}, u32[]{:S(2)}) %collective-permute-start.6) | collective-permute-done | bytes 196640 | tf_op jit(solution)/shard_map/ppermute | solution.py:55
  76.1 0.7 copy-done.8
  76.8 14.8 %blocks.1 = (bf16[32,64,128]{2,1,0:T(8,128)(2,1)}, f32[3,9,128,128]{3,2,1,0:T(8,128)}) custom-call(bf16[32,64,128]{2,1,0:T(8,128)(2,1)} %copy-done.3, bf16[2,32,64,128]{3,2,1,0:T(8,128)(2,1)} %copy-done, bf16[3,32,64,128]{3,2,1,0:T(8,128)(2,1)} %bitcast.25, bf16[15,64,128]{2,1,0:T(8,128)(2,1)} %copy-done.4, bf16[15,64,128]{2,1,0:T(8,128)(2,1)} %copy-done.5, ...), custom_call_target="tpu_custom_call" | custom-call | flops 8000000000 | bytes 20000000 | tf_op jit(solution)/shard_map/blocks/pallas_call | solution.py:69
  91.5 1.2 fusion.6
  92.9 1.8 %collective-permute-done.7 = bf16[1728,128]{1,0:T(8,128)(2,1)S(1)} collective-permute-done((bf16[1728,128]{1,0:T(8,128)(2,1)S(1)}, bf16[1728,128]{1,0:T(8,128)(2,1)S(1)}, u32[]{:S(2)}, u32[]{:S(2)}) %collective-permute-start.7) | collective-permute-done | bytes 442400 | tf_op jit(solution)/shard_map/ppermute | solution.py:55
  94.6 1.3 fusion.2
  96.1 28.2 %all_to_all.10 = bf16[64,27,128]{2,1,0:T(8,128)(2,1)S(1)} all-to-all(bf16[64,27,128]{2,1,0:T(8,128)(2,1)S(1)} %reshape.32), channel_id=1, replica_groups=mesh['y'=4,'xh'=2,'core'=2,'z'=4,'xl'=2] {'y','xh','z','xl'}, dimensions={0} | all-to-all | bytes 884736 | tf_op jit(solution)/shard_map/all_to_all | solution.py:221
  124.5 15.8 %all_to_all.11 = bf16[64,27,128]{2,1,0:T(8,128)(2,1)S(1)} all-to-all(bf16[64,27,128]{2,1,0:T(8,128)(2,1)S(1)} %broadcast_in_dim.14), channel_id=1, replica_groups=mesh['y'=4,'xh'=2,'core'=2,'z'=4,'xl'=2] {'y','xh','z','xl'}, dimensions={0} | all-to-all | bytes 884736 | tf_op jit(solution)/shard_map/all_to_all | solution.py:224
  140.5 3.0 %collective-permute-start.8 = (bf16[1728,128]{1,0:T(8,128)(2,1)S(1)}, bf16[1728,128]{1,0:T(8,128)(2,1)S(1)}, u32[]{:S(2)}, u32[]{:S(2)}) collective-permute-start(bf16[1728,128]{1,0:T(8,128)(2,1)S(1)} %reshape.33), channel_id=1, source_target_pairs={{0,8},{1,9},{2,10},{3,11},{4,12},{5,13},{6,14},{7,15},{8,0},{9,1},... | collective-permute-start | bytes 1327112 | tf_op jit(solution)/shard_map/ppermute | solution.py:55
  143.5 1.4 collective-permute-done.8
  145.0 1.4 convert.3
  (30 shorter events, 2.1 us)
Async XLA Ops:
  0.6 2.0 %copy-start.2 = (bf16[32,64,128]{2,1,0:T(8,128)(2,1)S(1)}, bf16[32,64,128]{2,1,0:T(8,128)(2,1)}, u32[]{:S(2)}) copy-start(bf16[32,64,128]{2,1,0:T(8,128)(2,1)} %cotangent_hbm.1) | copy-start | bytes 1572868
  2.6 61.1 %copy-start = (bf16[2,32,64,128]{3,2,1,0:T(8,128)(2,1)}, bf16[2,32,64,128]{3,2,1,0:T(8,128)(2,1)S(1)}, u32[]{:S(2)}) copy-start(bf16[2,32,64,128]{3,2,1,0:T(8,128)(2,1)S(1)} %fusion.own_ref) | copy-start | bytes 3145732
  2.7 3.4 %collective-permute-start = (bf16[3,32,32,128]{3,2,1,0:T(8,128)(2,1)S(1)}, bf16[3,32,32,128]{3,2,1,0:T(8,128)(2,1)S(1)}, u32[]{:S(2)}, u32[]{:S(2)}) collective-permute-start(bf16[3,32,32,128]{3,2,1,0:T(8,128)(2,1)S(1)} %fusion.3), channel_id=1, source_target_pairs={{0,8},{1,9},{2,10},{3,11},{4,12},{5,13},{6,14},{7,15},{8,0},{9,1},... | collective-permute-start | bytes 2359304 | tf_op jit(solution)/shard_map/ppermute | solution.py:55
  6.5 14.6 %copy-start.6 = (bf16[3,9,128,128]{3,2,1,0:T(8,128)(2,1)S(1)}, bf16[3,9,128,128]{3,2,1,0:T(8,128)(2,1)}, u32[]{:S(2)}) copy-start(bf16[3,9,128,128]{3,2,1,0:T(8,128)(2,1)} %param.7) | copy-start | bytes 2654212
  7.8 24.5 %collective-permute-start.1 = (bf16[3,64,32,128]{3,2,1,0:T(8,128)(2,1)}, bf16[3,64,32,128]{3,2,1,0:T(8,128)(2,1)}, u32[]{:S(2)}, u32[]{:S(2)}) collective-permute-start(bf16[3,64,32,128]{3,2,1,0:T(8,128)(2,1)} %pad_maximum_fusion.1), channel_id=1, source_target_pairs={{0,0},{1,16},{2,32},{3,48},{4,38},{5,54},{6,96},{7,112},{8,8},{9,2... | collective-permute-start | bytes 4718600 | tf_op jit(solution)/shard_map/ppermute | solution.py:55
  32.3 0.8 collective-permute-start.2
  35.3 28.5 %copy-start.1 = (bf16[3,64,32,128]{3,1,2,0:T(8,128)(2,1)}, bf16[3,64,32,128]{3,1,2,0:T(8,128)(2,1)S(1)}, u32[]{:S(2)}) copy-start(bf16[3,64,32,128]{3,1,2,0:T(8,128)(2,1)S(1)} %copy.17) | copy-start | bytes 4718596
  35.6 28.4 %copy-start.3 = (bf16[32,64,128]{2,1,0:T(8,128)(2,1)}, bf16[32,64,128]{2,1,0:T(8,128)(2,1)S(1)}, u32[]{:S(2)}) copy-start(bf16[32,64,128]{2,1,0:T(8,128)(2,1)S(1)} %get-tuple-element.14.sym_ref) | copy-start | bytes 1572868
  35.6 22.2 %collective-permute-start.3 = (bf16[15,64,128]{2,1,0:T(8,128)(2,1)S(1)}, bf16[15,64,128]{2,1,0:T(8,128)(2,1)S(1)}, u32[]{:S(2)}, u32[]{:S(2)}) collective-permute-start(bf16[15,64,128]{2,1,0:T(8,128)(2,1)S(1)} %get-tuple-element.15), channel_id=1, source_target_pairs={{0,8},{1,9},{2,10},{3,11},{4,12},{5,13},{6,14},{7,15},{8,16},{9,17... | collective-permute-start | bytes 737288 | tf_op jit(solution)/shard_map/ppermute | solution.py:55
  54.7 9.0 %collective-permute-start.4 = (bf16[15,64,128]{2,1,0:T(8,128)(2,1)S(1)}, bf16[15,64,128]{2,1,0:T(8,128)(2,1)S(1)}, u32[]{:S(2)}, u32[]{:S(2)}) collective-permute-start(bf16[15,64,128]{2,1,0:T(8,128)(2,1)S(1)} %get-tuple-element.16), channel_id=1, source_target_pairs={{8,0},{9,1},{10,2},{11,3},{12,4},{13,5},{14,6},{15,7},{16,8},{17,9... | collective-permute-start | bytes 737288 | tf_op jit(solution)/shard_map/ppermute | solution.py:55
  57.9 6.1 %copy-start.4 = (bf16[15,64,128]{2,1,0:T(8,128)(2,1)}, bf16[15,64,128]{2,1,0:T(8,128)(2,1)S(1)}, u32[]{:S(2)}) copy-start(bf16[15,64,128]{2,1,0:T(8,128)(2,1)S(1)} %collective-permute-done.3.low_ref) | copy-start | bytes 737284
  63.8 0.7 copy-start.5
  64.4 3.9 %collective-permute-start.5 = (bf16[48,16,128]{2,1,0:T(8,128)(2,1)S(1)}, bf16[48,16,128]{2,1,0:T(8,128)(2,1)S(1)}, u32[]{:S(2)}, u32[]{:S(2)}) collective-permute-start(bf16[48,16,128]{2,1,0:T(8,128)(2,1)S(1)} %get-tuple-element.17), channel_id=1, source_target_pairs={{0,1},{1,2},{2,3},{3,4},{4,5},{5,6},{6,7},{8,9},{9,10},{10,11},{11... | collective-permute-start | bytes 589832 | tf_op jit(solution)/shard_map/ppermute | solution.py:55
  65.7 10.4 %collective-permute-start.6 = (bf16[48,16,128]{2,1,0:T(8,128)(2,1)S(1)}, bf16[48,16,128]{2,1,0:T(8,128)(2,1)S(1)}, u32[]{:S(2)}, u32[]{:S(2)}) collective-permute-start(bf16[48,16,128]{2,1,0:T(8,128)(2,1)S(1)} %get-tuple-element.18), channel_id=1, source_target_pairs={{1,0},{2,1},{3,2},{4,3},{5,4},{6,5},{7,6},{9,8},{10,9},{11,10},{12... | collective-permute-start | bytes 589832 | tf_op jit(solution)/shard_map/ppermute | solution.py:55
  68.3 7.8 %copy-start.7 = (bf16[48,16,128]{2,1,0:T(8,128)(2,1)}, bf16[48,16,128]{2,1,0:T(8,128)(2,1)S(1)}, u32[]{:S(2)}) copy-start(bf16[48,16,128]{2,1,0:T(8,128)(2,1)S(1)} %collective-permute-done.5.left_ref) | copy-start | bytes 589828
  76.1 0.7 copy-start.8
  92.8 1.9 %collective-permute-start.7 = (bf16[1728,128]{1,0:T(8,128)(2,1)S(1)}, bf16[1728,128]{1,0:T(8,128)(2,1)S(1)}, u32[]{:S(2)}, u32[]{:S(2)}) collective-permute-start(bf16[1728,128]{1,0:T(8,128)(2,1)S(1)} %fusion.6), channel_id=1, source_target_pairs={{0,8},{1,9},{2,10},{3,11},{4,12},{5,13},{6,14},{7,15},{8,0},{9,1},... | collective-permute-start | bytes 1327112 | tf_op jit(solution)/shard_map/ppermute | solution.py:55
  140.5 4.4 %collective-permute-start.8 = (bf16[1728,128]{1,0:T(8,128)(2,1)S(1)}, bf16[1728,128]{1,0:T(8,128)(2,1)S(1)}, u32[]{:S(2)}, u32[]{:S(2)}) collective-permute-start(bf16[1728,128]{1,0:T(8,128)(2,1)S(1)} %reshape.33), channel_id=1, source_target_pairs={{0,8},{1,9},{2,10},{3,11},{4,12},{5,13},{6,14},{7,15},{8,0},{9,1},... | collective-permute-start | bytes 1327112 | tf_op jit(solution)/shard_map/ppermute | solution.py:55

commit v4 on v3

--- a/solution.py
+++ b/solution.py
@@ -69,7 +69,10 @@
     return pl.pallas_call(
         body,
         out_shape=out_shape,
-        in_specs=[pl.BlockSpec(memory_space=pltpu.VMEM)] * (len(args) - far) + [pl.BlockSpec(memory_space=pltpu.HBM)] * far,
+        in_specs=[
+            pl.BlockSpec(memory_space=pltpu.SMEM if a.ndim == 1 else pltpu.VMEM if n < len(args) - far else pltpu.HBM)
+            for n, a in enumerate(args)
+        ],
         scratch_shapes=list(scratch),
         compiler_params=pltpu.CompilerParams(vmem_limit_bytes=room * 2**20),
         cost_estimate=pl.CostEstimate(flops=flops, bytes_accessed=moved, transcendentals=0),
@@ -107,7 +110,7 @@
 
 def blocks_kernel(
     sym_ref, own_ref, flip_ref, low_ref, high_ref, left_ref, right_ref,
-    cotangent_hbm, mask_hbm, inputs_hbm, weights_hbm, gradient_ref, terms_ref,
+    core_ref, cotangent_hbm, mask_hbm, inputs_hbm, weights_hbm, gradient_ref, keep_ref, send_ref,
     sym, masks, patches, change, cotangent_ref, mask_ref, inputs_ref, weights_ref, arrived,
 ):
     copies = []
@@ -124,16 +127,16 @@
     before, after = left_ref[...].astype(F32), right_ref[...].astype(F32)
     sym[:, 80:88] = before[:, :8]
     sym[:, 72:80] = after[:, :8]
-    masks[:, 4:8] = jnp.zeros((4, 4, 80, 128), F32)
-    masks[:, 40:44] = jnp.zeros((4, 4, 80, 128), F32)
+    masks[:, 4:8] = jnp.zeros((4, 4, 80, 128), BF)
+    masks[:, 40:44] = jnp.zeros((4, 4, 80, 128), BF)
     tiles = (own_ref.at[0], own_ref.at[1], flip_ref.at[1], flip_ref.at[2])
     for k, (lows, highs) in enumerate(((7, 0), (4, 7), (3, 4), (0, 3))):
         w, at = WIDTHS[k + 1], STARTS[k + 1]
-        masks[k, 8:40, 0:64] = tiles[k][...].astype(F32)
-        masks[k, 8 - w : 8, 0:64] = low_ref[at : at + w].astype(F32)
-        masks[k, 40 : 40 + w, 0:64] = high_ref[at : at + w].astype(F32)
-        masks[k, :, 72:80] = roll8(before[:, 8:], lows)
-        masks[k, :, 64:72] = roll8(after[:, 8:], highs)
+        masks[k, 8:40, 0:64] = tiles[k][...]
+        masks[k, 8 - w : 8, 0:64] = low_ref[at : at + w]
+        masks[k, 40 : 40 + w, 0:64] = high_ref[at : at + w]
+        rim = jnp.concatenate([roll8(after[:, 8:], highs), roll8(before[:, 8:], lows)], axis=1)
+        masks[k, :, 64:80] = rim.astype(BF)
 
     for layer in (2, 1, 0):
         for copy in {2: copies[:2], 1: (), 0: copies[2:]}[layer]:
@@ -148,7 +151,7 @@
                 patches[f, :, v * 128 : (v + 1) * 128] = sym[f, 8 + d * (v - 1) : 88 + d * (v - 1)].astype(BF)
             return carry
 
-        lax.fori_loop(first - d, first + count + d, gather, 0, unroll=2)
+        lax.fori_loop(first - d, first + count + d, gather, 0, unroll=True)
         total = None
         for r in (8, 24):
             right = jnp.concatenate(
@@ -156,8 +159,13 @@
             )
             term = jnp.dot(inputs_ref[layer, :, (r - 8) * 64 : (r + 8) * 64], right, preferred_element_type=F32)
             total = term if total is None else total + term
+        total = total * (1.0 / 512.0)
+        lower = core_ref[0] == 0
+        kept = jnp.where(lower, total[:64], total[64:])
+        sent = jnp.where(lower, total[64:], total[:64]).astype(BF)
         for t in range(9):
-            terms_ref[layer, 8 - t] = total[:, t * 128 : (t + 1) * 128] * (1.0 / 512.0)
+            keep_ref[layer, 8 - t] = kept[:, t * 128 : (t + 1) * 128]
+            send_ref[layer, 8 - t] = sent[:, t * 128 : (t + 1) * 128]
         if layer:
             def step(i, carry):
                 f = first + size * i
@@ -166,8 +174,8 @@
                     [patches[pl.ds(f + d * (u - 1), size)].reshape(size * 80, 384) for u in range(3)], axis=1
                 )
                 out = jnp.dot(rows, weights_ref[layer], preferred_element_type=F32)
-                ahead = masks[layer - 1, here] * out[:, :128].reshape(size, 80, 128)
-                back = masks[layer + 1, here] * out[:, 128:].reshape(size, 80, 128)
+                ahead = masks[layer - 1, here].astype(F32) * out[:, :128].reshape(size, 80, 128)
+                back = masks[layer + 1, here].astype(F32) * out[:, 128:].reshape(size, 80, 128)
                 sym[here, 8:88] = sym[here, 8:88] + 0.5 * (ahead + back)
                 if layer == 2:
                     change[here] = ahead[:, :64]
@@ -210,22 +218,22 @@
     return jnp.swapaxes(arrived, -3, -2)
 
 
-def total(x):
-    core = lax.axis_index("core")
-    rows = x.shape[0] // 2
-    x = x.reshape(2, rows, 128)
-    keep = lax.dynamic_index_in_dim(x, core, 0, False)
-    send = lax.dynamic_index_in_dim(x, 1 - core, 0, False).astype(BF)
-    swap = core_swap()
-    part = (keep + shift(send, swap).astype(F32)).astype(BF).reshape(64, rows // 64, 128)
+def finish_kernel(core_ref, whole_ref, other_ref, out_ref):
+    lower = core_ref[0] == 0
+    whole, other = whole_ref[...].astype(F32), other_ref[...].astype(F32)
+    out_ref[:, :64] = jnp.where(lower, whole, other)
+    out_ref[:, 64:] = jnp.where(lower, other, whole)
+
+
+def total(keep, send, core):
+    part = (keep + shift(send, core_swap()).astype(F32)).astype(BF).reshape(64, -1, 128)
     terms = lax.all_to_all(part, CHIPS, 0, 0, tiled=True)
     mine = jnp.sum(terms.astype(F32), axis=0).astype(BF)
     copies = jnp.broadcast_to(mine[None], terms.shape)
-    whole = lax.all_to_all(copies, CHIPS, 0, 0, tiled=True).reshape(rows, 128)
-    other = shift(whole, swap)
-    low = jnp.where(core == 0, whole, other)
-    high = jnp.where(core == 0, other, whole)
-    return jnp.concatenate([low, high], axis=0).astype(F32)
+    whole = lax.all_to_all(copies, CHIPS, 0, 0, tiled=True).reshape(keep.shape)
+    other = shift(whole, core_swap())
+    out = jax.ShapeDtypeStruct((keep.shape[0], 128, 128), F32)
+    return call(finish_kernel, "finish", out, core, whole, other)
 
 
 def per_device(cotangent, activations, active_masks, weights):
@@ -233,15 +241,19 @@
     own = (active_masks[1:] > 0).astype(BF)
     piece = paired(jnp.concatenate([cotangent[None], own], axis=0))
     first, second = mirror_steps()
-    direct = shift(piece, first)
+    cut = piece.shape[1] // 2
+    direct = shift(piece[:, :cut], first)
+    direct2 = shift(piece[:, cut:], first)
     bottom = (active_masks[0] > 0).astype(BF)
     inputs = jnp.where(active_masks > 0, activations, jnp.zeros_like(activations))
     inputs = inputs.reshape(3, -1, channels).swapaxes(1, 2)
     kernels = weights.reshape(3, 3, 3, channels, channels)[:, ::-1, ::-1].swapaxes(3, 4)
     both = jnp.concatenate([kernels, kernels.swapaxes(1, 2)], axis=-1).reshape(3, -1, 2 * channels)
-    direct, bottom, inputs, both = lax.optimization_barrier((direct, bottom, inputs, both))
-
-    flip = turn(direct, shift(direct, second))
+    direct2, bottom, inputs, both = lax.optimization_barrier((direct2, bottom, inputs, both))
+
+    relayed = shift(direct, second)
+    relayed2 = shift(direct2, second)
+    flip = jnp.concatenate([turn(direct, relayed), turn(direct2, relayed2)], axis=2)
     tile = jax.ShapeDtypeStruct((32, 64, 128), BF)
     strip = jax.ShapeDtypeStruct((15, 64, 128), BF)
     sym, down, up = call(symmetric_kernel, "symmetric", (tile, strip, strip), cotangent, flip, own)
@@ -251,12 +263,13 @@
         pack_kernel, "pack", (edge, edge), sym, own, flip, low, high, scratch=[pltpu.VMEM((2, 5, 48, 8, 128), F32)]
     )
     left, right = shift(ends, neighbour(0, 1)), shift(starts, neighbour(0, -1))
-    gradient, terms = call(
-        blocks_kernel, "blocks", (tile, jax.ShapeDtypeStruct((3, 9, 128, 128), F32)),
-        sym, own, flip, low, high, left, right, cotangent, bottom, inputs, both,
+    core = lax.axis_index("core").astype(jnp.int32).reshape(1)
+    halves = [jax.ShapeDtypeStruct((3, 9, 64, 128), kind) for kind in (F32, BF)]
+    gradient, keep, send = call(
+        blocks_kernel, "blocks", (tile, *halves), sym, own, flip, low, high, left, right, core, cotangent, bottom, inputs, both,
         scratch=[
             pltpu.VMEM((48, 96, 128), F32),
-            pltpu.VMEM((4, 48, 80, 128), F32),
+            pltpu.VMEM((4, 48, 80, 128), BF),
             pltpu.VMEM((48, 80, 384), BF),
             pltpu.VMEM((48, 64, 128), F32),
             pltpu.VMEM((32, 64, 128), BF),
@@ -268,7 +281,8 @@
         far=4,
         flops=8 * 10**9, moved=2 * 10**7, room=60,
     )
-    return gradient, total(terms.reshape(-1, channels)).reshape(terms.shape)
+    sums = total(keep.reshape(27, 64, 128), send.reshape(27, 64, 128), core)
+    return gradient, sums.reshape(3, 9, 128, 128)
 
 
 def solution(mesh):

time: 148 us -> 144 us (0.973)
  blocking collectives: 44 us -> 40.4 us
    all_to_all x1, blocking collectives: 28.2 us -> 24.6 us  [total(): terms = lax.all_to_all(part, CHIPS, 0, 0, tiled=True)]
    pallas_call x3 -> x4, Pallas kernels: 15.2 us -> 16 us  [call(): pl.pallas_call(body, out_shape=out_shape, in_specs=[pl.BlockSpec(memory_s...]
    ppermute x9 -> x11, starting transfers between devices: 42.3 us -> 42.7 us  [shift(): return lax.ppermute(x, NAMES, pairs)]
    ppermute x9 -> x11, waiting for transfers between devices: 21.3 us -> 21.5 us  [shift(): return lax.ppermute(x, NAMES, pairs)]
  transfers between devices with their start and end apart: 9 -> 11, of which waited for: 7 -> 7; matrix products, arithmetic and copies ran while one was open for 8% -> 9% of each run, Pallas kernels for 0% -> 0%
where the time goes in v4:
time: 144 us; the launch traced here: 142 us
  starting transfers between devices  42.7 us (30%)
  blocking collectives  40.4 us (28%)
  waiting for transfers between devices  21.5 us (15%)
  Pallas kernels  16 us (11%)
  other arithmetic  13.1 us (9%)
  local copies, waits for them, and re-layouts  7.62 us (5%)
    ppermute x11, starting transfers between devices, shift(): return lax.ppermute(x, NAMES, pairs)  42.7 us
    all_to_all x1, blocking collectives, total(): terms = lax.all_to_all(part, CHIPS, 0, 0, tiled=True)  24.6 us
    ppermute x11, waiting for transfers between devices, shift(): return lax.ppermute(x, NAMES, pairs)  21.5 us
    pallas_call x4, Pallas kernels, call(): pl.pallas_call(body, out_shape=out_shape, in_specs=[pl.BlockSpec(memory_s...  16 us
    all_to_all x1, blocking collectives, total(): whole = lax.all_to_all(copies, CHIPS, 0, 0, tiled=True).reshape(keep.shape)  15.8 us
  transfers between devices with their start and end apart: 11, of which 7 were waited for; matrix products, arithmetic and copies ran while one was open for 9% of the time, Pallas kernels for 0%

profile of v4, /device:TPU:1, one launch (start us, length us, event | category | flops | bytes accessed | tf_op | source)
XLA Modules:
  0.0 142.1 jit_solution(2293353550703263911)
XLA Ops:
  0.6 2.0 %fusion.own_ref = bf16[2,32,64,128]{3,2,1,0:T(8,128)(2,1)S(1)} fusion(s32[3,32,64,128]{3,2,1,0:T(8,128)} %param.6), kind=kLoop, calls=%fused_computation.2 | loop fusion | flops 1048576 | bytes 3145728 | tf_op jit(solution)/shard_map/convert_element_type | solution.py:241
  2.7 1.5 %collective-permute-start = (bf16[3,32,32,128]{3,2,1,0:T(8,128)(2,1)S(1)}, bf16[3,32,32,128]{3,2,1,0:T(8,128)(2,1)S(1)}, u32[]{:S(2)}, u32[]{:S(2)}) collective-permute-start(bf16[3,32,32,128]{3,2,1,0:T(8,128)(2,1)S(1)} %fusion.3), channel_id=1, source_target_pairs={{0,8},{1,9},{2,10},{3,11},{4,12},{5,13},{6,14},{7,15},{8,0},{9,1},... | collective-permute-start | bytes 2359304 | tf_op jit(solution)/shard_map/ppermute | solution.py:55
  4.2 1.9 %collective-permute-done = bf16[3,32,32,128]{3,2,1,0:T(8,128)(2,1)S(1)} collective-permute-done((bf16[3,32,32,128]{3,2,1,0:T(8,128)(2,1)S(1)}, bf16[3,32,32,128]{3,2,1,0:T(8,128)(2,1)S(1)}, u32[]{:S(2)}, u32[]{:S(2)}) %collective-permute-start) | collective-permute-done | bytes 786464 | tf_op jit(solution)/shard_map/ppermute | solution.py:55
  6.1 1.5 %broadcast_select_fusion.1 = (bf16[3,32,32,128]{3,2,1,0:T(8,128)(2,1)}, bf16[3,32,32,128]{3,2,1,0:T(8,128)(2,1)}) fusion(bf16[3,32,32,128]{3,2,1,0:T(8,128)(2,1)S(1)} %collective-permute-done, pred[]{:T(512)S(6)} %eq.12, s32[]{:T(128)S(6)} %select_n.44, bf16[2,32,64,128]{3,2,1,0:T(8,128)(2,1)S(1)} %fusion.own_ref, bf16[1,32,64,128]{3,2,1,0:T(8,128)(2,1)S(1)} %bitcast.25), kind=kLoop, calls=%fused_computation.18 | loop fusion | flops 3932160 | bytes 3932165 | tf_op jit(solution)/shard_map/jit(_where)/select_n | solution.py:210
  7.7 7.4 %collective-permute-start.1 = (bf16[3,32,32,128]{3,2,1,0:T(8,128)(2,1)}, bf16[3,32,32,128]{3,2,1,0:T(8,128)(2,1)}, u32[]{:S(2)}, u32[]{:S(2)}) collective-permute-start(bf16[3,32,32,128]{3,2,1,0:T(8,128)(2,1)} %get-tuple-element.26), channel_id=1, source_target_pairs={{0,0},{1,16},{2,32},{3,48},{4,38},{5,54},{6,96},{7,112},{8,8},{9,2... | collective-permute-start | bytes 2359304 | tf_op jit(solution)/shard_map/ppermute | solution.py:55
  15.1 7.4 %collective-permute-start.3 = (bf16[3,32,32,128]{3,2,1,0:T(8,128)(2,1)}, bf16[3,32,32,128]{3,2,1,0:T(8,128)(2,1)}, u32[]{:S(2)}, u32[]{:S(2)}) collective-permute-start(bf16[3,32,32,128]{3,2,1,0:T(8,128)(2,1)} %get-tuple-element.27), channel_id=1, source_target_pairs={{0,0},{1,16},{2,32},{3,48},{4,38},{5,54},{6,96},{7,112},{8,8},{9,2... | collective-permute-start | bytes 2359304 | tf_op jit(solution)/shard_map/ppermute | solution.py:55
  22.5 1.8 %compare_select_fusion = bf16[3,32,64,128]{3,2,1,0:T(8,128)(2,1)S(1)} fusion(bf16[3,32,64,128]{3,2,1,0:T(8,128)(2,1)} %param.5, s32[3,32,64,128]{3,2,1,0:T(8,128)S(1)} %copy-done.6), kind=kLoop, calls=%fused_computation | loop fusion | flops 1572864 | bytes 6291456 | tf_op jit(solution)/shard_map/jit(_where)/select_n | solution.py:248
  24.3 2.3 %copy.13 = bf16[3,3,3,128,128]{3,4,1,2,0:T(8,128)(2,1)} copy(bf16[3,3,3,128,128]{4,3,2,1,0:T(8,128)(2,1)} %bitcast.32) | data formatting | bytes 1769472 | tf_op jit(solution)/shard_map/reshape | solution.py:250
  26.6 1.6 %copy.12 = bf16[3,2048,128]{1,2,0:T(8,128)(2,1)} copy(bf16[3,2048,128]{2,1,0:T(8,128)(2,1)S(1)} %bitcast.26) | data formatting | bytes 3145728 | tf_op jit(solution)/shard_map/reshape | solution.py:249
  28.2 1.6 %reverse_bitcast_fusion.1 = (bf16[3,3,3,128,128]{4,3,1,2,0:T(8,128)(2,1)S(1)}, bf16[3,3,3,128,128]{4,3,2,1,0:T(8,128)(2,1)S(1)}) fusion(bf16[3,3,3,128,128]{3,4,1,2,0:T(8,128)(2,1)} %copy.13), kind=kLoop, calls=%fused_computation.22 | loop fusion | bytes 2654208 | tf_op jit(solution)/shard_map/transpose | solution.py:250
  29.7 2.2 %fusion.5.mask_hbm = bf16[32,64,128]{2,1,0:T(8,128)(2,1)} fusion(s32[3,32,64,128]{3,2,1,0:T(8,128)} %param.6), kind=kLoop, calls=%fused_computation.23 | loop fusion | flops 524288 | bytes 1572864 | tf_op jit(solution)/shard_map/convert_element_type | solution.py:247
  31.9 0.7 collective-permute-start.2
  32.6 1.4 %pad_maximum_fusion = bf16[3,3,3,128,256]{4,3,2,1,0:T(8,128)(2,1)} fusion(bf16[3,3,3,128,128]{4,3,2,1,0:T(8,128)(2,1)S(1)} %get-tuple-element.29, bf16[3,3,3,128,128]{4,3,1,2,0:T(8,128)(2,1)S(1)} %get-tuple-element.28), kind=kLoop, calls=%fused_computation.5 | loop fusion | flops 3538944 | bytes 3538944 | tf_op jit(solution)/shard_map/concatenate | solution.py:251
  34.1 0.7 collective-permute-start.4
  34.8 1.2 broadcast_select_fusion.3
  36.4 1.2 broadcast_select_fusion.2
  38.4 17.2 %collective-permute-start.5 = (bf16[15,64,128]{2,1,0:T(8,128)(2,1)S(1)}, bf16[15,64,128]{2,1,0:T(8,128)(2,1)S(1)}, u32[]{:S(2)}, u32[]{:S(2)}) collective-permute-start(bf16[15,64,128]{2,1,0:T(8,128)(2,1)S(1)} %get-tuple-element.16), channel_id=1, source_target_pairs={{0,8},{1,9},{2,10},{3,11},{4,12},{5,13},{6,14},{7,15},{8,16},{9,17... | collective-permute-start | bytes 737288 | tf_op jit(solution)/shard_map/ppermute | solution.py:55
  55.7 1.9 %collective-permute-start.6 = (bf16[15,64,128]{2,1,0:T(8,128)(2,1)S(1)}, bf16[15,64,128]{2,1,0:T(8,128)(2,1)S(1)}, u32[]{:S(2)}, u32[]{:S(2)}) collective-permute-start(bf16[15,64,128]{2,1,0:T(8,128)(2,1)S(1)} %get-tuple-element.17), channel_id=1, source_target_pairs={{8,0},{9,1},{10,2},{11,3},{12,4},{13,5},{14,6},{15,7},{16,8},{17,9... | collective-permute-start | bytes 737288 | tf_op jit(solution)/shard_map/ppermute | solution.py:55
  57.6 1.2 collective-permute-done.5.low_ref
  58.8 5.9 %collective-permute-done.6.high_ref = bf16[15,64,128]{2,1,0:T(8,128)(2,1)S(1)} collective-permute-done((bf16[15,64,128]{2,1,0:T(8,128)(2,1)S(1)}, bf16[15,64,128]{2,1,0:T(8,128)(2,1)S(1)}, u32[]{:S(2)}, u32[]{:S(2)}) %collective-permute-start.6) | collective-permute-done | bytes 245792 | tf_op jit(solution)/shard_map/ppermute | solution.py:55
  65.4 1.3 collective-permute-start.7
  66.7 1.3 collective-permute-start.8
  68.0 1.3 collective-permute-done.7.left_ref
  69.3 7.8 %collective-permute-done.8.right_ref = bf16[48,16,128]{2,1,0:T(8,128)(2,1)S(1)} collective-permute-done((bf16[48,16,128]{2,1,0:T(8,128)(2,1)S(1)}, bf16[48,16,128]{2,1,0:T(8,128)(2,1)S(1)}, u32[]{:S(2)}, u32[]{:S(2)}) %collective-permute-start.8) | collective-permute-done | bytes 196640 | tf_op jit(solution)/shard_map/ppermute | solution.py:55
  77.7 14.1 %blocks.1 = (bf16[32,64,128]{2,1,0:T(8,128)(2,1)}, f32[3,9,64,128]{3,2,1,0:T(8,128)}, bf16[3,9,64,128]{3,2,1,0:T(8,128)(2,1)}) custom-call(bf16[32,64,128]{2,1,0:T(8,128)(2,1)} %copy-done.3, bf16[2,32,64,128]{3,2,1,0:T(8,128)(2,1)} %copy-done, bf16[3,32,64,128]{3,2,1,0:T(8,128)(2,1)} %copy-done.1, bf16[15,64,128]{2,1,0:T(8,128)(2,1)} %copy-done.4, ...), custom_call_target="tpu_custom_call" | custom-call | flops 8000000000 | bytes 20000000 | tf_op jit(solution)/shard_map/blocks/pallas_call | solution.py:69
  92.1 2.0 %collective-permute-done.9 = bf16[27,64,128]{2,1,0:T(8,128)(2,1)S(1)} collective-permute-done((bf16[27,64,128]{2,1,0:T(8,128)(2,1)}, bf16[27,64,128]{2,1,0:T(8,128)(2,1)S(1)}, u32[]{:S(2)}, u32[]{:S(2)}) %collective-permute-start.9) | collective-permute-done | bytes 442400 | tf_op jit(solution)/shard_map/ppermute | solution.py:55
  94.1 1.3 fusion.2
  95.6 24.6 %all_to_all.10 = bf16[64,27,128]{2,1,0:T(8,128)(2,1)S(1)} all-to-all(bf16[64,27,128]{2,1,0:T(8,128)(2,1)S(1)} %reshape.42), channel_id=1, replica_groups=mesh['y'=4,'xh'=2,'core'=2,'z'=4,'xl'=2] {'y','xh','z','xl'}, dimensions={0} | all-to-all | bytes 884736 | tf_op jit(solution)/shard_map/all_to_all | solution.py:230
  120.3 15.8 %all_to_all.11 = bf16[64,27,128]{2,1,0:T(8,128)(2,1)S(1)} all-to-all(bf16[64,27,128]{2,1,0:T(8,128)(2,1)S(1)} %broadcast_in_dim.14), channel_id=1, replica_groups=mesh['y'=4,'xh'=2,'core'=2,'z'=4,'xl'=2] {'y','xh','z','xl'}, dimensions={0} | all-to-all | bytes 884736 | tf_op jit(solution)/shard_map/all_to_all | solution.py:233
  136.3 3.0 %collective-permute-start.10 = (bf16[27,64,128]{2,1,0:T(8,128)(2,1)S(1)}, bf16[27,64,128]{2,1,0:T(8,128)(2,1)S(1)}, u32[]{:S(2)}, u32[]{:S(2)}) collective-permute-start(bf16[27,64,128]{2,1,0:T(8,128)(2,1)S(1)} %reshape.43.whole_ref), channel_id=1, source_target_pairs={{0,8},{1,9},{2,10},{3,11},{4,12},{5,13},{6,14},{7,15},{8,0},{9,1},... | collective-permute-start | bytes 1327112 | tf_op jit(solution)/shard_map/ppermute | solution.py:55
  139.3 1.4 collective-permute-done.10.other_ref
  140.7 1.4 %finish.1 = f32[27,128,128]{2,1,0:T(8,128)} custom-call(s32[1]{0:T(128)} %bitcast.10.core_ref, bf16[27,64,128]{2,1,0:T(8,128)(2,1)S(1)} %reshape.43.whole_ref, bf16[27,64,128]{2,1,0:T(8,128)(2,1)S(1)} %collective-permute-done.10.other_ref), custom_call_target="tpu_custom_call" | custom-call | flops 1000000 | bytes 1000000 | tf_op jit(solution)/shard_map/finish/pallas_call | solution.py:69
  (33 shorter events, 3.4 us)
Async XLA Ops:
  0.6 2.0 %copy-start.2 = (bf16[32,64,128]{2,1,0:T(8,128)(2,1)S(1)}, bf16[32,64,128]{2,1,0:T(8,128)(2,1)}, u32[]{:S(2)}) copy-start(bf16[32,64,128]{2,1,0:T(8,128)(2,1)} %cotangent_hbm.1) | copy-start | bytes 1572868
  2.6 62.1 %copy-start = (bf16[2,32,64,128]{3,2,1,0:T(8,128)(2,1)}, bf16[2,32,64,128]{3,2,1,0:T(8,128)(2,1)S(1)}, u32[]{:S(2)}) copy-start(bf16[2,32,64,128]{3,2,1,0:T(8,128)(2,1)S(1)} %fusion.own_ref) | copy-start | bytes 3145732
  2.7 3.4 %collective-permute-start = (bf16[3,32,32,128]{3,2,1,0:T(8,128)(2,1)S(1)}, bf16[3,32,32,128]{3,2,1,0:T(8,128)(2,1)S(1)}, u32[]{:S(2)}, u32[]{:S(2)}) collective-permute-start(bf16[3,32,32,128]{3,2,1,0:T(8,128)(2,1)S(1)} %fusion.3), channel_id=1, source_target_pairs={{0,8},{1,9},{2,10},{3,11},{4,12},{5,13},{6,14},{7,15},{8,0},{9,1},... | collective-permute-start | bytes 2359304 | tf_op jit(solution)/shard_map/ppermute | solution.py:55
  4.2 18.2 %copy-start.6 = (s32[3,32,64,128]{3,2,1,0:T(8,128)S(1)}, s32[3,32,64,128]{3,2,1,0:T(8,128)}, u32[]{:S(2)}) copy-start(s32[3,32,64,128]{3,2,1,0:T(8,128)} %param.6) | copy-start | bytes 9437188
  7.7 24.2 %collective-permute-start.1 = (bf16[3,32,32,128]{3,2,1,0:T(8,128)(2,1)}, bf16[3,32,32,128]{3,2,1,0:T(8,128)(2,1)}, u32[]{:S(2)}, u32[]{:S(2)}) collective-permute-start(bf16[3,32,32,128]{3,2,1,0:T(8,128)(2,1)} %get-tuple-element.26), channel_id=1, source_target_pairs={{0,0},{1,16},{2,32},{3,48},{4,38},{5,54},{6,96},{7,112},{8,8},{9,2... | collective-permute-start | bytes 2359304 | tf_op jit(solution)/shard_map/ppermute | solution.py:55
  15.1 19.0 %collective-permute-start.3 = (bf16[3,32,32,128]{3,2,1,0:T(8,128)(2,1)}, bf16[3,32,32,128]{3,2,1,0:T(8,128)(2,1)}, u32[]{:S(2)}, u32[]{:S(2)}) collective-permute-start(bf16[3,32,32,128]{3,2,1,0:T(8,128)(2,1)} %get-tuple-element.27), channel_id=1, source_target_pairs={{0,0},{1,16},{2,32},{3,48},{4,38},{5,54},{6,96},{7,112},{8,8},{9,2... | collective-permute-start | bytes 2359304 | tf_op jit(solution)/shard_map/ppermute | solution.py:55
  31.9 2.9 %collective-permute-start.2 = (bf16[3,32,32,128]{3,2,1,0:T(8,128)(2,1)}, bf16[3,32,32,128]{3,2,1,0:T(8,128)(2,1)S(1)}, u32[]{:S(2)}, u32[]{:S(2)}) collective-permute-start(bf16[3,32,32,128]{3,2,1,0:T(8,128)(2,1)} %collective-permute-done.1), channel_id=1, source_target_pairs={{38,64},{54,80},{106,72},{107,88},{39,65},{55,81},{122,73},{123,89... | collective-permute-start | bytes 2359304 | tf_op jit(solution)/shard_map/ppermute | solution.py:55
  34.1 2.3 %collective-permute-start.4 = (bf16[3,32,32,128]{3,2,1,0:T(8,128)(2,1)}, bf16[3,32,32,128]{3,2,1,0:T(8,128)(2,1)S(1)}, u32[]{:S(2)}, u32[]{:S(2)}) collective-permute-start(bf16[3,32,32,128]{3,2,1,0:T(8,128)(2,1)} %collective-permute-done.3), channel_id=1, source_target_pairs={{38,64},{54,80},{106,72},{107,88},{39,65},{55,81},{122,73},{123,89... | collective-permute-start | bytes 2359304 | tf_op jit(solution)/shard_map/ppermute | solution.py:55
  38.1 26.6 %copy-start.1 = (bf16[3,32,64,128]{3,2,1,0:T(8,128)(2,1)}, bf16[3,32,64,128]{3,2,1,0:T(8,128)(2,1)S(1)}, u32[]{:S(2)}) copy-start(bf16[3,32,64,128]{3,2,1,0:T(8,128)(2,1)S(1)} %pad_maximum_fusion.1.flip_ref) | copy-start | bytes 4718596
  38.4 26.5 %copy-start.3 = (bf16[32,64,128]{2,1,0:T(8,128)(2,1)}, bf16[32,64,128]{2,1,0:T(8,128)(2,1)S(1)}, u32[]{:S(2)}) copy-start(bf16[32,64,128]{2,1,0:T(8,128)(2,1)S(1)} %get-tuple-element.15.sym_ref) | copy-start | bytes 1572868
  38.4 20.4 %collective-permute-start.5 = (bf16[15,64,128]{2,1,0:T(8,128)(2,1)S(1)}, bf16[15,64,128]{2,1,0:T(8,128)(2,1)S(1)}, u32[]{:S(2)}, u32[]{:S(2)}) collective-permute-start(bf16[15,64,128]{2,1,0:T(8,128)(2,1)S(1)} %get-tuple-element.16), channel_id=1, source_target_pairs={{0,8},{1,9},{2,10},{3,11},{4,12},{5,13},{6,14},{7,15},{8,16},{9,17... | collective-permute-start | bytes 737288 | tf_op jit(solution)/shard_map/ppermute | solution.py:55
  55.7 9.0 %collective-permute-start.6 = (bf16[15,64,128]{2,1,0:T(8,128)(2,1)S(1)}, bf16[15,64,128]{2,1,0:T(8,128)(2,1)S(1)}, u32[]{:S(2)}, u32[]{:S(2)}) collective-permute-start(bf16[15,64,128]{2,1,0:T(8,128)(2,1)S(1)} %get-tuple-element.17), channel_id=1, source_target_pairs={{8,0},{9,1},{10,2},{11,3},{12,4},{13,5},{14,6},{15,7},{16,8},{17,9... | collective-permute-start | bytes 737288 | tf_op jit(solution)/shard_map/ppermute | solution.py:55
  58.8 6.1 %copy-start.4 = (bf16[15,64,128]{2,1,0:T(8,128)(2,1)}, bf16[15,64,128]{2,1,0:T(8,128)(2,1)S(1)}, u32[]{:S(2)}) copy-start(bf16[15,64,128]{2,1,0:T(8,128)(2,1)S(1)} %collective-permute-done.5.low_ref) | copy-start | bytes 737284
  64.7 0.7 copy-start.5
  65.4 3.9 %collective-permute-start.7 = (bf16[48,16,128]{2,1,0:T(8,128)(2,1)S(1)}, bf16[48,16,128]{2,1,0:T(8,128)(2,1)S(1)}, u32[]{:S(2)}, u32[]{:S(2)}) collective-permute-start(bf16[48,16,128]{2,1,0:T(8,128)(2,1)S(1)} %get-tuple-element.18), channel_id=1, source_target_pairs={{0,1},{1,2},{2,3},{3,4},{4,5},{5,6},{6,7},{8,9},{9,10},{10,11},{11... | collective-permute-start | bytes 589832 | tf_op jit(solution)/shard_map/ppermute | solution.py:55
  66.7 10.4 %collective-permute-start.8 = (bf16[48,16,128]{2,1,0:T(8,128)(2,1)S(1)}, bf16[48,16,128]{2,1,0:T(8,128)(2,1)S(1)}, u32[]{:S(2)}, u32[]{:S(2)}) collective-permute-start(bf16[48,16,128]{2,1,0:T(8,128)(2,1)S(1)} %get-tuple-element.19), channel_id=1, source_target_pairs={{1,0},{2,1},{3,2},{4,3},{5,4},{6,5},{7,6},{9,8},{10,9},{11,10},{12... | collective-permute-start | bytes 589832 | tf_op jit(solution)/shard_map/ppermute | solution.py:55
  69.3 7.8 %copy-start.7 = (bf16[48,16,128]{2,1,0:T(8,128)(2,1)}, bf16[48,16,128]{2,1,0:T(8,128)(2,1)S(1)}, u32[]{:S(2)}) copy-start(bf16[48,16,128]{2,1,0:T(8,128)(2,1)S(1)} %collective-permute-done.7.left_ref) | copy-start | bytes 589828
  77.1 0.7 copy-start.8
  91.8 2.3 %collective-permute-start.9 = (bf16[27,64,128]{2,1,0:T(8,128)(2,1)}, bf16[27,64,128]{2,1,0:T(8,128)(2,1)S(1)}, u32[]{:S(2)}, u32[]{:S(2)}) collective-permute-start(bf16[27,64,128]{2,1,0:T(8,128)(2,1)} %bitcast.33), channel_id=1, source_target_pairs={{0,8},{1,9},{2,10},{3,11},{4,12},{5,13},{6,14},{7,15},{8,0},{9,1},... | collective-permute-start | bytes 1327112 | tf_op jit(solution)/shard_map/ppermute | solution.py:55
  136.3 4.4 %collective-permute-start.10 = (bf16[27,64,128]{2,1,0:T(8,128)(2,1)S(1)}, bf16[27,64,128]{2,1,0:T(8,128)(2,1)S(1)}, u32[]{:S(2)}, u32[]{:S(2)}) collective-permute-start(bf16[27,64,128]{2,1,0:T(8,128)(2,1)S(1)} %reshape.43.whole_ref), channel_id=1, source_target_pairs={{0,8},{1,9},{2,10},{3,11},{4,12},{5,13},{6,14},{7,15},{8,0},{9,1},... | collective-permute-start | bytes 1327112 | tf_op jit(solution)/shard_map/ppermute | solution.py:55

commit v5 on v4

--- a/solution.py
+++ b/solution.py
@@ -27,17 +27,18 @@
     return pairs
 
 
-def mirror_steps():
+def mirror_steps(other):
     grid = index_grid()
     first, second = [], []
     for y, xh, c, z, xl in np.ndindex(*SIZES):
         source = int(grid[y, xh, c, z, xl])
-        target = int(grid[z, xl, c, y, xh])
+        target = int(grid[z, xl, 1 - c if other else c, y, xh])
         if (z - y) % 4 == 2:
             step = 1 if c == 0 else -1
-            relay = ((y + step) % 4, xl, c, (z + step) % 4, xh) if c == 0 else ((y + step) % 4, xh, c, (z + step) % 4, xl)
-            first.append((source, int(grid[relay])))
-            second.append((int(grid[relay]), target))
+            across = (xl, xh) if c == 0 else (xh, xl)
+            relay = int(grid[(y + step) % 4, across[0], c, (z + step) % 4, across[1]])
+            first.append((source, relay))
+            second.append((relay, target))
         else:
             first.append((source, target))
     return first, second
@@ -201,21 +202,10 @@
             lax.fori_loop(0, 32 // size, step, 0)
 
 
-def paired(x):
-    core = lax.axis_index("core")
-    half = x.shape[2] // 2
-    keep = lax.dynamic_slice_in_dim(x, half * core, half, axis=2)
-    send = lax.dynamic_slice_in_dim(x, half * (1 - core), half, axis=2)
-    got = shift(send, core_swap())
-    low = jnp.where(core == 0, keep, got)
-    high = jnp.where(core == 0, got, keep)
-    return with_layout_constraint(jnp.concatenate([low, high], axis=1), Layout((0, 1, 2, 3)))
-
-
-def turn(direct, relayed):
+def turn(direct, second):
     far = ((lax.axis_index("z") - lax.axis_index("y")) % 4) == 2
-    arrived = with_layout_constraint(jnp.where(far, relayed, direct), Layout((0, 1, 2, 3)))
-    return jnp.swapaxes(arrived, -3, -2)
+    arrived = jnp.where(far, shift(direct, second), direct)
+    return jnp.swapaxes(with_layout_constraint(arrived, Layout((0, 1, 2, 3))), -3, -2)
 
 
 def finish_kernel(core_ref, whole_ref, other_ref, out_ref):
@@ -239,11 +229,15 @@
 def per_device(cotangent, activations, active_masks, weights):
     channels = cotangent.shape[-1]
     own = (active_masks[1:] > 0).astype(BF)
-    piece = paired(jnp.concatenate([cotangent[None], own], axis=0))
-    first, second = mirror_steps()
-    cut = piece.shape[1] // 2
-    direct = shift(piece[:, :cut], first)
-    direct2 = shift(piece[:, cut:], first)
+    core = lax.axis_index("core")
+    stack = jnp.concatenate([cotangent[None], own], axis=0)
+    half = stack.shape[2] // 2
+    arriving = []
+    for other, start in ((False, half * core), (True, half * (1 - core))):
+        piece = with_layout_constraint(lax.dynamic_slice_in_dim(stack, start, half, axis=2), Layout((0, 1, 2, 3)))
+        first, second = mirror_steps(other)
+        arriving.append((shift(piece, first), second, start))
+    (direct, second, start), (direct2, second2, start2) = arriving
     bottom = (active_masks[0] > 0).astype(BF)
     inputs = jnp.where(active_masks > 0, activations, jnp.zeros_like(activations))
     inputs = inputs.reshape(3, -1, channels).swapaxes(1, 2)
@@ -251,9 +245,9 @@
     both = jnp.concatenate([kernels, kernels.swapaxes(1, 2)], axis=-1).reshape(3, -1, 2 * channels)
     direct2, bottom, inputs, both = lax.optimization_barrier((direct2, bottom, inputs, both))
 
-    relayed = shift(direct, second)
-    relayed2 = shift(direct2, second)
-    flip = jnp.concatenate([turn(direct, relayed), turn(direct2, relayed2)], axis=2)
+    flip = jnp.zeros_like(stack)
+    flip = lax.dynamic_update_slice_in_dim(flip, turn(direct, second), start, axis=2)
+    flip = lax.dynamic_update_slice_in_dim(flip, turn(direct2, second2), start2, axis=2)
     tile = jax.ShapeDtypeStruct((32, 64, 128), BF)
     strip = jax.ShapeDtypeStruct((15, 64, 128), BF)
     sym, down, up = call(symmetric_kernel, "symmetric", (tile, strip, strip), cotangent, flip, own)
@@ -263,7 +257,7 @@
         pack_kernel, "pack", (edge, edge), sym, own, flip, low, high, scratch=[pltpu.VMEM((2, 5, 48, 8, 128), F32)]
     )
     left, right = shift(ends, neighbour(0, 1)), shift(starts, neighbour(0, -1))
-    core = lax.axis_index("core").astype(jnp.int32).reshape(1)
+    core = core.astype(jnp.int32).reshape(1)
     halves = [jax.ShapeDtypeStruct((3, 9, 64, 128), kind) for kind in (F32, BF)]
     gradient, keep, send = call(
         blocks_kernel, "blocks", (tile, *halves), sym, own, flip, low, high, left, right, core, cotangent, bottom, inputs, both,

time: 144 us -> 140 us (0.972)
  waiting for transfers between devices: 21.5 us -> 17.5 us
    ppermute x11 -> x10, waiting for transfers between devices: 21.5 us -> 17.5 us  [shift(): return lax.ppermute(x, NAMES, pairs)]
    select_n x3 -> x2, other arithmetic: 3.97 us -> 2.45 us  [turn(): arrived = jnp.where(far, shift(direct, second), direct)]
    ppermute x11 -> x10, starting transfers between devices: 42.7 us -> 42.9 us  [shift(): return lax.ppermute(x, NAMES, pairs)]
  transfers between devices with their start and end apart: 11 -> 10, of which waited for: 7 -> 6; matrix products, arithmetic and copies ran while one was open for 9% -> 9% of each run, Pallas kernels for 0% -> 0%
where the time goes in v5:
time: 140 us; the launch traced here: 139 us
  starting transfers between devices  42.9 us (31%)
  blocking collectives  40.4 us (29%)
  waiting for transfers between devices  17.5 us (12%)
  Pallas kernels  16 us (11%)
  other arithmetic  12.8 us (9%)
  local copies, waits for them, and re-layouts  8.09 us (6%)
    ppermute x10, starting transfers between devices, shift(): return lax.ppermute(x, NAMES, pairs)  42.9 us
    all_to_all x1, blocking collectives, total(): terms = lax.all_to_all(part, CHIPS, 0, 0, tiled=True)  24.6 us
    ppermute x10, waiting for transfers between devices, shift(): return lax.ppermute(x, NAMES, pairs)  17.5 us
    pallas_call x4, Pallas kernels, call(): pl.pallas_call(body, out_shape=out_shape, in_specs=[pl.BlockSpec(memory_s...  16 us
    all_to_all x1, blocking collectives, total(): whole = lax.all_to_all(copies, CHIPS, 0, 0, tiled=True).reshape(keep.shape)  15.8 us
  transfers between devices with their start and end apart: 10, of which 6 were waited for; matrix products, arithmetic and copies ran while one was open for 9% of the time, Pallas kernels for 0%

profile of v5, /device:TPU:1, one launch (start us, length us, event | category | flops | bytes accessed | tf_op | source)
XLA Modules:
  0.0 138.7 jit_solution(6548884847579023884)
XLA Ops:
  0.6 2.0 %fusion.own_ref = bf16[2,32,64,128]{3,2,1,0:T(8,128)(2,1)S(1)} fusion(s32[3,32,64,128]{3,2,1,0:T(8,128)} %param.6), kind=kLoop, calls=%fused_computation.2 | loop fusion | flops 1048576 | bytes 3145728 | tf_op jit(solution)/shard_map/convert_element_type | solution.py:231
  2.6 1.5 %fusion.3 = (bf16[3,32,32,128]{3,2,1,0:T(8,128)(2,1)}, bf16[3,32,32,128]{3,2,1,0:T(8,128)(2,1)}) fusion(s32[]{:T(128)S(6)} %select_n.37, bf16[2,32,64,128]{3,2,1,0:T(8,128)(2,1)S(1)} %fusion.own_ref, bf16[1,32,64,128]{3,2,1,0:T(8,128)(2,1)S(1)} %bitcast.22, s32[]{:T(128)S(6)} %select_n.35), kind=kLoop, calls=%fused_computation.12 | loop fusion | flops 3145728 | bytes 3145736 | tf_op jit(solution)/shard_map/concatenate | solution.py:233
  4.2 7.5 %collective-permute-start = (bf16[3,32,32,128]{3,2,1,0:T(8,128)(2,1)}, bf16[3,32,32,128]{3,2,1,0:T(8,128)(2,1)}, u32[]{:S(2)}, u32[]{:S(2)}) collective-permute-start(bf16[3,32,32,128]{3,2,1,0:T(8,128)(2,1)} %get-tuple-element.27), channel_id=1, source_target_pairs={{0,0},{1,16},{2,32},{3,48},{4,38},{5,54},{6,96},{7,112},{8,8},{9,2... | collective-permute-start | bytes 2359304 | tf_op jit(solution)/shard_map/ppermute | solution.py:56
  11.7 1.4 %collective-permute-start.2 = (bf16[3,32,32,128]{3,2,1,0:T(8,128)(2,1)}, bf16[3,32,32,128]{3,2,1,0:T(8,128)(2,1)}, u32[]{:S(2)}, u32[]{:S(2)}) collective-permute-start(bf16[3,32,32,128]{3,2,1,0:T(8,128)(2,1)} %get-tuple-element.26), channel_id=1, source_target_pairs={{0,8},{1,24},{2,40},{3,56},{4,38},{5,54},{6,104},{7,120},{8,0},{9,... | collective-permute-start | bytes 2359304 | tf_op jit(solution)/shard_map/ppermute | solution.py:56
  13.2 1.8 %compare_select_fusion = bf16[3,32,64,128]{3,2,1,0:T(8,128)(2,1)S(1)} fusion(bf16[3,32,64,128]{3,2,1,0:T(8,128)(2,1)} %param.5, s32[3,32,64,128]{3,2,1,0:T(8,128)S(1)} %copy-done.6), kind=kLoop, calls=%fused_computation | loop fusion | flops 1572864 | bytes 6291456 | tf_op jit(solution)/shard_map/jit(_where)/select_n | solution.py:242
  15.0 2.3 %copy.13 = bf16[3,3,3,128,128]{3,4,1,2,0:T(8,128)(2,1)} copy(bf16[3,3,3,128,128]{4,3,2,1,0:T(8,128)(2,1)} %bitcast.27) | data formatting | bytes 1769472 | tf_op jit(solution)/shard_map/reshape | solution.py:244
  17.3 1.6 %copy.12 = bf16[3,2048,128]{1,2,0:T(8,128)(2,1)} copy(bf16[3,2048,128]{2,1,0:T(8,128)(2,1)S(1)} %bitcast.23) | data formatting | bytes 3145728 | tf_op jit(solution)/shard_map/reshape | solution.py:243
  18.8 1.6 %reverse_bitcast_fusion.1 = (bf16[3,3,3,128,128]{4,3,1,2,0:T(8,128)(2,1)S(1)}, bf16[3,3,3,128,128]{4,3,2,1,0:T(8,128)(2,1)S(1)}) fusion(bf16[3,3,3,128,128]{3,4,1,2,0:T(8,128)(2,1)} %copy.13), kind=kLoop, calls=%fused_computation.19 | loop fusion | bytes 2654208 | tf_op jit(solution)/shard_map/transpose | solution.py:244
  20.4 0.7 collective-permute-start.1
  21.1 2.2 %fusion.5.mask_hbm = bf16[32,64,128]{2,1,0:T(8,128)(2,1)} fusion(s32[3,32,64,128]{3,2,1,0:T(8,128)} %param.6), kind=kLoop, calls=%fused_computation.20 | loop fusion | flops 524288 | bytes 1572864 | tf_op jit(solution)/shard_map/convert_element_type | solution.py:241
  23.3 1.4 %pad_maximum_fusion = bf16[3,3,3,128,256]{4,3,2,1,0:T(8,128)(2,1)} fusion(bf16[3,3,3,128,128]{4,3,2,1,0:T(8,128)(2,1)S(1)} %get-tuple-element.29, bf16[3,3,3,128,128]{4,3,1,2,0:T(8,128)(2,1)S(1)} %get-tuple-element.28), kind=kLoop, calls=%fused_computation.5 | loop fusion | flops 3538944 | bytes 3538944 | tf_op jit(solution)/shard_map/concatenate | solution.py:245
  24.8 0.7 collective-permute-start.3
  25.5 1.2 broadcast_select_fusion.1
  27.5 1.2 broadcast_select_fusion
  29.4 22.7 %collective-permute-start.4 = (bf16[15,64,128]{2,1,0:T(8,128)(2,1)S(1)}, bf16[15,64,128]{2,1,0:T(8,128)(2,1)S(1)}, u32[]{:S(2)}, u32[]{:S(2)}) collective-permute-start(bf16[15,64,128]{2,1,0:T(8,128)(2,1)S(1)} %get-tuple-element.16), channel_id=1, source_target_pairs={{0,8},{1,9},{2,10},{3,11},{4,12},{5,13},{6,14},{7,15},{8,16},{9,17... | collective-permute-start | bytes 737288 | tf_op jit(solution)/shard_map/ppermute | solution.py:56
  52.2 1.9 %collective-permute-start.5 = (bf16[15,64,128]{2,1,0:T(8,128)(2,1)S(1)}, bf16[15,64,128]{2,1,0:T(8,128)(2,1)S(1)}, u32[]{:S(2)}, u32[]{:S(2)}) collective-permute-start(bf16[15,64,128]{2,1,0:T(8,128)(2,1)S(1)} %get-tuple-element.17), channel_id=1, source_target_pairs={{8,0},{9,1},{10,2},{11,3},{12,4},{13,5},{14,6},{15,7},{16,8},{17,9... | collective-permute-start | bytes 737288 | tf_op jit(solution)/shard_map/ppermute | solution.py:56
  54.1 1.2 collective-permute-done.4.low_ref
  55.3 5.9 %collective-permute-done.5.high_ref = bf16[15,64,128]{2,1,0:T(8,128)(2,1)S(1)} collective-permute-done((bf16[15,64,128]{2,1,0:T(8,128)(2,1)S(1)}, bf16[15,64,128]{2,1,0:T(8,128)(2,1)S(1)}, u32[]{:S(2)}, u32[]{:S(2)}) %collective-permute-start.5) | collective-permute-done | bytes 245792 | tf_op jit(solution)/shard_map/ppermute | solution.py:56
  61.4 0.5 copy-done.5
  61.9 3.3 %collective-permute-start.6 = (bf16[48,16,128]{2,1,0:T(8,128)(2,1)S(1)}, bf16[48,16,128]{2,1,0:T(8,128)(2,1)S(1)}, u32[]{:S(2)}, u32[]{:S(2)}) collective-permute-start(bf16[48,16,128]{2,1,0:T(8,128)(2,1)S(1)} %get-tuple-element.18), channel_id=1, source_target_pairs={{0,1},{1,2},{2,3},{3,4},{4,5},{5,6},{6,7},{8,9},{9,10},{10,11},{11... | collective-permute-start | bytes 589832 | tf_op jit(solution)/shard_map/ppermute | solution.py:56
  65.3 1.3 collective-permute-start.7
  66.6 1.3 collective-permute-done.6.left_ref
  67.8 5.7 %collective-permute-done.7.right_ref = bf16[48,16,128]{2,1,0:T(8,128)(2,1)S(1)} collective-permute-done((bf16[48,16,128]{2,1,0:T(8,128)(2,1)S(1)}, bf16[48,16,128]{2,1,0:T(8,128)(2,1)S(1)}, u32[]{:S(2)}, u32[]{:S(2)}) %collective-permute-start.7) | collective-permute-done | bytes 196640 | tf_op jit(solution)/shard_map/ppermute | solution.py:56
  73.6 0.7 copy-done.8
  74.3 14.1 %blocks.1 = (bf16[32,64,128]{2,1,0:T(8,128)(2,1)}, f32[3,9,64,128]{3,2,1,0:T(8,128)}, bf16[3,9,64,128]{3,2,1,0:T(8,128)(2,1)}) custom-call(bf16[32,64,128]{2,1,0:T(8,128)(2,1)} %copy-done.3, bf16[2,32,64,128]{3,2,1,0:T(8,128)(2,1)} %copy-done, bf16[3,32,64,128]{3,2,1,0:T(8,128)(2,1)} %copy-done.1, bf16[15,64,128]{2,1,0:T(8,128)(2,1)} %copy-done.4, ...), custom_call_target="tpu_custom_call" | custom-call | flops 8000000000 | bytes 20000000 | tf_op jit(solution)/shard_map/blocks/pallas_call | solution.py:70
  88.6 2.0 %collective-permute-done.8 = bf16[27,64,128]{2,1,0:T(8,128)(2,1)S(1)} collective-permute-done((bf16[27,64,128]{2,1,0:T(8,128)(2,1)}, bf16[27,64,128]{2,1,0:T(8,128)(2,1)S(1)}, u32[]{:S(2)}, u32[]{:S(2)}) %collective-permute-start.8) | collective-permute-done | bytes 442400 | tf_op jit(solution)/shard_map/ppermute | solution.py:56
  90.6 1.3 fusion.2
  92.1 24.6 %all_to_all.10 = bf16[64,27,128]{2,1,0:T(8,128)(2,1)S(1)} all-to-all(bf16[64,27,128]{2,1,0:T(8,128)(2,1)S(1)} %reshape.42), channel_id=1, replica_groups=mesh['y'=4,'xh'=2,'core'=2,'z'=4,'xl'=2] {'y','xh','z','xl'}, dimensions={0} | all-to-all | bytes 884736 | tf_op jit(solution)/shard_map/all_to_all | solution.py:220
  116.9 15.8 %all_to_all.11 = bf16[64,27,128]{2,1,0:T(8,128)(2,1)S(1)} all-to-all(bf16[64,27,128]{2,1,0:T(8,128)(2,1)S(1)} %broadcast_in_dim.10), channel_id=1, replica_groups=mesh['y'=4,'xh'=2,'core'=2,'z'=4,'xl'=2] {'y','xh','z','xl'}, dimensions={0} | all-to-all | bytes 884736 | tf_op jit(solution)/shard_map/all_to_all | solution.py:223
  132.8 3.0 %collective-permute-start.9 = (bf16[27,64,128]{2,1,0:T(8,128)(2,1)S(1)}, bf16[27,64,128]{2,1,0:T(8,128)(2,1)S(1)}, u32[]{:S(2)}, u32[]{:S(2)}) collective-permute-start(bf16[27,64,128]{2,1,0:T(8,128)(2,1)S(1)} %reshape.43.whole_ref), channel_id=1, source_target_pairs={{0,8},{1,9},{2,10},{3,11},{4,12},{5,13},{6,14},{7,15},{8,0},{9,1},... | collective-permute-start | bytes 1327112 | tf_op jit(solution)/shard_map/ppermute | solution.py:56
  135.8 1.4 %collective-permute-done.9.other_ref = bf16[27,64,128]{2,1,0:T(8,128)(2,1)S(1)} collective-permute-done((bf16[27,64,128]{2,1,0:T(8,128)(2,1)S(1)}, bf16[27,64,128]{2,1,0:T(8,128)(2,1)S(1)}, u32[]{:S(2)}, u32[]{:S(2)}) %collective-permute-start.9) | collective-permute-done | bytes 442400 | tf_op jit(solution)/shard_map/ppermute | solution.py:56
  137.2 1.4 %finish.1 = f32[27,128,128]{2,1,0:T(8,128)} custom-call(s32[1]{0:T(128)} %bitcast.10.core_ref, bf16[27,64,128]{2,1,0:T(8,128)(2,1)S(1)} %reshape.43.whole_ref, bf16[27,64,128]{2,1,0:T(8,128)(2,1)S(1)} %collective-permute-done.9.other_ref), custom_call_target="tpu_custom_call" | custom-call | flops 1000000 | bytes 1000000 | tf_op jit(solution)/shard_map/finish/pallas_call | solution.py:70
  (30 shorter events, 2.4 us)
Async XLA Ops:
  0.6 2.0 %copy-start.2 = (bf16[32,64,128]{2,1,0:T(8,128)(2,1)S(1)}, bf16[32,64,128]{2,1,0:T(8,128)(2,1)}, u32[]{:S(2)}) copy-start(bf16[32,64,128]{2,1,0:T(8,128)(2,1)} %cotangent_hbm.1) | copy-start | bytes 1572868
  2.6 58.6 %copy-start = (bf16[2,32,64,128]{3,2,1,0:T(8,128)(2,1)}, bf16[2,32,64,128]{3,2,1,0:T(8,128)(2,1)S(1)}, u32[]{:S(2)}) copy-start(bf16[2,32,64,128]{3,2,1,0:T(8,128)(2,1)S(1)} %fusion.own_ref) | copy-start | bytes 3145732
  2.6 10.5 %copy-start.6 = (s32[3,32,64,128]{3,2,1,0:T(8,128)S(1)}, s32[3,32,64,128]{3,2,1,0:T(8,128)}, u32[]{:S(2)}) copy-start(s32[3,32,64,128]{3,2,1,0:T(8,128)} %param.6) | copy-start | bytes 9437188
  4.2 16.2 %collective-permute-start = (bf16[3,32,32,128]{3,2,1,0:T(8,128)(2,1)}, bf16[3,32,32,128]{3,2,1,0:T(8,128)(2,1)}, u32[]{:S(2)}, u32[]{:S(2)}) collective-permute-start(bf16[3,32,32,128]{3,2,1,0:T(8,128)(2,1)} %get-tuple-element.27), channel_id=1, source_target_pairs={{0,0},{1,16},{2,32},{3,48},{4,38},{5,54},{6,96},{7,112},{8,8},{9,2... | collective-permute-start | bytes 2359304 | tf_op jit(solution)/shard_map/ppermute | solution.py:56
  11.7 13.1 %collective-permute-start.2 = (bf16[3,32,32,128]{3,2,1,0:T(8,128)(2,1)}, bf16[3,32,32,128]{3,2,1,0:T(8,128)(2,1)}, u32[]{:S(2)}, u32[]{:S(2)}) collective-permute-start(bf16[3,32,32,128]{3,2,1,0:T(8,128)(2,1)} %get-tuple-element.26), channel_id=1, source_target_pairs={{0,8},{1,24},{2,40},{3,56},{4,38},{5,54},{6,104},{7,120},{8,0},{9,... | collective-permute-start | bytes 2359304 | tf_op jit(solution)/shard_map/ppermute | solution.py:56
  20.4 5.1 %collective-permute-start.1 = (bf16[3,32,32,128]{3,2,1,0:T(8,128)(2,1)}, bf16[3,32,32,128]{3,2,1,0:T(8,128)(2,1)S(1)}, u32[]{:S(2)}, u32[]{:S(2)}) collective-permute-start(bf16[3,32,32,128]{3,2,1,0:T(8,128)(2,1)} %collective-permute-done), channel_id=1, source_target_pairs={{38,64},{54,80},{106,72},{107,88},{39,65},{55,81},{122,73},{123,89... | collective-permute-start | bytes 2359304 | tf_op jit(solution)/shard_map/ppermute | solution.py:56
  24.8 2.7 %collective-permute-start.3 = (bf16[3,32,32,128]{3,2,1,0:T(8,128)(2,1)}, bf16[3,32,32,128]{3,2,1,0:T(8,128)(2,1)S(1)}, u32[]{:S(2)}, u32[]{:S(2)}) collective-permute-start(bf16[3,32,32,128]{3,2,1,0:T(8,128)(2,1)} %collective-permute-done.2), channel_id=1, source_target_pairs={{38,72},{54,88},{106,64},{107,80},{39,73},{55,89},{122,65},{123,81... | collective-permute-start | bytes 2359304 | tf_op jit(solution)/shard_map/ppermute | solution.py:56
  29.1 32.1 %copy-start.1 = (bf16[3,32,64,128]{3,2,1,0:T(8,128)(2,1)}, bf16[3,32,64,128]{3,2,1,0:T(8,128)(2,1)S(1)}, u32[]{:S(2)}) copy-start(bf16[3,32,64,128]{3,2,1,0:T(8,128)(2,1)S(1)} %bitcast_dynamic-update-slice_fusion.flip_ref) | copy-start | bytes 4718596
  29.4 32.0 %copy-start.3 = (bf16[32,64,128]{2,1,0:T(8,128)(2,1)}, bf16[32,64,128]{2,1,0:T(8,128)(2,1)S(1)}, u32[]{:S(2)}) copy-start(bf16[32,64,128]{2,1,0:T(8,128)(2,1)S(1)} %get-tuple-element.15.sym_ref) | copy-start | bytes 1572868
  29.4 25.9 %collective-permute-start.4 = (bf16[15,64,128]{2,1,0:T(8,128)(2,1)S(1)}, bf16[15,64,128]{2,1,0:T(8,128)(2,1)S(1)}, u32[]{:S(2)}, u32[]{:S(2)}) collective-permute-start(bf16[15,64,128]{2,1,0:T(8,128)(2,1)S(1)} %get-tuple-element.16), channel_id=1, source_target_pairs={{0,8},{1,9},{2,10},{3,11},{4,12},{5,13},{6,14},{7,15},{8,16},{9,17... | collective-permute-start | bytes 737288 | tf_op jit(solution)/shard_map/ppermute | solution.py:56
  52.2 9.0 %collective-permute-start.5 = (bf16[15,64,128]{2,1,0:T(8,128)(2,1)S(1)}, bf16[15,64,128]{2,1,0:T(8,128)(2,1)S(1)}, u32[]{:S(2)}, u32[]{:S(2)}) collective-permute-start(bf16[15,64,128]{2,1,0:T(8,128)(2,1)S(1)} %get-tuple-element.17), channel_id=1, source_target_pairs={{8,0},{9,1},{10,2},{11,3},{12,4},{13,5},{14,6},{15,7},{16,8},{17,9... | collective-permute-start | bytes 737288 | tf_op jit(solution)/shard_map/ppermute | solution.py:56
  55.3 6.1 %copy-start.4 = (bf16[15,64,128]{2,1,0:T(8,128)(2,1)}, bf16[15,64,128]{2,1,0:T(8,128)(2,1)S(1)}, u32[]{:S(2)}) copy-start(bf16[15,64,128]{2,1,0:T(8,128)(2,1)S(1)} %collective-permute-done.4.low_ref) | copy-start | bytes 737284
  61.2 0.7 copy-start.5
  61.9 5.9 %collective-permute-start.6 = (bf16[48,16,128]{2,1,0:T(8,128)(2,1)S(1)}, bf16[48,16,128]{2,1,0:T(8,128)(2,1)S(1)}, u32[]{:S(2)}, u32[]{:S(2)}) collective-permute-start(bf16[48,16,128]{2,1,0:T(8,128)(2,1)S(1)} %get-tuple-element.18), channel_id=1, source_target_pairs={{0,1},{1,2},{2,3},{3,4},{4,5},{5,6},{6,7},{8,9},{9,10},{10,11},{11... | collective-permute-start | bytes 589832 | tf_op jit(solution)/shard_map/ppermute | solution.py:56
  65.3 8.3 %collective-permute-start.7 = (bf16[48,16,128]{2,1,0:T(8,128)(2,1)S(1)}, bf16[48,16,128]{2,1,0:T(8,128)(2,1)S(1)}, u32[]{:S(2)}, u32[]{:S(2)}) collective-permute-start(bf16[48,16,128]{2,1,0:T(8,128)(2,1)S(1)} %get-tuple-element.19), channel_id=1, source_target_pairs={{1,0},{2,1},{3,2},{4,3},{5,4},{6,5},{7,6},{9,8},{10,9},{11,10},{12... | collective-permute-start | bytes 589832 | tf_op jit(solution)/shard_map/ppermute | solution.py:56
  67.8 5.7 %copy-start.7 = (bf16[48,16,128]{2,1,0:T(8,128)(2,1)}, bf16[48,16,128]{2,1,0:T(8,128)(2,1)S(1)}, u32[]{:S(2)}) copy-start(bf16[48,16,128]{2,1,0:T(8,128)(2,1)S(1)} %collective-permute-done.6.left_ref) | copy-start | bytes 589828
  73.6 0.7 copy-start.8
  88.3 2.3 %collective-permute-start.8 = (bf16[27,64,128]{2,1,0:T(8,128)(2,1)}, bf16[27,64,128]{2,1,0:T(8,128)(2,1)S(1)}, u32[]{:S(2)}, u32[]{:S(2)}) collective-permute-start(bf16[27,64,128]{2,1,0:T(8,128)(2,1)} %bitcast.28), channel_id=1, source_target_pairs={{0,8},{1,9},{2,10},{3,11},{4,12},{5,13},{6,14},{7,15},{8,0},{9,1},... | collective-permute-start | bytes 1327112 | tf_op jit(solution)/shard_map/ppermute | solution.py:56
  132.8 4.4 %collective-permute-start.9 = (bf16[27,64,128]{2,1,0:T(8,128)(2,1)S(1)}, bf16[27,64,128]{2,1,0:T(8,128)(2,1)S(1)}, u32[]{:S(2)}, u32[]{:S(2)}) collective-permute-start(bf16[27,64,128]{2,1,0:T(8,128)(2,1)S(1)} %reshape.43.whole_ref), channel_id=1, source_target_pairs={{0,8},{1,9},{2,10},{3,11},{4,12},{5,13},{6,14},{7,15},{8,0},{9,1},... | collective-permute-start | bytes 1327112 | tf_op jit(solution)/shard_map/ppermute | solution.py:56

commit v6 on v5

--- a/solution.py
+++ b/solution.py
@@ -110,16 +110,29 @@
 
 
 def blocks_kernel(
-    sym_ref, own_ref, flip_ref, low_ref, high_ref, left_ref, right_ref,
-    core_ref, cotangent_hbm, mask_hbm, inputs_hbm, weights_hbm, gradient_ref, keep_ref, send_ref,
+    sym_ref, low_ref, high_ref, left_ref, right_ref, core_ref, own_hbm, flip_hbm, cotangent_hbm, mask_hbm, inputs_hbm, weights_hbm,
+    gradient_ref, keep_ref, send_ref,
     sym, masks, patches, change, cotangent_ref, mask_ref, inputs_ref, weights_ref, arrived,
 ):
-    copies = []
-    for n, (far, near) in enumerate((
-        (inputs_hbm, inputs_ref), (weights_hbm, weights_ref), (cotangent_hbm, cotangent_ref), (mask_hbm, mask_ref),
-    )):
-        copies.append(pltpu.make_async_copy(far, near, arrived.at[n]))
-        copies[-1].start()
+    def fetch(n, far, near):
+        copy = pltpu.make_async_copy(far, near, arrived.at[n])
+        copy.start()
+        return copy
+
+    tile = (slice(8, 40), slice(0, 64))
+    needed = {}
+    for layer in (2, 1, 0):
+        n = 4 * layer
+        ahead = [fetch(n, inputs_hbm.at[layer], inputs_ref.at[layer])]
+        beside = [fetch(n + 1, weights_hbm.at[layer], weights_ref.at[layer])]
+        if layer:
+            beside.append(fetch(n + 2, own_hbm.at[layer - 1], masks.at[(layer - 1, *tile)]))
+            beside.append(fetch(n + 3, flip_hbm.at[layer], masks.at[(layer + 1, *tile)]))
+        else:
+            beside.append(fetch(n + 2, cotangent_hbm, cotangent_ref))
+            beside.append(fetch(n + 3, mask_hbm, mask_ref))
+        needed[layer] = (ahead, beside)
+
     sym[0:1] = jnp.zeros((1, 96, 128), F32)
     sym[47:48] = jnp.zeros((1, 96, 128), F32)
     sym[8:40, 8:72] = sym_ref[...].astype(F32)
@@ -130,18 +143,14 @@
     sym[:, 72:80] = after[:, :8]
     masks[:, 4:8] = jnp.zeros((4, 4, 80, 128), BF)
     masks[:, 40:44] = jnp.zeros((4, 4, 80, 128), BF)
-    tiles = (own_ref.at[0], own_ref.at[1], flip_ref.at[1], flip_ref.at[2])
     for k, (lows, highs) in enumerate(((7, 0), (4, 7), (3, 4), (0, 3))):
         w, at = WIDTHS[k + 1], STARTS[k + 1]
-        masks[k, 8:40, 0:64] = tiles[k][...]
         masks[k, 8 - w : 8, 0:64] = low_ref[at : at + w]
         masks[k, 40 : 40 + w, 0:64] = high_ref[at : at + w]
         rim = jnp.concatenate([roll8(after[:, 8:], highs), roll8(before[:, 8:], lows)], axis=1)
         masks[k, :, 64:80] = rim.astype(BF)
 
     for layer in (2, 1, 0):
-        for copy in {2: copies[:2], 1: (), 0: copies[2:]}[layer]:
-            copy.wait()
         d = 2**layer
         first, count = ((8, 32), (6, 36), (4, 40))[layer]
         sym[:, 0:8] = sym[:, 80:88]
@@ -153,6 +162,8 @@
             return carry
 
         lax.fori_loop(first - d, first + count + d, gather, 0, unroll=True)
+        for copy in needed[layer][0]:
+            copy.wait()
         total = None
         for r in (8, 24):
             right = jnp.concatenate(
@@ -167,6 +178,8 @@
         for t in range(9):
             keep_ref[layer, 8 - t] = kept[:, t * 128 : (t + 1) * 128]
             send_ref[layer, 8 - t] = sent[:, t * 128 : (t + 1) * 128]
+        for copy in needed[layer][1]:
+            copy.wait()
         if layer:
             def step(i, carry):
                 f = first + size * i
@@ -205,7 +218,7 @@
 def turn(direct, second):
     far = ((lax.axis_index("z") - lax.axis_index("y")) % 4) == 2
     arrived = jnp.where(far, shift(direct, second), direct)
-    return jnp.swapaxes(with_layout_constraint(arrived, Layout((0, 1, 2, 3))), -3, -2)
+    return jnp.swapaxes(arrived, -3, -2)
 
 
 def finish_kernel(core_ref, whole_ref, other_ref, out_ref):
@@ -260,7 +273,8 @@
     core = core.astype(jnp.int32).reshape(1)
     halves = [jax.ShapeDtypeStruct((3, 9, 64, 128), kind) for kind in (F32, BF)]
     gradient, keep, send = call(
-        blocks_kernel, "blocks", (tile, *halves), sym, own, flip, low, high, left, right, core, cotangent, bottom, inputs, both,
+        blocks_kernel, "blocks", (tile, *halves), sym, low, high, left, right, core,
+        own, flip, cotangent, bottom, inputs, both,
         scratch=[
             pltpu.VMEM((48, 96, 128), F32),
             pltpu.VMEM((4, 48, 80, 128), BF),
@@ -270,9 +284,9 @@
             pltpu.VMEM((32, 64, 128), BF),
             pltpu.VMEM((3, 128, 2048), BF),
             pltpu.VMEM((3, 1152, 256), BF),
-            pltpu.SemaphoreType.DMA((4,)),
+            pltpu.SemaphoreType.DMA((12,)),
         ],
-        far=4,
+        far=6,
         flops=8 * 10**9, moved=2 * 10**7, room=60,
     )
     sums = total(keep.reshape(27, 64, 128), send.reshape(27, 64, 128), core)

time: 140 us -> 138 us (0.986)
  other arithmetic: 12.8 us -> 10.6 us
  local copies, waits for them, and re-layouts: 8.09 us -> 9.79 us
  Pallas kernels: 16 us -> 14.6 us
    dynamic_update_slice x0 -> x2, other arithmetic: none -> 2.87 us  [the longest x1 1.44 us: per_device(): lax.dynamic_update_slice_in_dim(flip, turn(direct2, second2), start2, axi...]
    select_n x2 -> x0, other arithmetic: 2.45 us -> none  [turn(): arrived = jnp.where(far, shift(direct, second), direct)]
    another operation x1 -> x3, local copies, waits for them, and re-layouts: 0.38 us -> 2.78 us  [the longest x2 2.4 us: per_device(): with_layout_constraint(lax.dynamic_slice_in_dim(stack, start, half, axis=...]
    select_n x1, other arithmetic: 1.82 us -> 0.36 us  [per_device(): jnp.where(active_masks > 0, activations, jnp.zeros_like(activations))]
where the time goes in v6:
time: 138 us; the launch traced here: 137 us
  starting transfers between devices  43.2 us (31%)
  blocking collectives  40.4 us (29%)
  waiting for transfers between devices  17.4 us (13%)
  Pallas kernels  14.6 us (11%)
  other arithmetic  10.6 us (8%)
  local copies, waits for them, and re-layouts  9.79 us (7%)
    ppermute x10, starting transfers between devices, shift(): return lax.ppermute(x, NAMES, pairs)  43.2 us
    all_to_all x1, blocking collectives, total(): terms = lax.all_to_all(part, CHIPS, 0, 0, tiled=True)  24.6 us
    ppermute x10, waiting for transfers between devices, shift(): return lax.ppermute(x, NAMES, pairs)  17.4 us
    all_to_all x1, blocking collectives, total(): whole = lax.all_to_all(copies, CHIPS, 0, 0, tiled=True).reshape(keep.shape)  15.8 us
    pallas_call x4, Pallas kernels, call(): pl.pallas_call(body, out_shape=out_shape, in_specs=[pl.BlockSpec(memory_s...  14.6 us
  transfers between devices with their start and end apart: 10, of which 6 were waited for; matrix products, arithmetic and copies ran while one was open for 9% of the time, Pallas kernels for 0%

profile of v6, /device:TPU:1, one launch (start us, length us, event | category | flops | bytes accessed | tf_op | source)
XLA Modules:
  0.0 136.9 jit_solution(12768046805466908760)
XLA Ops:
  0.6 2.0 %fusion.own_ref.own_hbm = bf16[2,32,64,128]{3,2,1,0:T(8,128)(2,1)S(1)} fusion(s32[3,32,64,128]{3,2,1,0:T(8,128)} %param.6), kind=kLoop, calls=%fused_computation.2 | loop fusion | flops 1048576 | bytes 3145728 | tf_op jit(solution)/shard_map/convert_element_type | solution.py:244
  3.0 1.2 copy.11
  4.2 7.5 %collective-permute-start = (bf16[3,32,32,128]{3,1,2,0:T(8,128)(2,1)}, bf16[3,32,32,128]{3,1,2,0:T(8,128)(2,1)}, u32[]{:S(2)}, u32[]{:S(2)}) collective-permute-start(bf16[3,32,32,128]{3,1,2,0:T(8,128)(2,1)} %copy.11), channel_id=1, source_target_pairs={{0,0},{1,16},{2,32},{3,48},{4,38},{5,54},{6,96},{7,112},{8,8},{9,2... | collective-permute-start | bytes 2359304 | tf_op jit(solution)/shard_map/ppermute | solution.py:56
  11.8 1.2 copy.12
  13.0 1.4 %collective-permute-start.2 = (bf16[3,32,32,128]{3,1,2,0:T(8,128)(2,1)}, bf16[3,32,32,128]{3,1,2,0:T(8,128)(2,1)}, u32[]{:S(2)}, u32[]{:S(2)}) collective-permute-start(bf16[3,32,32,128]{3,1,2,0:T(8,128)(2,1)} %copy.12), channel_id=1, source_target_pairs={{0,8},{1,24},{2,40},{3,56},{4,38},{5,54},{6,104},{7,120},{8,0},{9,... | collective-permute-start | bytes 2359304 | tf_op jit(solution)/shard_map/ppermute | solution.py:56
  14.7 2.3 %copy.14 = bf16[3,3,3,128,128]{3,4,1,2,0:T(8,128)(2,1)} copy(bf16[3,3,3,128,128]{4,3,2,1,0:T(8,128)(2,1)} %bitcast.27) | data formatting | bytes 1769472 | tf_op jit(solution)/shard_map/reshape | solution.py:257
  17.0 1.6 %copy.13 = bf16[3,2048,128]{1,2,0:T(8,128)(2,1)} copy(bf16[3,2048,128]{2,1,0:T(8,128)(2,1)S(1)} %bitcast.23) | data formatting | bytes 3145728 | tf_op jit(solution)/shard_map/reshape | solution.py:256
  18.6 1.6 %reverse_bitcast_fusion.1 = (bf16[3,3,3,128,128]{4,3,1,2,0:T(8,128)(2,1)S(1)}, bf16[3,3,3,128,128]{4,3,2,1,0:T(8,128)(2,1)S(1)}) fusion(bf16[3,3,3,128,128]{3,4,1,2,0:T(8,128)(2,1)} %copy.14), kind=kLoop, calls=%fused_computation.17 | loop fusion | bytes 2654208 | tf_op jit(solution)/shard_map/transpose | solution.py:257
  20.2 2.2 %fusion.5.mask_hbm = bf16[32,64,128]{2,1,0:T(8,128)(2,1)} fusion(s32[3,32,64,128]{3,2,1,0:T(8,128)} %param.6), kind=kLoop, calls=%fused_computation.18 | loop fusion | flops 524288 | bytes 1572864 | tf_op jit(solution)/shard_map/convert_element_type | solution.py:254
  22.4 0.7 collective-permute-start.1
  23.1 1.4 %pad_maximum_fusion = bf16[3,3,3,128,256]{4,3,2,1,0:T(8,128)(2,1)} fusion(bf16[3,3,3,128,128]{4,3,2,1,0:T(8,128)(2,1)S(1)} %get-tuple-element.29, bf16[3,3,3,128,128]{4,3,1,2,0:T(8,128)(2,1)S(1)} %get-tuple-element.28), kind=kLoop, calls=%fused_computation.5 | loop fusion | flops 3538944 | bytes 3538944 | tf_op jit(solution)/shard_map/concatenate | solution.py:258
  24.5 0.7 collective-permute-start.3
  25.7 1.4 %bitcast_dynamic-update-slice_fusion.1 = bf16[3,32,64,128]{3,2,1,0:T(8,128)(2,1)S(1)} fusion(bf16[3,32,64,128]{3,2,1,0:T(8,128)(2,1)S(1)} %broadcast.7, s32[]{:T(128)S(6)} %select_n.35, bf16[3,32,32,128]{3,1,2,0:T(8,128)(2,1)S(1)} %collective-permute-done.1, bf16[3,32,32,128]{3,1,2,0:T(8,128)(2,1)} %collective-permute-done, pred[]{:T(512)S(6)} %eq.7), kind=kLoop, calls=%fused_computation.15 | loop fusion | flops 393216 | bytes 2359301 | tf_op jit(solution)/shard_map/dynamic_update_slice | solution.py:262
  27.1 1.4 %bitcast_dynamic-update-slice_fusion.flip_ref.flip_hbm = bf16[3,32,64,128]{3,2,1,0:T(8,128)(2,1)S(1)} fusion(bf16[3,32,64,128]{3,2,1,0:T(8,128)(2,1)S(1)} %bitcast_dynamic-update-slice_fusion.1, s32[]{:T(128)S(6)} %select_n.37, bf16[3,32,32,128]{3,1,2,0:T(8,128)(2,1)S(1)} %collective-permute-done.3, bf16[3,32,32,128]{3,1,2,0:T(8,128)(2,1)} %collective-permute-done.2, ...), kind=kLoop, calls=%fused_computation.14 | loop fusion | flops 393216 | bytes 2359301 | tf_op jit(solution)/shard_map/dynamic_update_slice | solution.py:263
  28.9 23.1 %collective-permute-start.4 = (bf16[15,64,128]{2,1,0:T(8,128)(2,1)S(1)}, bf16[15,64,128]{2,1,0:T(8,128)(2,1)S(1)}, u32[]{:S(2)}, u32[]{:S(2)}) collective-permute-start(bf16[15,64,128]{2,1,0:T(8,128)(2,1)S(1)} %get-tuple-element.16), channel_id=1, source_target_pairs={{0,8},{1,9},{2,10},{3,11},{4,12},{5,13},{6,14},{7,15},{8,16},{9,17... | collective-permute-start | bytes 737288 | tf_op jit(solution)/shard_map/ppermute | solution.py:56
  51.9 1.9 %collective-permute-start.5 = (bf16[15,64,128]{2,1,0:T(8,128)(2,1)S(1)}, bf16[15,64,128]{2,1,0:T(8,128)(2,1)S(1)}, u32[]{:S(2)}, u32[]{:S(2)}) collective-permute-start(bf16[15,64,128]{2,1,0:T(8,128)(2,1)S(1)} %get-tuple-element.17), channel_id=1, source_target_pairs={{8,0},{9,1},{10,2},{11,3},{12,4},{13,5},{14,6},{15,7},{16,8},{17,9... | collective-permute-start | bytes 737288 | tf_op jit(solution)/shard_map/ppermute | solution.py:56
  53.9 1.2 collective-permute-done.4.low_ref
  55.0 5.9 %collective-permute-done.5.high_ref = bf16[15,64,128]{2,1,0:T(8,128)(2,1)S(1)} collective-permute-done((bf16[15,64,128]{2,1,0:T(8,128)(2,1)S(1)}, bf16[15,64,128]{2,1,0:T(8,128)(2,1)S(1)}, u32[]{:S(2)}, u32[]{:S(2)}) %collective-permute-start.5) | collective-permute-done | bytes 245792 | tf_op jit(solution)/shard_map/ppermute | solution.py:56
  61.2 0.5 copy-done.5
  61.7 3.3 %collective-permute-start.6 = (bf16[48,16,128]{2,1,0:T(8,128)(2,1)S(1)}, bf16[48,16,128]{2,1,0:T(8,128)(2,1)S(1)}, u32[]{:S(2)}, u32[]{:S(2)}) collective-permute-start(bf16[48,16,128]{2,1,0:T(8,128)(2,1)S(1)} %get-tuple-element.18), channel_id=1, source_target_pairs={{0,1},{1,2},{2,3},{3,4},{4,5},{5,6},{6,7},{8,9},{9,10},{10,11},{11... | collective-permute-start | bytes 589832 | tf_op jit(solution)/shard_map/ppermute | solution.py:56
  65.0 1.5 %collective-permute-start.7 = (bf16[48,16,128]{2,1,0:T(8,128)(2,1)S(1)}, bf16[48,16,128]{2,1,0:T(8,128)(2,1)S(1)}, u32[]{:S(2)}, u32[]{:S(2)}) collective-permute-start(bf16[48,16,128]{2,1,0:T(8,128)(2,1)S(1)} %get-tuple-element.19), channel_id=1, source_target_pairs={{1,0},{2,1},{3,2},{4,3},{5,4},{6,5},{7,6},{9,8},{10,9},{11,10},{12... | collective-permute-start | bytes 589832 | tf_op jit(solution)/shard_map/ppermute | solution.py:56
  66.5 1.1 collective-permute-done.6.left_ref
  67.6 5.7 %collective-permute-done.7.right_ref = bf16[48,16,128]{2,1,0:T(8,128)(2,1)S(1)} collective-permute-done((bf16[48,16,128]{2,1,0:T(8,128)(2,1)S(1)}, bf16[48,16,128]{2,1,0:T(8,128)(2,1)S(1)}, u32[]{:S(2)}, u32[]{:S(2)}) %collective-permute-start.7) | collective-permute-done | bytes 196640 | tf_op jit(solution)/shard_map/ppermute | solution.py:56
  73.3 0.7 copy-done.9
  74.0 12.7 %blocks.1 = (bf16[32,64,128]{2,1,0:T(8,128)(2,1)}, f32[3,9,64,128]{3,2,1,0:T(8,128)}, bf16[3,9,64,128]{3,2,1,0:T(8,128)(2,1)}) custom-call(bf16[32,64,128]{2,1,0:T(8,128)(2,1)} %copy-done.3, bf16[15,64,128]{2,1,0:T(8,128)(2,1)} %copy-done.4, bf16[15,64,128]{2,1,0:T(8,128)(2,1)} %copy-done.5, bf16[48,16,128]{2,1,0:T(8,128)(2,1)} %copy-done.8, ...), custom_call_target="tpu_custom_call" | custom-call | flops 8000000000 | bytes 20000000 | tf_op jit(solution)/shard_map/blocks/pallas_call | solution.py:70
  86.8 2.0 %collective-permute-done.8 = bf16[27,64,128]{2,1,0:T(8,128)(2,1)S(1)} collective-permute-done((bf16[27,64,128]{2,1,0:T(8,128)(2,1)}, bf16[27,64,128]{2,1,0:T(8,128)(2,1)S(1)}, u32[]{:S(2)}, u32[]{:S(2)}) %collective-permute-start.8) | collective-permute-done | bytes 442400 | tf_op jit(solution)/shard_map/ppermute | solution.py:56
  88.8 1.3 fusion.2
  90.3 24.6 %all_to_all.10 = bf16[64,27,128]{2,1,0:T(8,128)(2,1)S(1)} all-to-all(bf16[64,27,128]{2,1,0:T(8,128)(2,1)S(1)} %reshape.42), channel_id=1, replica_groups=mesh['y'=4,'xh'=2,'core'=2,'z'=4,'xl'=2] {'y','xh','z','xl'}, dimensions={0} | all-to-all | bytes 884736 | tf_op jit(solution)/shard_map/all_to_all | solution.py:233
  115.1 15.8 %all_to_all.11 = bf16[64,27,128]{2,1,0:T(8,128)(2,1)S(1)} all-to-all(bf16[64,27,128]{2,1,0:T(8,128)(2,1)S(1)} %broadcast_in_dim.10), channel_id=1, replica_groups=mesh['y'=4,'xh'=2,'core'=2,'z'=4,'xl'=2] {'y','xh','z','xl'}, dimensions={0} | all-to-all | bytes 884736 | tf_op jit(solution)/shard_map/all_to_all | solution.py:236
  131.0 3.0 %collective-permute-start.9 = (bf16[27,64,128]{2,1,0:T(8,128)(2,1)S(1)}, bf16[27,64,128]{2,1,0:T(8,128)(2,1)S(1)}, u32[]{:S(2)}, u32[]{:S(2)}) collective-permute-start(bf16[27,64,128]{2,1,0:T(8,128)(2,1)S(1)} %reshape.43.whole_ref), channel_id=1, source_target_pairs={{0,8},{1,9},{2,10},{3,11},{4,12},{5,13},{6,14},{7,15},{8,0},{9,1},... | collective-permute-start | bytes 1327112 | tf_op jit(solution)/shard_map/ppermute | solution.py:56
  134.0 1.4 %collective-permute-done.9.other_ref = bf16[27,64,128]{2,1,0:T(8,128)(2,1)S(1)} collective-permute-done((bf16[27,64,128]{2,1,0:T(8,128)(2,1)S(1)}, bf16[27,64,128]{2,1,0:T(8,128)(2,1)S(1)}, u32[]{:S(2)}, u32[]{:S(2)}) %collective-permute-start.9) | collective-permute-done | bytes 442400 | tf_op jit(solution)/shard_map/ppermute | solution.py:56
  135.5 1.4 %finish.1 = f32[27,128,128]{2,1,0:T(8,128)} custom-call(s32[1]{0:T(128)} %bitcast.10.core_ref, bf16[27,64,128]{2,1,0:T(8,128)(2,1)S(1)} %reshape.43.whole_ref, bf16[27,64,128]{2,1,0:T(8,128)(2,1)S(1)} %collective-permute-done.9.other_ref), custom_call_target="tpu_custom_call" | custom-call | flops 1000000 | bytes 1000000 | tf_op jit(solution)/shard_map/finish/pallas_call | solution.py:70
  (32 shorter events, 2.2 us)
Async XLA Ops:
  0.6 2.0 %copy-start.2 = (bf16[32,64,128]{2,1,0:T(8,128)(2,1)S(1)}, bf16[32,64,128]{2,1,0:T(8,128)(2,1)}, u32[]{:S(2)}) copy-start(bf16[32,64,128]{2,1,0:T(8,128)(2,1)} %cotangent_hbm.1) | copy-start | bytes 1572868
  2.6 58.3 %copy-start = (bf16[2,32,64,128]{3,2,1,0:T(8,128)(2,1)}, bf16[2,32,64,128]{3,2,1,0:T(8,128)(2,1)S(1)}, u32[]{:S(2)}) copy-start(bf16[2,32,64,128]{3,2,1,0:T(8,128)(2,1)S(1)} %fusion.own_ref.own_hbm) | copy-start | bytes 3145732
  2.6 11.7 %copy-start.7 = (bf16[3,32,64,128]{3,2,1,0:T(8,128)(2,1)S(1)}, bf16[3,32,64,128]{3,2,1,0:T(8,128)(2,1)}, u32[]{:S(2)}) copy-start(bf16[3,32,64,128]{3,2,1,0:T(8,128)(2,1)} %param.5) | copy-start | bytes 4718596
  3.0 11.4 %copy-start.6 = (s32[3,32,64,128]{3,2,1,0:T(8,128)S(1)}, s32[3,32,64,128]{3,2,1,0:T(8,128)}, u32[]{:S(2)}) copy-start(s32[3,32,64,128]{3,2,1,0:T(8,128)} %param.6) | copy-start | bytes 9437188
  4.2 18.1 %collective-permute-start = (bf16[3,32,32,128]{3,1,2,0:T(8,128)(2,1)}, bf16[3,32,32,128]{3,1,2,0:T(8,128)(2,1)}, u32[]{:S(2)}, u32[]{:S(2)}) collective-permute-start(bf16[3,32,32,128]{3,1,2,0:T(8,128)(2,1)} %copy.11), channel_id=1, source_target_pairs={{0,0},{1,16},{2,32},{3,48},{4,38},{5,54},{6,96},{7,112},{8,8},{9,2... | collective-permute-start | bytes 2359304 | tf_op jit(solution)/shard_map/ppermute | solution.py:56
  13.0 11.6 %collective-permute-start.2 = (bf16[3,32,32,128]{3,1,2,0:T(8,128)(2,1)}, bf16[3,32,32,128]{3,1,2,0:T(8,128)(2,1)}, u32[]{:S(2)}, u32[]{:S(2)}) collective-permute-start(bf16[3,32,32,128]{3,1,2,0:T(8,128)(2,1)} %copy.12), channel_id=1, source_target_pairs={{0,8},{1,24},{2,40},{3,56},{4,38},{5,54},{6,104},{7,120},{8,0},{9,... | collective-permute-start | bytes 2359304 | tf_op jit(solution)/shard_map/ppermute | solution.py:56
  22.4 2.9 %collective-permute-start.1 = (bf16[3,32,32,128]{3,1,2,0:T(8,128)(2,1)}, bf16[3,32,32,128]{3,1,2,0:T(8,128)(2,1)S(1)}, u32[]{:S(2)}, u32[]{:S(2)}) collective-permute-start(bf16[3,32,32,128]{3,1,2,0:T(8,128)(2,1)} %collective-permute-done), channel_id=1, source_target_pairs={{38,64},{54,80},{106,72},{107,88},{39,65},{55,81},{122,73},{123,89... | collective-permute-start | bytes 2359304 | tf_op jit(solution)/shard_map/ppermute | solution.py:56
  24.5 2.6 %collective-permute-start.3 = (bf16[3,32,32,128]{3,1,2,0:T(8,128)(2,1)}, bf16[3,32,32,128]{3,1,2,0:T(8,128)(2,1)S(1)}, u32[]{:S(2)}, u32[]{:S(2)}) collective-permute-start(bf16[3,32,32,128]{3,1,2,0:T(8,128)(2,1)} %collective-permute-done.2), channel_id=1, source_target_pairs={{38,72},{54,88},{106,64},{107,80},{39,73},{55,89},{122,65},{123,81... | collective-permute-start | bytes 2359304 | tf_op jit(solution)/shard_map/ppermute | solution.py:56
  28.5 32.4 %copy-start.1 = (bf16[3,32,64,128]{3,2,1,0:T(8,128)(2,1)}, bf16[3,32,64,128]{3,2,1,0:T(8,128)(2,1)S(1)}, u32[]{:S(2)}) copy-start(bf16[3,32,64,128]{3,2,1,0:T(8,128)(2,1)S(1)} %bitcast_dynamic-update-slice_fusion.flip_ref.flip_hbm) | copy-start | bytes 4718596
  28.8 32.3 %copy-start.3 = (bf16[32,64,128]{2,1,0:T(8,128)(2,1)}, bf16[32,64,128]{2,1,0:T(8,128)(2,1)S(1)}, u32[]{:S(2)}) copy-start(bf16[32,64,128]{2,1,0:T(8,128)(2,1)S(1)} %get-tuple-element.15.sym_ref) | copy-start | bytes 1572868
  28.9 26.2 %collective-permute-start.4 = (bf16[15,64,128]{2,1,0:T(8,128)(2,1)S(1)}, bf16[15,64,128]{2,1,0:T(8,128)(2,1)S(1)}, u32[]{:S(2)}, u32[]{:S(2)}) collective-permute-start(bf16[15,64,128]{2,1,0:T(8,128)(2,1)S(1)} %get-tuple-element.16), channel_id=1, source_target_pairs={{0,8},{1,9},{2,10},{3,11},{4,12},{5,13},{6,14},{7,15},{8,16},{9,17... | collective-permute-start | bytes 737288 | tf_op jit(solution)/shard_map/ppermute | solution.py:56
  51.9 9.0 %collective-permute-start.5 = (bf16[15,64,128]{2,1,0:T(8,128)(2,1)S(1)}, bf16[15,64,128]{2,1,0:T(8,128)(2,1)S(1)}, u32[]{:S(2)}, u32[]{:S(2)}) collective-permute-start(bf16[15,64,128]{2,1,0:T(8,128)(2,1)S(1)} %get-tuple-element.17), channel_id=1, source_target_pairs={{8,0},{9,1},{10,2},{11,3},{12,4},{13,5},{14,6},{15,7},{16,8},{17,9... | collective-permute-start | bytes 737288 | tf_op jit(solution)/shard_map/ppermute | solution.py:56
  55.0 6.1 %copy-start.4 = (bf16[15,64,128]{2,1,0:T(8,128)(2,1)}, bf16[15,64,128]{2,1,0:T(8,128)(2,1)S(1)}, u32[]{:S(2)}) copy-start(bf16[15,64,128]{2,1,0:T(8,128)(2,1)S(1)} %collective-permute-done.4.low_ref) | copy-start | bytes 737284
  60.9 0.7 copy-start.5
  61.7 5.9 %collective-permute-start.6 = (bf16[48,16,128]{2,1,0:T(8,128)(2,1)S(1)}, bf16[48,16,128]{2,1,0:T(8,128)(2,1)S(1)}, u32[]{:S(2)}, u32[]{:S(2)}) collective-permute-start(bf16[48,16,128]{2,1,0:T(8,128)(2,1)S(1)} %get-tuple-element.18), channel_id=1, source_target_pairs={{0,1},{1,2},{2,3},{3,4},{4,5},{5,6},{6,7},{8,9},{9,10},{10,11},{11... | collective-permute-start | bytes 589832 | tf_op jit(solution)/shard_map/ppermute | solution.py:56
  65.0 8.3 %collective-permute-start.7 = (bf16[48,16,128]{2,1,0:T(8,128)(2,1)S(1)}, bf16[48,16,128]{2,1,0:T(8,128)(2,1)S(1)}, u32[]{:S(2)}, u32[]{:S(2)}) collective-permute-start(bf16[48,16,128]{2,1,0:T(8,128)(2,1)S(1)} %get-tuple-element.19), channel_id=1, source_target_pairs={{1,0},{2,1},{3,2},{4,3},{5,4},{6,5},{7,6},{9,8},{10,9},{11,10},{12... | collective-permute-start | bytes 589832 | tf_op jit(solution)/shard_map/ppermute | solution.py:56
  67.6 5.7 %copy-start.8 = (bf16[48,16,128]{2,1,0:T(8,128)(2,1)}, bf16[48,16,128]{2,1,0:T(8,128)(2,1)S(1)}, u32[]{:S(2)}) copy-start(bf16[48,16,128]{2,1,0:T(8,128)(2,1)S(1)} %collective-permute-done.6.left_ref) | copy-start | bytes 589828
  73.3 0.7 copy-start.9
  86.7 2.1 %collective-permute-start.8 = (bf16[27,64,128]{2,1,0:T(8,128)(2,1)}, bf16[27,64,128]{2,1,0:T(8,128)(2,1)S(1)}, u32[]{:S(2)}, u32[]{:S(2)}) collective-permute-start(bf16[27,64,128]{2,1,0:T(8,128)(2,1)} %bitcast.28), channel_id=1, source_target_pairs={{0,8},{1,9},{2,10},{3,11},{4,12},{5,13},{6,14},{7,15},{8,0},{9,1},... | collective-permute-start | bytes 1327112 | tf_op jit(solution)/shard_map/ppermute | solution.py:56
  131.0 4.4 %collective-permute-start.9 = (bf16[27,64,128]{2,1,0:T(8,128)(2,1)S(1)}, bf16[27,64,128]{2,1,0:T(8,128)(2,1)S(1)}, u32[]{:S(2)}, u32[]{:S(2)}) collective-permute-start(bf16[27,64,128]{2,1,0:T(8,128)(2,1)S(1)} %reshape.43.whole_ref), channel_id=1, source_target_pairs={{0,8},{1,9},{2,10},{3,11},{4,12},{5,13},{6,14},{7,15},{8,0},{9,1},... | collective-permute-start | bytes 1327112 | tf_op jit(solution)/shard_map/ppermute | solution.py:56

commit v7 on v6

--- a/solution.py
+++ b/solution.py
@@ -229,11 +229,13 @@
 
 
 def total(keep, send, core):
-    part = (keep + shift(send, core_swap()).astype(F32)).astype(BF).reshape(64, -1, 128)
+    flat = (keep + shift(send, core_swap()).astype(F32)).astype(BF).reshape(-1, 128)
+    count = flat.shape[0]
+    part = jnp.pad(flat, ((0, 2048 - count), (0, 0))).reshape(64, 32, 128)
     terms = lax.all_to_all(part, CHIPS, 0, 0, tiled=True)
     mine = jnp.sum(terms.astype(F32), axis=0).astype(BF)
     copies = jnp.broadcast_to(mine[None], terms.shape)
-    whole = lax.all_to_all(copies, CHIPS, 0, 0, tiled=True).reshape(keep.shape)
+    whole = lax.all_to_all(copies, CHIPS, 0, 0, tiled=True).reshape(2048, 128)[:count].reshape(keep.shape)
     other = shift(whole, core_swap())
     out = jax.ShapeDtypeStruct((keep.shape[0], 128, 128), F32)
     return call(finish_kernel, "finish", out, core, whole, other)
@@ -287,7 +289,7 @@
             pltpu.SemaphoreType.DMA((12,)),
         ],
         far=6,
-        flops=8 * 10**9, moved=2 * 10**7, room=60,
+        flops=8 * 10**9, moved=2 * 10**7, room=42,
     )
     sums = total(keep.reshape(27, 64, 128), send.reshape(27, 64, 128), core)
     return gradient, sums.reshape(3, 9, 128, 128)

time: 138 us -> 135 us (0.978)
  other arithmetic: 10.6 us -> 8.2 us
  starting transfers between devices: 43.2 us -> 45.5 us
  local copies, waits for them, and re-layouts: 9.79 us -> 8.34 us
    ppermute x10, starting transfers between devices: 43.2 us -> 45.5 us  [shift(): return lax.ppermute(x, NAMES, pairs)]
  transfers between devices with their start and end apart: 10 -> 10, of which waited for: 6 -> 6; matrix products, arithmetic and copies ran while one was open for 9% -> 8% of each run, Pallas kernels for 0% -> 0%
where the time goes in v7:
time: 135 us; the launch traced here: 134 us
  starting transfers between devices  45.5 us (34%)
  blocking collectives  40.4 us (30%)
  waiting for transfers between devices  17.1 us (13%)
  Pallas kernels  13.7 us (10%)
  local copies, waits for them, and re-layouts  8.34 us (6%)
  other arithmetic  8.2 us (6%)
    ppermute x10, starting transfers between devices, shift(): return lax.ppermute(x, NAMES, pairs)  45.5 us
    all_to_all x1, blocking collectives, total(): terms = lax.all_to_all(part, CHIPS, 0, 0, tiled=True)  24.6 us
    ppermute x10, waiting for transfers between devices, shift(): return lax.ppermute(x, NAMES, pairs)  17.1 us
    all_to_all x1, blocking collectives, total(): lax.all_to_all(copies, CHIPS, 0, 0, tiled=True).reshape(2048, 128)[:count]  15.8 us
    pallas_call x4, Pallas kernels, call(): pl.pallas_call(body, out_shape=out_shape, in_specs=[pl.BlockSpec(memory_s...  13.7 us
  transfers between devices with their start and end apart: 10, of which 6 were waited for; matrix products, arithmetic and copies ran while one was open for 8% of the time, Pallas kernels for 0%

profile of v7, /device:TPU:1, one launch (start us, length us, event | category | flops | bytes accessed | tf_op | source)
XLA Modules:
  0.0 134.1 jit_solution(8252758883902579016)
XLA Ops:
  0.6 2.0 %fusion.own_ref.own_hbm = bf16[2,32,64,128]{3,2,1,0:T(8,128)(2,1)S(1)} fusion(s32[3,32,64,128]{3,2,1,0:T(8,128)} %param.6), kind=kLoop, calls=%fused_computation.2 | loop fusion | flops 1048576 | bytes 3145728 | tf_op jit(solution)/shard_map/convert_element_type | solution.py:246
  2.6 0.4 fusion.3
  3.0 1.2 copy.11
  4.2 7.5 %collective-permute-start = (bf16[3,32,32,128]{3,1,2,0:T(8,128)(2,1)}, bf16[3,32,32,128]{3,1,2,0:T(8,128)(2,1)}, u32[]{:S(2)}, u32[]{:S(2)}) collective-permute-start(bf16[3,32,32,128]{3,1,2,0:T(8,128)(2,1)} %copy.11), channel_id=1, source_target_pairs={{0,0},{1,16},{2,32},{3,48},{4,38},{5,54},{6,96},{7,112},{8,8},{9,2... | collective-permute-start | bytes 2359304 | tf_op jit(solution)/shard_map/ppermute | solution.py:56
  11.8 1.2 copy.12
  12.9 1.4 %collective-permute-start.2 = (bf16[3,32,32,128]{3,1,2,0:T(8,128)(2,1)}, bf16[3,32,32,128]{3,1,2,0:T(8,128)(2,1)}, u32[]{:S(2)}, u32[]{:S(2)}) collective-permute-start(bf16[3,32,32,128]{3,1,2,0:T(8,128)(2,1)} %copy.12), channel_id=1, source_target_pairs={{0,8},{1,24},{2,40},{3,56},{4,38},{5,54},{6,104},{7,120},{8,0},{9,... | collective-permute-start | bytes 2359304 | tf_op jit(solution)/shard_map/ppermute | solution.py:56
  14.4 0.4 compare_select_fusion
  14.7 2.3 %copy.14 = bf16[3,3,3,128,128]{3,4,1,2,0:T(8,128)(2,1)} copy(bf16[3,3,3,128,128]{4,3,2,1,0:T(8,128)(2,1)} %bitcast.35) | data formatting | bytes 1769472 | tf_op jit(solution)/shard_map/reshape | solution.py:259
  17.0 1.6 %copy.13 = bf16[3,2048,128]{1,2,0:T(8,128)(2,1)} copy(bf16[3,2048,128]{2,1,0:T(8,128)(2,1)S(1)} %bitcast.31) | data formatting | bytes 3145728 | tf_op jit(solution)/shard_map/reshape | solution.py:258
  18.6 1.6 %reverse_bitcast_fusion.1 = (bf16[3,3,3,128,128]{4,3,1,2,0:T(8,128)(2,1)S(1)}, bf16[3,3,3,128,128]{4,3,2,1,0:T(8,128)(2,1)S(1)}) fusion(bf16[3,3,3,128,128]{3,4,1,2,0:T(8,128)(2,1)} %copy.14), kind=kLoop, calls=%fused_computation.17 | loop fusion | bytes 2654208 | tf_op jit(solution)/shard_map/transpose | solution.py:259
  20.1 2.2 %fusion.5.mask_hbm = bf16[32,64,128]{2,1,0:T(8,128)(2,1)} fusion(s32[3,32,64,128]{3,2,1,0:T(8,128)} %param.6), kind=kLoop, calls=%fused_computation.18 | loop fusion | flops 524288 | bytes 1572864 | tf_op jit(solution)/shard_map/convert_element_type | solution.py:256
  22.3 1.6 %collective-permute-start.1 = (bf16[3,32,32,128]{3,1,2,0:T(8,128)(2,1)}, bf16[3,32,32,128]{3,1,2,0:T(8,128)(2,1)}, u32[]{:S(2)}, u32[]{:S(2)}) collective-permute-start(bf16[3,32,32,128]{3,1,2,0:T(8,128)(2,1)} %collective-permute-done), channel_id=1, source_target_pairs={{38,64},{54,80},{106,72},{107,88},{39,65},{55,81},{122,73},{123,89... | collective-permute-start | bytes 2359304 | tf_op jit(solution)/shard_map/ppermute | solution.py:56
  24.1 1.6 %collective-permute-start.3 = (bf16[3,32,32,128]{3,1,2,0:T(8,128)(2,1)}, bf16[3,32,32,128]{3,1,2,0:T(8,128)(2,1)}, u32[]{:S(2)}, u32[]{:S(2)}) collective-permute-start(bf16[3,32,32,128]{3,1,2,0:T(8,128)(2,1)} %collective-permute-done.2), channel_id=1, source_target_pairs={{38,72},{54,88},{106,64},{107,80},{39,73},{55,89},{122,65},{123,81... | collective-permute-start | bytes 2359304 | tf_op jit(solution)/shard_map/ppermute | solution.py:56
  25.7 0.4 broadcast.9
  26.1 1.5 %bitcast_dynamic-update-slice_fusion.1 = bf16[3,32,64,128]{3,2,1,0:T(8,128)(2,1)S(1)} fusion(bf16[3,32,64,128]{3,2,1,0:T(8,128)(2,1)S(1)} %broadcast.9, s32[]{:T(128)S(6)} %select_n.35, bf16[3,32,32,128]{3,1,2,0:T(8,128)(2,1)} %collective-permute-done.1, bf16[3,32,32,128]{3,1,2,0:T(8,128)(2,1)} %collective-permute-done, pred[]{:T(512)S(6)} %eq.7), kind=kLoop, calls=%fused_computation.15 | loop fusion | flops 393216 | bytes 2359301 | tf_op jit(solution)/shard_map/dynamic_update_slice | solution.py:264
  27.5 1.4 %bitcast_dynamic-update-slice_fusion.flip_ref.flip_hbm = bf16[3,32,64,128]{3,2,1,0:T(8,128)(2,1)S(1)} fusion(bf16[3,32,64,128]{3,2,1,0:T(8,128)(2,1)S(1)} %bitcast_dynamic-update-slice_fusion.1, s32[]{:T(128)S(6)} %select_n.37, bf16[3,32,32,128]{3,1,2,0:T(8,128)(2,1)} %collective-permute-done.3, bf16[3,32,32,128]{3,1,2,0:T(8,128)(2,1)} %collective-permute-done.2, ...), kind=kLoop, calls=%fused_computation.14 | loop fusion | flops 393216 | bytes 2359301 | tf_op jit(solution)/shard_map/dynamic_update_slice | solution.py:265
  29.0 0.3 symmetric.1
  29.3 23.4 %collective-permute-start.4 = (bf16[15,64,128]{2,1,0:T(8,128)(2,1)S(1)}, bf16[15,64,128]{2,1,0:T(8,128)(2,1)S(1)}, u32[]{:S(2)}, u32[]{:S(2)}) collective-permute-start(bf16[15,64,128]{2,1,0:T(8,128)(2,1)S(1)} %get-tuple-element.16), channel_id=1, source_target_pairs={{0,8},{1,9},{2,10},{3,11},{4,12},{5,13},{6,14},{7,15},{8,16},{9,17... | collective-permute-start | bytes 737288 | tf_op jit(solution)/shard_map/ppermute | solution.py:56
  52.7 1.9 %collective-permute-start.5 = (bf16[15,64,128]{2,1,0:T(8,128)(2,1)S(1)}, bf16[15,64,128]{2,1,0:T(8,128)(2,1)S(1)}, u32[]{:S(2)}, u32[]{:S(2)}) collective-permute-start(bf16[15,64,128]{2,1,0:T(8,128)(2,1)S(1)} %get-tuple-element.17), channel_id=1, source_target_pairs={{8,0},{9,1},{10,2},{11,3},{12,4},{13,5},{14,6},{15,7},{16,8},{17,9... | collective-permute-start | bytes 737288 | tf_op jit(solution)/shard_map/ppermute | solution.py:56
  54.7 1.2 collective-permute-done.4.low_ref
  55.9 5.9 %collective-permute-done.5.high_ref = bf16[15,64,128]{2,1,0:T(8,128)(2,1)S(1)} collective-permute-done((bf16[15,64,128]{2,1,0:T(8,128)(2,1)S(1)}, bf16[15,64,128]{2,1,0:T(8,128)(2,1)S(1)}, u32[]{:S(2)}, u32[]{:S(2)}) %collective-permute-start.5) | collective-permute-done | bytes 245792 | tf_op jit(solution)/shard_map/ppermute | solution.py:56
  62.0 3.5 %collective-permute-start.6 = (bf16[48,16,128]{2,1,0:T(8,128)(2,1)S(1)}, bf16[48,16,128]{2,1,0:T(8,128)(2,1)S(1)}, u32[]{:S(2)}, u32[]{:S(2)}) collective-permute-start(bf16[48,16,128]{2,1,0:T(8,128)(2,1)S(1)} %get-tuple-element.18), channel_id=1, source_target_pairs={{0,1},{1,2},{2,3},{3,4},{4,5},{5,6},{6,7},{8,9},{9,10},{10,11},{11... | collective-permute-start | bytes 589832 | tf_op jit(solution)/shard_map/ppermute | solution.py:56
  65.4 1.5 %collective-permute-start.7 = (bf16[48,16,128]{2,1,0:T(8,128)(2,1)S(1)}, bf16[48,16,128]{2,1,0:T(8,128)(2,1)S(1)}, u32[]{:S(2)}, u32[]{:S(2)}) collective-permute-start(bf16[48,16,128]{2,1,0:T(8,128)(2,1)S(1)} %get-tuple-element.19), channel_id=1, source_target_pairs={{1,0},{2,1},{3,2},{4,3},{5,4},{6,5},{7,6},{9,8},{10,9},{11,10},{12... | collective-permute-start | bytes 589832 | tf_op jit(solution)/shard_map/ppermute | solution.py:56
  66.9 1.1 collective-permute-done.6.left_ref
  68.0 5.7 %collective-permute-done.7.right_ref = bf16[48,16,128]{2,1,0:T(8,128)(2,1)S(1)} collective-permute-done((bf16[48,16,128]{2,1,0:T(8,128)(2,1)S(1)}, bf16[48,16,128]{2,1,0:T(8,128)(2,1)S(1)}, u32[]{:S(2)}, u32[]{:S(2)}) %collective-permute-start.7) | collective-permute-done | bytes 196640 | tf_op jit(solution)/shard_map/ppermute | solution.py:56
  73.8 11.8 %blocks.1 = (bf16[32,64,128]{2,1,0:T(8,128)(2,1)}, f32[3,9,64,128]{3,2,1,0:T(8,128)S(1)}, bf16[3,9,64,128]{3,2,1,0:T(8,128)(2,1)S(1)}) custom-call(bf16[32,64,128]{2,1,0:T(8,128)(2,1)S(1)} %get-tuple-element.15.sym_ref, bf16[15,64,128]{2,1,0:T(8,128)(2,1)S(1)} %collective-permute-done.4.low_ref, bf16[15,64,128]{2,1,0:T(8,128)(2,1)S(1)} %collective-permute-done.5.high_ref, ...), custom_call_target="tpu_custom_call" | custom-call | flops 8000000000 | bytes 20000000 | tf_op jit(solution)/shard_map/blocks/pallas_call | solution.py:70
  85.6 1.8 %collective-permute-done.8 = bf16[27,64,128]{2,1,0:T(8,128)(2,1)S(1)} collective-permute-done((bf16[27,64,128]{2,1,0:T(8,128)(2,1)S(1)}, bf16[27,64,128]{2,1,0:T(8,128)(2,1)S(1)}, u32[]{:S(2)}, u32[]{:S(2)}) %collective-permute-start.8) | collective-permute-done | bytes 442400 | tf_op jit(solution)/shard_map/ppermute | solution.py:56
  87.6 24.6 %all_to_all.10 = bf16[64,32,128]{2,1,0:T(8,128)(2,1)S(1)} all-to-all(bf16[64,32,128]{2,1,0:T(8,128)(2,1)S(1)} %bitcast.32), channel_id=1, replica_groups=mesh['y'=4,'xh'=2,'core'=2,'z'=4,'xl'=2] {'y','xh','z','xl'}, dimensions={0} | all-to-all | bytes 1048576 | tf_op jit(solution)/shard_map/all_to_all | solution.py:235
  112.4 15.8 %all_to_all.11 = bf16[64,32,128]{2,1,0:T(8,128)(2,1)S(1)} all-to-all(bf16[64,32,128]{2,1,0:T(8,128)(2,1)S(1)} %broadcast_in_dim.10), channel_id=1, replica_groups=mesh['y'=4,'xh'=2,'core'=2,'z'=4,'xl'=2] {'y','xh','z','xl'}, dimensions={0} | all-to-all | bytes 1048576 | tf_op jit(solution)/shard_map/all_to_all | solution.py:238
  128.2 3.0 %collective-permute-start.9 = (bf16[27,64,128]{2,1,0:T(8,128)(2,1)S(1)}, bf16[27,64,128]{2,1,0:T(8,128)(2,1)S(1)}, u32[]{:S(2)}, u32[]{:S(2)}) collective-permute-start(bf16[27,64,128]{2,1,0:T(8,128)(2,1)S(1)} %bitcast.27), channel_id=1, source_target_pairs={{0,8},{1,9},{2,10},{3,11},{4,12},{5,13},{6,14},{7,15},{8,0},{9,1},... | collective-permute-start | bytes 1327112 | tf_op jit(solution)/shard_map/ppermute | solution.py:56
  131.2 1.4 %collective-permute-done.9.other_ref = bf16[27,64,128]{2,1,0:T(8,128)(2,1)S(1)} collective-permute-done((bf16[27,64,128]{2,1,0:T(8,128)(2,1)S(1)}, bf16[27,64,128]{2,1,0:T(8,128)(2,1)S(1)}, u32[]{:S(2)}, u32[]{:S(2)}) %collective-permute-start.9) | collective-permute-done | bytes 442400 | tf_op jit(solution)/shard_map/ppermute | solution.py:56
  132.6 1.4 %finish.1 = f32[27,128,128]{2,1,0:T(8,128)} custom-call(s32[1]{0:T(128)} %bitcast.10.core_ref, bf16[27,64,128]{2,1,0:T(8,128)(2,1)S(1)} %bitcast.28, bf16[27,64,128]{2,1,0:T(8,128)(2,1)S(1)} %collective-permute-done.9.other_ref), custom_call_target="tpu_custom_call" | custom-call | flops 1000000 | bytes 1000000 | tf_op jit(solution)/shard_map/finish/pallas_call | solution.py:70
  (22 shorter events, 0.9 us)
Async XLA Ops:
  0.6 2.0 %copy-start = (bf16[32,64,128]{2,1,0:T(8,128)(2,1)S(1)}, bf16[32,64,128]{2,1,0:T(8,128)(2,1)}, u32[]{:S(2)}) copy-start(bf16[32,64,128]{2,1,0:T(8,128)(2,1)} %cotangent_hbm.1) | copy-start | bytes 1572868
  2.6 11.7 %copy-start.4 = (bf16[3,32,64,128]{3,2,1,0:T(8,128)(2,1)S(1)}, bf16[3,32,64,128]{3,2,1,0:T(8,128)(2,1)}, u32[]{:S(2)}) copy-start(bf16[3,32,64,128]{3,2,1,0:T(8,128)(2,1)} %param.5) | copy-start | bytes 4718596
  3.0 11.4 %copy-start.3 = (s32[3,32,64,128]{3,2,1,0:T(8,128)S(1)}, s32[3,32,64,128]{3,2,1,0:T(8,128)}, u32[]{:S(2)}) copy-start(s32[3,32,64,128]{3,2,1,0:T(8,128)} %param.6) | copy-start | bytes 9437188
  4.2 18.1 %collective-permute-start = (bf16[3,32,32,128]{3,1,2,0:T(8,128)(2,1)}, bf16[3,32,32,128]{3,1,2,0:T(8,128)(2,1)}, u32[]{:S(2)}, u32[]{:S(2)}) collective-permute-start(bf16[3,32,32,128]{3,1,2,0:T(8,128)(2,1)} %copy.11), channel_id=1, source_target_pairs={{0,0},{1,16},{2,32},{3,48},{4,38},{5,54},{6,96},{7,112},{8,8},{9,2... | collective-permute-start | bytes 2359304 | tf_op jit(solution)/shard_map/ppermute | solution.py:56
  12.9 11.2 %collective-permute-start.2 = (bf16[3,32,32,128]{3,1,2,0:T(8,128)(2,1)}, bf16[3,32,32,128]{3,1,2,0:T(8,128)(2,1)}, u32[]{:S(2)}, u32[]{:S(2)}) collective-permute-start(bf16[3,32,32,128]{3,1,2,0:T(8,128)(2,1)} %copy.12), channel_id=1, source_target_pairs={{0,8},{1,24},{2,40},{3,56},{4,38},{5,54},{6,104},{7,120},{8,0},{9,... | collective-permute-start | bytes 2359304 | tf_op jit(solution)/shard_map/ppermute | solution.py:56
  22.3 3.4 %collective-permute-start.1 = (bf16[3,32,32,128]{3,1,2,0:T(8,128)(2,1)}, bf16[3,32,32,128]{3,1,2,0:T(8,128)(2,1)}, u32[]{:S(2)}, u32[]{:S(2)}) collective-permute-start(bf16[3,32,32,128]{3,1,2,0:T(8,128)(2,1)} %collective-permute-done), channel_id=1, source_target_pairs={{38,64},{54,80},{106,72},{107,88},{39,65},{55,81},{122,73},{123,89... | collective-permute-start | bytes 2359304 | tf_op jit(solution)/shard_map/ppermute | solution.py:56
  24.1 3.4 %collective-permute-start.3 = (bf16[3,32,32,128]{3,1,2,0:T(8,128)(2,1)}, bf16[3,32,32,128]{3,1,2,0:T(8,128)(2,1)}, u32[]{:S(2)}, u32[]{:S(2)}) collective-permute-start(bf16[3,32,32,128]{3,1,2,0:T(8,128)(2,1)} %collective-permute-done.2), channel_id=1, source_target_pairs={{38,72},{54,88},{106,64},{107,80},{39,73},{55,89},{122,65},{123,81... | collective-permute-start | bytes 2359304 | tf_op jit(solution)/shard_map/ppermute | solution.py:56
  29.3 26.6 %collective-permute-start.4 = (bf16[15,64,128]{2,1,0:T(8,128)(2,1)S(1)}, bf16[15,64,128]{2,1,0:T(8,128)(2,1)S(1)}, u32[]{:S(2)}, u32[]{:S(2)}) collective-permute-start(bf16[15,64,128]{2,1,0:T(8,128)(2,1)S(1)} %get-tuple-element.16), channel_id=1, source_target_pairs={{0,8},{1,9},{2,10},{3,11},{4,12},{5,13},{6,14},{7,15},{8,16},{9,17... | collective-permute-start | bytes 737288 | tf_op jit(solution)/shard_map/ppermute | solution.py:56
  52.7 9.0 %collective-permute-start.5 = (bf16[15,64,128]{2,1,0:T(8,128)(2,1)S(1)}, bf16[15,64,128]{2,1,0:T(8,128)(2,1)S(1)}, u32[]{:S(2)}, u32[]{:S(2)}) collective-permute-start(bf16[15,64,128]{2,1,0:T(8,128)(2,1)S(1)} %get-tuple-element.17), channel_id=1, source_target_pairs={{8,0},{9,1},{10,2},{11,3},{12,4},{13,5},{14,6},{15,7},{16,8},{17,9... | collective-permute-start | bytes 737288 | tf_op jit(solution)/shard_map/ppermute | solution.py:56
  61.8 12.0 %copy-start.1 = (bf16[3,2048,128]{1,2,0:T(8,128)(2,1)S(1)}, bf16[3,2048,128]{1,2,0:T(8,128)(2,1)}, u32[]{:S(2)}) copy-start(bf16[3,2048,128]{1,2,0:T(8,128)(2,1)} %copy.13) | copy-start | bytes 4718596
  61.8 12.0 %copy-start.2 = (bf16[32,64,128]{2,1,0:T(8,128)(2,1)S(1)}, bf16[32,64,128]{2,1,0:T(8,128)(2,1)}, u32[]{:S(2)}) copy-start(bf16[32,64,128]{2,1,0:T(8,128)(2,1)} %fusion.5.mask_hbm) | copy-start | bytes 1572868
  62.0 6.1 %collective-permute-start.6 = (bf16[48,16,128]{2,1,0:T(8,128)(2,1)S(1)}, bf16[48,16,128]{2,1,0:T(8,128)(2,1)S(1)}, u32[]{:S(2)}, u32[]{:S(2)}) collective-permute-start(bf16[48,16,128]{2,1,0:T(8,128)(2,1)S(1)} %get-tuple-element.18), channel_id=1, source_target_pairs={{0,1},{1,2},{2,3},{3,4},{4,5},{5,6},{6,7},{8,9},{9,10},{10,11},{11... | collective-permute-start | bytes 589832 | tf_op jit(solution)/shard_map/ppermute | solution.py:56
  65.4 8.3 %collective-permute-start.7 = (bf16[48,16,128]{2,1,0:T(8,128)(2,1)S(1)}, bf16[48,16,128]{2,1,0:T(8,128)(2,1)S(1)}, u32[]{:S(2)}, u32[]{:S(2)}) collective-permute-start(bf16[48,16,128]{2,1,0:T(8,128)(2,1)S(1)} %get-tuple-element.19), channel_id=1, source_target_pairs={{1,0},{2,1},{3,2},{4,3},{5,4},{6,5},{7,6},{9,8},{10,9},{11,10},{12... | collective-permute-start | bytes 589832 | tf_op jit(solution)/shard_map/ppermute | solution.py:56
  85.6 1.9 %collective-permute-start.8 = (bf16[27,64,128]{2,1,0:T(8,128)(2,1)S(1)}, bf16[27,64,128]{2,1,0:T(8,128)(2,1)S(1)}, u32[]{:S(2)}, u32[]{:S(2)}) collective-permute-start(bf16[27,64,128]{2,1,0:T(8,128)(2,1)S(1)} %bitcast.30), channel_id=1, source_target_pairs={{0,8},{1,9},{2,10},{3,11},{4,12},{5,13},{6,14},{7,15},{8,0},{9,1},... | collective-permute-start | bytes 1327112 | tf_op jit(solution)/shard_map/ppermute | solution.py:56
  128.2 4.4 %collective-permute-start.9 = (bf16[27,64,128]{2,1,0:T(8,128)(2,1)S(1)}, bf16[27,64,128]{2,1,0:T(8,128)(2,1)S(1)}, u32[]{:S(2)}, u32[]{:S(2)}) collective-permute-start(bf16[27,64,128]{2,1,0:T(8,128)(2,1)S(1)} %bitcast.27), channel_id=1, source_target_pairs={{0,8},{1,9},{2,10},{3,11},{4,12},{5,13},{6,14},{7,15},{8,0},{9,1},... | collective-permute-start | bytes 1327112 | tf_op jit(solution)/shard_map/ppermute | solution.py:56

commit v8 on v7

--- a/solution.py
+++ b/solution.py
@@ -260,7 +260,7 @@
     both = jnp.concatenate([kernels, kernels.swapaxes(1, 2)], axis=-1).reshape(3, -1, 2 * channels)
     direct2, bottom, inputs, both = lax.optimization_barrier((direct2, bottom, inputs, both))
 
-    flip = jnp.zeros_like(stack)
+    flip = stack
     flip = lax.dynamic_update_slice_in_dim(flip, turn(direct, second), start, axis=2)
     flip = lax.dynamic_update_slice_in_dim(flip, turn(direct2, second2), start2, axis=2)
     tile = jax.ShapeDtypeStruct((32, 64, 128), BF)

time: 135 us -> 135 us (level)
  no operation moved by 1% of the time
where the time goes in v8:
time: 135 us; the launch traced here: 134 us
  starting transfers between devices  45.5 us (34%)
  blocking collectives  40.4 us (30%)
  waiting for transfers between devices  17.1 us (13%)
  Pallas kernels  13.7 us (10%)
  other arithmetic  8.34 us (6%)
  local copies, waits for them, and re-layouts  7.96 us (6%)
    ppermute x10, starting transfers between devices, shift(): return lax.ppermute(x, NAMES, pairs)  45.5 us
    all_to_all x1, blocking collectives, total(): terms = lax.all_to_all(part, CHIPS, 0, 0, tiled=True)  24.6 us
    ppermute x10, waiting for transfers between devices, shift(): return lax.ppermute(x, NAMES, pairs)  17.1 us
    all_to_all x1, blocking collectives, total(): lax.all_to_all(copies, CHIPS, 0, 0, tiled=True).reshape(2048, 128)[:count]  15.8 us
    pallas_call x4, Pallas kernels, call(): pl.pallas_call(body, out_shape=out_shape, in_specs=[pl.BlockSpec(memory_s...  13.7 us
  transfers between devices with their start and end apart: 10, of which 6 were waited for; matrix products, arithmetic and copies ran while one was open for 8% of the time, Pallas kernels for 0%

profile of v8, /device:TPU:1, one launch (start us, length us, event | category | flops | bytes accessed | tf_op | source)
XLA Modules:
  0.0 133.8 jit_solution(7239539087826016591)
XLA Ops:
  0.6 2.0 %fusion.own_ref.own_hbm = bf16[2,32,64,128]{3,2,1,0:T(8,128)(2,1)S(1)} fusion(s32[3,32,64,128]{3,2,1,0:T(8,128)} %param.6), kind=kLoop, calls=%fused_computation.5 | loop fusion | flops 1048576 | bytes 3145728 | tf_op jit(solution)/shard_map/convert_element_type | solution.py:246
  2.6 0.4 fusion.4
  3.0 1.2 copy.11
  4.2 7.5 %collective-permute-start = (bf16[3,32,32,128]{3,1,2,0:T(8,128)(2,1)}, bf16[3,32,32,128]{3,1,2,0:T(8,128)(2,1)}, u32[]{:S(2)}, u32[]{:S(2)}) collective-permute-start(bf16[3,32,32,128]{3,1,2,0:T(8,128)(2,1)} %copy.11), channel_id=1, source_target_pairs={{0,0},{1,16},{2,32},{3,48},{4,38},{5,54},{6,96},{7,112},{8,8},{9,2... | collective-permute-start | bytes 2359304 | tf_op jit(solution)/shard_map/ppermute | solution.py:56
  11.8 1.2 copy.12
  12.9 1.4 %collective-permute-start.2 = (bf16[3,32,32,128]{3,1,2,0:T(8,128)(2,1)}, bf16[3,32,32,128]{3,1,2,0:T(8,128)(2,1)}, u32[]{:S(2)}, u32[]{:S(2)}) collective-permute-start(bf16[3,32,32,128]{3,1,2,0:T(8,128)(2,1)} %copy.12), channel_id=1, source_target_pairs={{0,8},{1,24},{2,40},{3,56},{4,38},{5,54},{6,104},{7,120},{8,0},{9,... | collective-permute-start | bytes 2359304 | tf_op jit(solution)/shard_map/ppermute | solution.py:56
  14.4 0.4 compare_select_fusion
  14.7 2.3 %copy.14 = bf16[3,3,3,128,128]{3,4,1,2,0:T(8,128)(2,1)} copy(bf16[3,3,3,128,128]{4,3,2,1,0:T(8,128)(2,1)} %bitcast.36) | data formatting | bytes 1769472 | tf_op jit(solution)/shard_map/reshape | solution.py:259
  17.0 1.6 %copy.13 = bf16[3,2048,128]{1,2,0:T(8,128)(2,1)} copy(bf16[3,2048,128]{2,1,0:T(8,128)(2,1)S(1)} %bitcast.32) | data formatting | bytes 3145728 | tf_op jit(solution)/shard_map/reshape | solution.py:258
  18.6 1.6 %reverse_bitcast_fusion.1 = (bf16[3,3,3,128,128]{4,3,1,2,0:T(8,128)(2,1)S(1)}, bf16[3,3,3,128,128]{4,3,2,1,0:T(8,128)(2,1)S(1)}) fusion(bf16[3,3,3,128,128]{3,4,1,2,0:T(8,128)(2,1)} %copy.14), kind=kLoop, calls=%fused_computation.18 | loop fusion | bytes 2654208 | tf_op jit(solution)/shard_map/transpose | solution.py:259
  20.1 2.2 %fusion.5.mask_hbm = bf16[32,64,128]{2,1,0:T(8,128)(2,1)} fusion(s32[3,32,64,128]{3,2,1,0:T(8,128)} %param.6), kind=kLoop, calls=%fused_computation.19 | loop fusion | flops 524288 | bytes 1572864 | tf_op jit(solution)/shard_map/convert_element_type | solution.py:256
  22.3 1.6 %collective-permute-start.1 = (bf16[3,32,32,128]{3,1,2,0:T(8,128)(2,1)}, bf16[3,32,32,128]{3,1,2,0:T(8,128)(2,1)}, u32[]{:S(2)}, u32[]{:S(2)}) collective-permute-start(bf16[3,32,32,128]{3,1,2,0:T(8,128)(2,1)} %collective-permute-done), channel_id=1, source_target_pairs={{38,64},{54,80},{106,72},{107,88},{39,65},{55,81},{122,73},{123,89... | collective-permute-start | bytes 2359304 | tf_op jit(solution)/shard_map/ppermute | solution.py:56
  23.9 0.2 pad_maximum_fusion.1
  24.1 1.6 %collective-permute-start.3 = (bf16[3,32,32,128]{3,1,2,0:T(8,128)(2,1)}, bf16[3,32,32,128]{3,1,2,0:T(8,128)(2,1)}, u32[]{:S(2)}, u32[]{:S(2)}) collective-permute-start(bf16[3,32,32,128]{3,1,2,0:T(8,128)(2,1)} %collective-permute-done.2), channel_id=1, source_target_pairs={{38,72},{54,88},{106,64},{107,80},{39,73},{55,89},{122,65},{123,81... | collective-permute-start | bytes 2359304 | tf_op jit(solution)/shard_map/ppermute | solution.py:56
  25.8 1.5 %bitcast_dynamic-update-slice_fusion.1 = bf16[3,32,64,128]{3,2,1,0:T(8,128)(2,1)S(1)} fusion(bf16[3,32,64,128]{3,2,1,0:T(8,128)(2,1)S(1)} %pad_maximum_fusion, s32[]{:T(128)S(6)} %select_n.35, bf16[3,32,32,128]{3,1,2,0:T(8,128)(2,1)} %collective-permute-done.1, bf16[3,32,32,128]{3,1,2,0:T(8,128)(2,1)} %collective-permute-done, pred[]{:T(512)S(6)} %eq.7), kind=kLoop, calls=%fused_computation.16 | loop fusion | flops 393216 | bytes 2359301 | tf_op jit(solution)/shard_map/dynamic_update_slice | solution.py:264
  27.3 1.4 %bitcast_dynamic-update-slice_fusion.flip_ref.flip_hbm = bf16[3,32,64,128]{3,2,1,0:T(8,128)(2,1)S(1)} fusion(bf16[3,32,64,128]{3,2,1,0:T(8,128)(2,1)S(1)} %bitcast_dynamic-update-slice_fusion.1, s32[]{:T(128)S(6)} %select_n.37, bf16[3,32,32,128]{3,1,2,0:T(8,128)(2,1)} %collective-permute-done.3, bf16[3,32,32,128]{3,1,2,0:T(8,128)(2,1)} %collective-permute-done.2, ...), kind=kLoop, calls=%fused_computation.15 | loop fusion | flops 393216 | bytes 2359301 | tf_op jit(solution)/shard_map/dynamic_update_slice | solution.py:265
  28.8 0.3 symmetric.1
  29.1 23.4 %collective-permute-start.4 = (bf16[15,64,128]{2,1,0:T(8,128)(2,1)S(1)}, bf16[15,64,128]{2,1,0:T(8,128)(2,1)S(1)}, u32[]{:S(2)}, u32[]{:S(2)}) collective-permute-start(bf16[15,64,128]{2,1,0:T(8,128)(2,1)S(1)} %get-tuple-element.16), channel_id=1, source_target_pairs={{0,8},{1,9},{2,10},{3,11},{4,12},{5,13},{6,14},{7,15},{8,16},{9,17... | collective-permute-start | bytes 737288 | tf_op jit(solution)/shard_map/ppermute | solution.py:56
  52.5 1.9 %collective-permute-start.5 = (bf16[15,64,128]{2,1,0:T(8,128)(2,1)S(1)}, bf16[15,64,128]{2,1,0:T(8,128)(2,1)S(1)}, u32[]{:S(2)}, u32[]{:S(2)}) collective-permute-start(bf16[15,64,128]{2,1,0:T(8,128)(2,1)S(1)} %get-tuple-element.17), channel_id=1, source_target_pairs={{8,0},{9,1},{10,2},{11,3},{12,4},{13,5},{14,6},{15,7},{16,8},{17,9... | collective-permute-start | bytes 737288 | tf_op jit(solution)/shard_map/ppermute | solution.py:56
  54.4 1.2 collective-permute-done.4.low_ref
  55.6 5.9 %collective-permute-done.5.high_ref = bf16[15,64,128]{2,1,0:T(8,128)(2,1)S(1)} collective-permute-done((bf16[15,64,128]{2,1,0:T(8,128)(2,1)S(1)}, bf16[15,64,128]{2,1,0:T(8,128)(2,1)S(1)}, u32[]{:S(2)}, u32[]{:S(2)}) %collective-permute-start.5) | collective-permute-done | bytes 245792 | tf_op jit(solution)/shard_map/ppermute | solution.py:56
  61.7 3.5 %collective-permute-start.6 = (bf16[48,16,128]{2,1,0:T(8,128)(2,1)S(1)}, bf16[48,16,128]{2,1,0:T(8,128)(2,1)S(1)}, u32[]{:S(2)}, u32[]{:S(2)}) collective-permute-start(bf16[48,16,128]{2,1,0:T(8,128)(2,1)S(1)} %get-tuple-element.18), channel_id=1, source_target_pairs={{0,1},{1,2},{2,3},{3,4},{4,5},{5,6},{6,7},{8,9},{9,10},{10,11},{11... | collective-permute-start | bytes 589832 | tf_op jit(solution)/shard_map/ppermute | solution.py:56
  65.2 1.5 %collective-permute-start.7 = (bf16[48,16,128]{2,1,0:T(8,128)(2,1)S(1)}, bf16[48,16,128]{2,1,0:T(8,128)(2,1)S(1)}, u32[]{:S(2)}, u32[]{:S(2)}) collective-permute-start(bf16[48,16,128]{2,1,0:T(8,128)(2,1)S(1)} %get-tuple-element.19), channel_id=1, source_target_pairs={{1,0},{2,1},{3,2},{4,3},{5,4},{6,5},{7,6},{9,8},{10,9},{11,10},{12... | collective-permute-start | bytes 589832 | tf_op jit(solution)/shard_map/ppermute | solution.py:56
  66.7 1.1 collective-permute-done.6.left_ref
  67.8 5.7 %collective-permute-done.7.right_ref = bf16[48,16,128]{2,1,0:T(8,128)(2,1)S(1)} collective-permute-done((bf16[48,16,128]{2,1,0:T(8,128)(2,1)S(1)}, bf16[48,16,128]{2,1,0:T(8,128)(2,1)S(1)}, u32[]{:S(2)}, u32[]{:S(2)}) %collective-permute-start.7) | collective-permute-done | bytes 196640 | tf_op jit(solution)/shard_map/ppermute | solution.py:56
  73.5 11.8 %blocks.1 = (bf16[32,64,128]{2,1,0:T(8,128)(2,1)}, f32[3,9,64,128]{3,2,1,0:T(8,128)S(1)}, bf16[3,9,64,128]{3,2,1,0:T(8,128)(2,1)S(1)}) custom-call(bf16[32,64,128]{2,1,0:T(8,128)(2,1)S(1)} %get-tuple-element.15.sym_ref, bf16[15,64,128]{2,1,0:T(8,128)(2,1)S(1)} %collective-permute-done.4.low_ref, bf16[15,64,128]{2,1,0:T(8,128)(2,1)S(1)} %collective-permute-done.5.high_ref, ...), custom_call_target="tpu_custom_call" | custom-call | flops 8000000000 | bytes 20000000 | tf_op jit(solution)/shard_map/blocks/pallas_call | solution.py:70
  85.4 1.8 %collective-permute-done.8 = bf16[27,64,128]{2,1,0:T(8,128)(2,1)S(1)} collective-permute-done((bf16[27,64,128]{2,1,0:T(8,128)(2,1)S(1)}, bf16[27,64,128]{2,1,0:T(8,128)(2,1)S(1)}, u32[]{:S(2)}, u32[]{:S(2)}) %collective-permute-start.8) | collective-permute-done | bytes 442400 | tf_op jit(solution)/shard_map/ppermute | solution.py:56
  87.4 24.6 %all_to_all.10 = bf16[64,32,128]{2,1,0:T(8,128)(2,1)S(1)} all-to-all(bf16[64,32,128]{2,1,0:T(8,128)(2,1)S(1)} %bitcast.33), channel_id=1, replica_groups=mesh['y'=4,'xh'=2,'core'=2,'z'=4,'xl'=2] {'y','xh','z','xl'}, dimensions={0} | all-to-all | bytes 1048576 | tf_op jit(solution)/shard_map/all_to_all | solution.py:235
  112.1 15.8 %all_to_all.11 = bf16[64,32,128]{2,1,0:T(8,128)(2,1)S(1)} all-to-all(bf16[64,32,128]{2,1,0:T(8,128)(2,1)S(1)} %broadcast_in_dim.14), channel_id=1, replica_groups=mesh['y'=4,'xh'=2,'core'=2,'z'=4,'xl'=2] {'y','xh','z','xl'}, dimensions={0} | all-to-all | bytes 1048576 | tf_op jit(solution)/shard_map/all_to_all | solution.py:238
  128.0 3.0 %collective-permute-start.9 = (bf16[27,64,128]{2,1,0:T(8,128)(2,1)S(1)}, bf16[27,64,128]{2,1,0:T(8,128)(2,1)S(1)}, u32[]{:S(2)}, u32[]{:S(2)}) collective-permute-start(bf16[27,64,128]{2,1,0:T(8,128)(2,1)S(1)} %bitcast.28), channel_id=1, source_target_pairs={{0,8},{1,9},{2,10},{3,11},{4,12},{5,13},{6,14},{7,15},{8,0},{9,1},... | collective-permute-start | bytes 1327112 | tf_op jit(solution)/shard_map/ppermute | solution.py:56
  131.0 1.4 %collective-permute-done.9.other_ref = bf16[27,64,128]{2,1,0:T(8,128)(2,1)S(1)} collective-permute-done((bf16[27,64,128]{2,1,0:T(8,128)(2,1)S(1)}, bf16[27,64,128]{2,1,0:T(8,128)(2,1)S(1)}, u32[]{:S(2)}, u32[]{:S(2)}) %collective-permute-start.9) | collective-permute-done | bytes 442400 | tf_op jit(solution)/shard_map/ppermute | solution.py:56
  132.4 1.4 %finish.1 = f32[27,128,128]{2,1,0:T(8,128)} custom-call(s32[1]{0:T(128)} %bitcast.10.core_ref, bf16[27,64,128]{2,1,0:T(8,128)(2,1)S(1)} %bitcast.29, bf16[27,64,128]{2,1,0:T(8,128)(2,1)S(1)} %collective-permute-done.9.other_ref), custom_call_target="tpu_custom_call" | custom-call | flops 1000000 | bytes 1000000 | tf_op jit(solution)/shard_map/finish/pallas_call | solution.py:70
  (22 shorter events, 0.8 us)
Async XLA Ops:
  0.6 2.0 %copy-start = (bf16[32,64,128]{2,1,0:T(8,128)(2,1)S(1)}, bf16[32,64,128]{2,1,0:T(8,128)(2,1)}, u32[]{:S(2)}) copy-start(bf16[32,64,128]{2,1,0:T(8,128)(2,1)} %cotangent_hbm.1) | copy-start | bytes 1572868
  2.6 11.7 %copy-start.4 = (bf16[3,32,64,128]{3,2,1,0:T(8,128)(2,1)S(1)}, bf16[3,32,64,128]{3,2,1,0:T(8,128)(2,1)}, u32[]{:S(2)}) copy-start(bf16[3,32,64,128]{3,2,1,0:T(8,128)(2,1)} %param.5) | copy-start | bytes 4718596
  3.0 11.4 %copy-start.3 = (s32[3,32,64,128]{3,2,1,0:T(8,128)S(1)}, s32[3,32,64,128]{3,2,1,0:T(8,128)}, u32[]{:S(2)}) copy-start(s32[3,32,64,128]{3,2,1,0:T(8,128)} %param.6) | copy-start | bytes 9437188
  4.2 18.1 %collective-permute-start = (bf16[3,32,32,128]{3,1,2,0:T(8,128)(2,1)}, bf16[3,32,32,128]{3,1,2,0:T(8,128)(2,1)}, u32[]{:S(2)}, u32[]{:S(2)}) collective-permute-start(bf16[3,32,32,128]{3,1,2,0:T(8,128)(2,1)} %copy.11), channel_id=1, source_target_pairs={{0,0},{1,16},{2,32},{3,48},{4,38},{5,54},{6,96},{7,112},{8,8},{9,2... | collective-permute-start | bytes 2359304 | tf_op jit(solution)/shard_map/ppermute | solution.py:56
  12.9 11.2 %collective-permute-start.2 = (bf16[3,32,32,128]{3,1,2,0:T(8,128)(2,1)}, bf16[3,32,32,128]{3,1,2,0:T(8,128)(2,1)}, u32[]{:S(2)}, u32[]{:S(2)}) collective-permute-start(bf16[3,32,32,128]{3,1,2,0:T(8,128)(2,1)} %copy.12), channel_id=1, source_target_pairs={{0,8},{1,24},{2,40},{3,56},{4,38},{5,54},{6,104},{7,120},{8,0},{9,... | collective-permute-start | bytes 2359304 | tf_op jit(solution)/shard_map/ppermute | solution.py:56
  22.3 3.5 %collective-permute-start.1 = (bf16[3,32,32,128]{3,1,2,0:T(8,128)(2,1)}, bf16[3,32,32,128]{3,1,2,0:T(8,128)(2,1)}, u32[]{:S(2)}, u32[]{:S(2)}) collective-permute-start(bf16[3,32,32,128]{3,1,2,0:T(8,128)(2,1)} %collective-permute-done), channel_id=1, source_target_pairs={{38,64},{54,80},{106,72},{107,88},{39,65},{55,81},{122,73},{123,89... | collective-permute-start | bytes 2359304 | tf_op jit(solution)/shard_map/ppermute | solution.py:56
  24.1 3.2 %collective-permute-start.3 = (bf16[3,32,32,128]{3,1,2,0:T(8,128)(2,1)}, bf16[3,32,32,128]{3,1,2,0:T(8,128)(2,1)}, u32[]{:S(2)}, u32[]{:S(2)}) collective-permute-start(bf16[3,32,32,128]{3,1,2,0:T(8,128)(2,1)} %collective-permute-done.2), channel_id=1, source_target_pairs={{38,72},{54,88},{106,64},{107,80},{39,73},{55,89},{122,65},{123,81... | collective-permute-start | bytes 2359304 | tf_op jit(solution)/shard_map/ppermute | solution.py:56
  29.1 26.6 %collective-permute-start.4 = (bf16[15,64,128]{2,1,0:T(8,128)(2,1)S(1)}, bf16[15,64,128]{2,1,0:T(8,128)(2,1)S(1)}, u32[]{:S(2)}, u32[]{:S(2)}) collective-permute-start(bf16[15,64,128]{2,1,0:T(8,128)(2,1)S(1)} %get-tuple-element.16), channel_id=1, source_target_pairs={{0,8},{1,9},{2,10},{3,11},{4,12},{5,13},{6,14},{7,15},{8,16},{9,17... | collective-permute-start | bytes 737288 | tf_op jit(solution)/shard_map/ppermute | solution.py:56
  52.5 9.0 %collective-permute-start.5 = (bf16[15,64,128]{2,1,0:T(8,128)(2,1)S(1)}, bf16[15,64,128]{2,1,0:T(8,128)(2,1)S(1)}, u32[]{:S(2)}, u32[]{:S(2)}) collective-permute-start(bf16[15,64,128]{2,1,0:T(8,128)(2,1)S(1)} %get-tuple-element.17), channel_id=1, source_target_pairs={{8,0},{9,1},{10,2},{11,3},{12,4},{13,5},{14,6},{15,7},{16,8},{17,9... | collective-permute-start | bytes 737288 | tf_op jit(solution)/shard_map/ppermute | solution.py:56
  61.5 12.0 %copy-start.1 = (bf16[3,2048,128]{1,2,0:T(8,128)(2,1)S(1)}, bf16[3,2048,128]{1,2,0:T(8,128)(2,1)}, u32[]{:S(2)}) copy-start(bf16[3,2048,128]{1,2,0:T(8,128)(2,1)} %copy.13) | copy-start | bytes 4718596
  61.5 12.0 %copy-start.2 = (bf16[32,64,128]{2,1,0:T(8,128)(2,1)S(1)}, bf16[32,64,128]{2,1,0:T(8,128)(2,1)}, u32[]{:S(2)}) copy-start(bf16[32,64,128]{2,1,0:T(8,128)(2,1)} %fusion.5.mask_hbm) | copy-start | bytes 1572868
  61.7 6.1 %collective-permute-start.6 = (bf16[48,16,128]{2,1,0:T(8,128)(2,1)S(1)}, bf16[48,16,128]{2,1,0:T(8,128)(2,1)S(1)}, u32[]{:S(2)}, u32[]{:S(2)}) collective-permute-start(bf16[48,16,128]{2,1,0:T(8,128)(2,1)S(1)} %get-tuple-element.18), channel_id=1, source_target_pairs={{0,1},{1,2},{2,3},{3,4},{4,5},{5,6},{6,7},{8,9},{9,10},{10,11},{11... | collective-permute-start | bytes 589832 | tf_op jit(solution)/shard_map/ppermute | solution.py:56
  65.2 8.3 %collective-permute-start.7 = (bf16[48,16,128]{2,1,0:T(8,128)(2,1)S(1)}, bf16[48,16,128]{2,1,0:T(8,128)(2,1)S(1)}, u32[]{:S(2)}, u32[]{:S(2)}) collective-permute-start(bf16[48,16,128]{2,1,0:T(8,128)(2,1)S(1)} %get-tuple-element.19), channel_id=1, source_target_pairs={{1,0},{2,1},{3,2},{4,3},{5,4},{6,5},{7,6},{9,8},{10,9},{11,10},{12... | collective-permute-start | bytes 589832 | tf_op jit(solution)/shard_map/ppermute | solution.py:56
  85.3 1.9 %collective-permute-start.8 = (bf16[27,64,128]{2,1,0:T(8,128)(2,1)S(1)}, bf16[27,64,128]{2,1,0:T(8,128)(2,1)S(1)}, u32[]{:S(2)}, u32[]{:S(2)}) collective-permute-start(bf16[27,64,128]{2,1,0:T(8,128)(2,1)S(1)} %bitcast.31), channel_id=1, source_target_pairs={{0,8},{1,9},{2,10},{3,11},{4,12},{5,13},{6,14},{7,15},{8,0},{9,1},... | collective-permute-start | bytes 1327112 | tf_op jit(solution)/shard_map/ppermute | solution.py:56
  128.0 4.4 %collective-permute-start.9 = (bf16[27,64,128]{2,1,0:T(8,128)(2,1)S(1)}, bf16[27,64,128]{2,1,0:T(8,128)(2,1)S(1)}, u32[]{:S(2)}, u32[]{:S(2)}) collective-permute-start(bf16[27,64,128]{2,1,0:T(8,128)(2,1)S(1)} %bitcast.28), channel_id=1, source_target_pairs={{0,8},{1,9},{2,10},{3,11},{4,12},{5,13},{6,14},{7,15},{8,0},{9,1},... | collective-permute-start | bytes 1327112 | tf_op jit(solution)/shard_map/ppermute | solution.py:56
